TPU v7x, 128 devices: a whole 4x4x4 slice. The times are simulated.
128 devices in a mesh: segment: 8 (over x, core), mp: 16 (over z, y).
Axes of the slice: x: 4, y: 4, z: 4, core: 2. Of those that a mesh axis runs over, the one named last changes fastest.
Arguments:
- token_ids: int32 [128], replicated, may hold values from 0 to 128255
- teacher_seeds: int32 [8], P('segment'), may hold values from 0 to 16777215
- student_seeds: int32 [8], P('segment'), may hold values from 0 to 16777215
- teacher_gain: bfloat16 [8, 16384], P('segment', 'mp'), may hold values from 0.099609375 to 1.8984375
- student_gain: bfloat16 [8, 16384], P('segment'), may hold values from 0.099609375 to 1.8984375
Outputs:
- losses: float32 [8], P('segment')
- grad_up: float32 [8, 16384, 128], P('segment', 'mp')
- grad_down: float32 [8, 16384, 128], P('segment', 'mp')
All inputs are finite; a program needn't handle non-finite values.
Results may differ from a plain program's by a relative error of at most 0.029.
Values may be sent and summed in bfloat16 or wider, within the bound.
No kernel may reach another device: no remote copies, remote signals or barrier semaphores. Data moves between devices by JAX's collectives and lax.ppermute only.
A program may use at most 64 MiB of HBM per device.

v0:
```python
import math

import jax
import jax.numpy as jnp
from jax import lax
from jax.sharding import PartitionSpec as P

D = 16384
R = 128
MB_TOK = 128


EPSILON = 1e-05
EMBED_KEY = 7919


def shifted(value, axis, steps):
    count = lax.axis_size(axis)
    leading, last = (max(0, -steps), min(count, count - steps))
    return lax.ppermute(value, axis, [(source, source + steps) for source in range(leading, last)])


def scramble(mixed_bits):
    multiplier = jnp.int32(73244475)
    mixed_bits = jnp.bitwise_xor(mixed_bits, lax.shift_right_logical(mixed_bits, jnp.int32(16)))
    mixed_bits = mixed_bits * multiplier
    mixed_bits = jnp.bitwise_xor(mixed_bits, lax.shift_right_logical(mixed_bits, jnp.int32(16)))
    mixed_bits = mixed_bits * multiplier
    mixed_bits = jnp.bitwise_xor(mixed_bits, lax.shift_right_logical(mixed_bits, jnp.int32(16)))
    return mixed_bits


def uniform_bits(layer_seed, row_index, col_index):
    mixed_bits = layer_seed * jnp.int32(1000003) + row_index * jnp.int32(16411) + col_index
    return lax.shift_right_logical(scramble(scramble(mixed_bits)), jnp.int32(8))


def hashed(layer_seed, row_index, col_index, magnitude):
    bits_value = uniform_bits(layer_seed, row_index, col_index)
    return (bits_value.astype(jnp.float32) * (2.0 / 16777216.0) - 1.0) * magnitude


def ternary(layer_seed, row_index, col_index, magnitude):
    bits_value = uniform_bits(layer_seed, row_index, col_index)
    return (jnp.remainder(bits_value, jnp.int32(3)) - jnp.int32(1)).astype(jnp.float32) * magnitude


def local(token_ids, teacher_seeds, student_seeds, teacher_gain, student_gain):
    mp_index = lax.axis_index("mp")
    segment_index = lax.axis_index("segment")
    segment_count = lax.axis_size("segment")
    local_width = teacher_gain.shape[1]
    token_count = token_ids.shape[0]
    first_col = mp_index * local_width
    columns = first_col + jnp.arange(local_width, dtype=jnp.int32)
    stream = hashed(
        jnp.int32(EMBED_KEY), token_ids[:, None], columns[None, :], math.sqrt(3.0)
    ).astype(jnp.bfloat16)
    teacher_seed = teacher_seeds[0]

    def teacher(layer_in, active):
        partial_sum = jnp.zeros((token_count, local_width), jnp.float32)
        stream_piece = lax.all_gather(layer_in, "mp", axis=1, tiled=True)
        gain_piece = lax.all_gather(teacher_gain, "mp", axis=1, tiled=True)
        width_now = stream_piece.shape[1]

        def multiply(total):
            row_index = jnp.arange(width_now, dtype=jnp.int32)
            weight = hashed(
                teacher_seed, row_index[:, None], columns[None, :], math.sqrt(3.0 / D)
            ).astype(jnp.bfloat16)
            scaled_in = (stream_piece.astype(jnp.float32) * gain_piece.astype(jnp.float32)).astype(
                jnp.bfloat16
            )
            return jnp.dot(scaled_in, weight, preferred_element_type=jnp.float32)

        def keep_total(total):
            return total

        partial_sum = lax.cond(active, multiply, keep_total, partial_sum)
        squares = jnp.sum(jnp.square(stream_piece.astype(jnp.float32)), axis=1, keepdims=True)
        partial_sum, squares = (partial_sum, squares)
        scale_rows = lax.rsqrt(squares / D + EPSILON)
        result = (layer_in.astype(jnp.float32) + partial_sum * scale_rows).astype(jnp.bfloat16)
        return jnp.where(active, result, layer_in)

    first_out = teacher(stream, segment_index == 0)

    def forward_step(turn, state):
        outgoing, saved_in, saved_out = state
        incoming = shifted(outgoing, "segment", 1)
        active = segment_index == turn
        result = teacher(incoming, active)
        saved_in = jnp.where(active, incoming, saved_in)
        saved_out = jnp.where(active, result, saved_out)
        return (result, saved_in, saved_out)

    final_state = lax.fori_loop(1, segment_count, forward_step, (first_out, stream, first_out))
    layer_in = final_state[1]
    layer_out = final_state[2]
    student_seed = student_seeds[0]
    rank_index = jnp.arange(R, dtype=jnp.int32)[None, :]
    rows_in, rows_target = (
        lax.all_to_all(layer_in, "mp", split_axis=0, concat_axis=1, tiled=True),
        lax.all_to_all(layer_out, "mp", split_axis=0, concat_axis=1, tiled=True),
    )
    all_rows = jnp.arange(D, dtype=jnp.int32)[:, None]
    up_weight = ternary(student_seed, all_rows, rank_index, math.sqrt(1.5 / D)).astype(jnp.bfloat16)
    down_weight = ternary(student_seed, all_rows, rank_index + R, math.sqrt(1.5 / R)).astype(
        jnp.bfloat16
    )
    hidden_in = rows_in.astype(jnp.float32)
    mean_sq = jnp.mean(hidden_in * hidden_in, axis=1, keepdims=True)
    normed = (hidden_in * lax.rsqrt(mean_sq + EPSILON) * student_gain.astype(jnp.float32)).astype(
        jnp.bfloat16
    )
    pre_act = jnp.dot(normed, up_weight, preferred_element_type=jnp.float32)
    rectified = jnp.maximum(pre_act, 0.0)
    squared = (rectified * rectified).astype(jnp.bfloat16)
    student_out = hidden_in + lax.dot_general(
        squared, down_weight, (((1,), (1,)), ((), ())), preferred_element_type=jnp.float32
    )
    error = student_out - rows_target.astype(jnp.float32)
    scaled_error = (error / MB_TOK).astype(jnp.bfloat16)
    back = jnp.dot(scaled_error, down_weight, preferred_element_type=jnp.float32)
    back_pre = (back * 2.0 * rectified).astype(jnp.bfloat16)
    up_part = lax.dot_general(
        normed, back_pre, (((0,), (0,)), ((), ())), preferred_element_type=jnp.float32
    )
    down_part = lax.dot_general(
        scaled_error, squared, (((0,), (0,)), ((), ())), preferred_element_type=jnp.float32
    )
    grads = lax.psum_scatter(
        jnp.concatenate([up_part, down_part], axis=1), "mp", scatter_dimension=0, tiled=True
    )
    total_error = lax.psum(jnp.sum(error * error), "mp")
    grad_up = grads[:, :R]
    grad_down = grads[:, R:]
    layer_loss = (total_error / (MB_TOK * D)).reshape(1)
    return (layer_loss, grad_up[None], grad_down[None])


def solution(mesh):
    in_specs = (P(), P("segment"), P("segment"), P("segment", "mp"), P("segment", None))
    out_specs = (P("segment"), P("segment", "mp", None), P("segment", "mp", None))
    return jax.shard_map(local, mesh=mesh, in_specs=in_specs, out_specs=out_specs, check_vma=False)
```

profile of v0, /device:TPU:0, one launch (start us, length us, event | category | flops | bytes accessed | tf_op | source)
XLA Modules:
  0.0 1155.8 jit_solution(8616805068947674919)
XLA Ops:
  9.1 25.3 %all_gather.21 = bf16[1,16384]{1,0:T(2,128)(2,1)S(1)} all-gather(bf16[1,1024]{1,0:T(2,128)(2,1)} %param.14), channel_id=1, replica_groups=mesh['segment'=8,'mp'=16] {'mp'}, dimensions={1}, use_global_device_ids=true | all-gather | bytes 34816 | tf_op jit(solution)/shard_map/all_gather | solution.py:64
  34.4 30.6 %all-gather.3.cloned.1.call-done = bf16[128,16384]{1,0:T(8,128)(2,1)} async-done(((bf16[128,1024]{1,0:T(8,128)(2,1)}), bf16[128,16384]{1,0:T(8,128)(2,1)}) %all-gather.3.cloned.1.call-update) | async-done | bytes 4194320 | tf_op jit(solution)/shard_map/all_gather | solution.py:63
  65.0 3.1 multiply_reduce_fusion.1
  68.1 57.3 %conditional.2 = (f32[128,1024]{1,0:T(8,128)S(1)}) conditional(s32[]{:T(128)} %convert_element_type.122, () %tuple.34, (bf16[128,16384]{1,0:T(8,128)(2,1)}, bf16[1,16384]{1,0:T(2,128)(2,1)S(1)}, s32[]{:T(128)}, s32[1024]{0:T(1024)S(1)}) %tuple.35), branch_computations={%region_0.0_spmd, %region_1.0_spmd} | conditional | flops 4687183872 | bytes 5017624 | solution.py:80
  68.8 56.5 %fusion.12 = f32[128,1024]{1,0:T(8,128)S(1)} fusion(s32[1024]{0:T(1024)S(1)} %get-tuple-element.158, s32[16384]{0:T(1024)S(1)} %multiply_add_fusion, bf16[128,16384]{1,0:T(8,128)(2,1)} %get-tuple-element.155, f32[16384]{0:T(1024)S(1)} %bitcast.25), kind=kOutput, calls=%fused_computation.17 | convolution fusion | flops 4687134720 | bytes 4853760 | tf_op jit(solution)/shard_map/cond/branch_1_fun/dot_general | solution.py:75
  126.6 778.0 %while.18 = (s32[]{:T(128)}, bf16[128,1024]{1,0:T(8,128)(2,1)S(1)}, bf16[128,1024]{1,0:T(8,128)(2,1)}, bf16[128,1024]{1,0:T(8,128)(2,1)}, s32[]{:T(128)}, /*inde...) while((s32[]{:T(128)}, bf16[128,1024]{1,0:T(8,128)(2,1)S(1)}, ...), condition=%wide.region_7.8_spmd.clone, body=%wide.region_3.7_spmd.clone.sunk | while | flops 4694393856 | bytes 27873592 | solution.py:98
  129.9 23.3 %all_gather.27 = bf16[1,16384]{1,0:T(2,128)(2,1)S(1)} all-gather(bf16[1,1024]{1,0:T(2,128)(2,1)S(1)} %get-tuple-element.305), channel_id=1, replica_groups=mesh['segment'=8,'mp'=16] {'mp'}, dimensions={1}, use_global_device_ids=true | all-gather | bytes 34816 | tf_op jit(solution)/shard_map/while/body/eval_jaxpr/all_gather | solution.py:64
  153.3 25.7 %all-gather.5.cloned.1.call-done = bf16[128,16384]{1,0:T(8,128)(2,1)} async-done(((bf16[128,1024]{1,0:T(8,128)(2,1)}), bf16[128,16384]{1,0:T(8,128)(2,1)}) %all-gather.5.cloned.1.call-update) | async-done | bytes 4194320 | tf_op jit(solution)/shard_map/while/body/eval_jaxpr/all_gather | solution.py:63
  179.0 3.1 multiply_reduce_fusion.5
  185.0 57.2 %collective-permute-start = (bf16[128,1024]{1,0:T(8,128)(2,1)S(1)}, bf16[128,1024]{1,0:T(8,128)(2,1)S(1)}, u32[]{:S(2)}, u32[]{:S(2)}) collective-permute-start(bf16[128,1024]{1,0:T(8,128)(2,1)S(1)} %get-tuple-element.292), channel_id=1, source_target_pairs={{0,16},{16,32},{32,48},{48,64},{64,80},{80,96},{96,112},{1,17},{17... | collective-permute-start | bytes 786440 | tf_op jit(solution)/shard_map/while/body/eval_jaxpr/ppermute | solution.py:20
  244.1 23.3 %all_gather.27 = bf16[1,16384]{1,0:T(2,128)(2,1)S(1)} all-gather(bf16[1,1024]{1,0:T(2,128)(2,1)S(1)} %get-tuple-element.305), channel_id=1, replica_groups=mesh['segment'=8,'mp'=16] {'mp'}, dimensions={1}, use_global_device_ids=true | all-gather | bytes 34816 | tf_op jit(solution)/shard_map/while/body/eval_jaxpr/all_gather | solution.py:64
  267.4 29.6 %all-gather.5.cloned.1.call-done = bf16[128,16384]{1,0:T(8,128)(2,1)} async-done(((bf16[128,1024]{1,0:T(8,128)(2,1)}), bf16[128,16384]{1,0:T(8,128)(2,1)}) %all-gather.5.cloned.1.call-update) | async-done | bytes 4194320 | tf_op jit(solution)/shard_map/while/body/eval_jaxpr/all_gather | solution.py:63
  306.7 23.3 %all_gather.27 = bf16[1,16384]{1,0:T(2,128)(2,1)S(1)} all-gather(bf16[1,1024]{1,0:T(2,128)(2,1)S(1)} %get-tuple-element.305), channel_id=1, replica_groups=mesh['segment'=8,'mp'=16] {'mp'}, dimensions={1}, use_global_device_ids=true | all-gather | bytes 34816 | tf_op jit(solution)/shard_map/while/body/eval_jaxpr/all_gather | solution.py:64
  330.0 86.8 %all-gather.5.cloned.1.call-done = bf16[128,16384]{1,0:T(8,128)(2,1)} async-done(((bf16[128,1024]{1,0:T(8,128)(2,1)}), bf16[128,16384]{1,0:T(8,128)(2,1)}) %all-gather.5.cloned.1.call-update) | async-done | bytes 4194320 | tf_op jit(solution)/shard_map/while/body/eval_jaxpr/all_gather | solution.py:63
  426.5 23.3 %all_gather.27 = bf16[1,16384]{1,0:T(2,128)(2,1)S(1)} all-gather(bf16[1,1024]{1,0:T(2,128)(2,1)S(1)} %get-tuple-element.305), channel_id=1, replica_groups=mesh['segment'=8,'mp'=16] {'mp'}, dimensions={1}, use_global_device_ids=true | all-gather | bytes 34816 | tf_op jit(solution)/shard_map/while/body/eval_jaxpr/all_gather | solution.py:64
  449.9 86.6 %all-gather.5.cloned.1.call-done = bf16[128,16384]{1,0:T(8,128)(2,1)} async-done(((bf16[128,1024]{1,0:T(8,128)(2,1)}), bf16[128,16384]{1,0:T(8,128)(2,1)}) %all-gather.5.cloned.1.call-update) | async-done | bytes 4194320 | tf_op jit(solution)/shard_map/while/body/eval_jaxpr/all_gather | solution.py:63
  546.1 23.3 %all_gather.27 = bf16[1,16384]{1,0:T(2,128)(2,1)S(1)} all-gather(bf16[1,1024]{1,0:T(2,128)(2,1)S(1)} %get-tuple-element.305), channel_id=1, replica_groups=mesh['segment'=8,'mp'=16] {'mp'}, dimensions={1}, use_global_device_ids=true | all-gather | bytes 34816 | tf_op jit(solution)/shard_map/while/body/eval_jaxpr/all_gather | solution.py:64
  569.5 88.4 %all-gather.5.cloned.1.call-done = bf16[128,16384]{1,0:T(8,128)(2,1)} async-done(((bf16[128,1024]{1,0:T(8,128)(2,1)}), bf16[128,16384]{1,0:T(8,128)(2,1)}) %all-gather.5.cloned.1.call-update) | async-done | bytes 4194320 | tf_op jit(solution)/shard_map/while/body/eval_jaxpr/all_gather | solution.py:63
  667.5 23.3 %all_gather.27 = bf16[1,16384]{1,0:T(2,128)(2,1)S(1)} all-gather(bf16[1,1024]{1,0:T(2,128)(2,1)S(1)} %get-tuple-element.305), channel_id=1, replica_groups=mesh['segment'=8,'mp'=16] {'mp'}, dimensions={1}, use_global_device_ids=true | all-gather | bytes 34816 | tf_op jit(solution)/shard_map/while/body/eval_jaxpr/all_gather | solution.py:64
  690.8 86.7 %all-gather.5.cloned.1.call-done = bf16[128,16384]{1,0:T(8,128)(2,1)} async-done(((bf16[128,1024]{1,0:T(8,128)(2,1)}), bf16[128,16384]{1,0:T(8,128)(2,1)}) %all-gather.5.cloned.1.call-update) | async-done | bytes 4194320 | tf_op jit(solution)/shard_map/while/body/eval_jaxpr/all_gather | solution.py:63
  787.1 23.3 %all_gather.27 = bf16[1,16384]{1,0:T(2,128)(2,1)S(1)} all-gather(bf16[1,1024]{1,0:T(2,128)(2,1)S(1)} %get-tuple-element.305), channel_id=1, replica_groups=mesh['segment'=8,'mp'=16] {'mp'}, dimensions={1}, use_global_device_ids=true | all-gather | bytes 34816 | tf_op jit(solution)/shard_map/while/body/eval_jaxpr/all_gather | solution.py:64
  810.5 88.1 %all-gather.5.cloned.1.call-done = bf16[128,16384]{1,0:T(8,128)(2,1)} async-done(((bf16[128,1024]{1,0:T(8,128)(2,1)}), bf16[128,16384]{1,0:T(8,128)(2,1)}) %all-gather.5.cloned.1.call-update) | async-done | bytes 4194320 | tf_op jit(solution)/shard_map/while/body/eval_jaxpr/all_gather | solution.py:63
  904.6 5.3 all-to-all-start
  910.6 7.9 all-to-all-done
  918.6 3.5 all-to-all-start.1
  922.1 11.3 reduce-scatter.2.cloned.1.call-start
  933.7 10.1 fusion.73
  943.9 11.2 multiply_reduce_fusion.2
  955.1 14.6 %fusion.80 = f32[16384,128]{0,1:T(8,128)} fusion(f32[8,128]{1,0:T(8,128)S(1)} %fusion.73, s32[128]{0:T(128)S(1)} %iota_add_fusion.1, s32[16384]{0:T(1024)S(1)} %multiply_add_fusion.2, f32[8,16384]{1,0:T(8,128)S(1)} %get-tuple-element.226, f32[8,16384]{1,0:T(8,128)S(1)} %bitcast.21, f32[16384]{0:T(1024)S(1)} %bitcast.24, f32[8]{0:T(128)S(1)} %add_rsqrt_fusion.1), kind=kOutput, calls=%fused_computation.104 | convolution fusion | flops 126487552 | bytes 9572896 | tf_op jit(solution)/shard_map/dot_general | solution.py:127
  973.1 6.2 pad_maximum_fusion
  979.2 41.3 %psum.7 = f32[]{:T(128)} all-reduce(f32[]{:T(128)} %get-tuple-element.225), channel_id=1, replica_groups=mesh['segment'=8,'mp'=16] {'mp'}, use_global_device_ids=true, to_apply=%region_10.11 | all-reduce | flops 1 | bytes 8 | tf_op jit(solution)/shard_map/psum | solution.py:136
  1021.2 123.3 %reduce-scatter.2.cloned.1.call-done = f32[1024,256]{0,1:T(8,128)} async-done(((f32[16384,256]{0,1:T(8,128)}), f32[1024,256]{0,1:T(8,128)}) %reduce-scatter.2.cloned.1.call-update) | async-done | bytes 1048592 | tf_op jit(solution)/shard_map/reduce_scatter | solution.py:133
  (125 shorter events, 72.7 us)
Async XLA Ops:
  7.2 57.8 %all-gather.3.cloned.1.call-start = ((), (), s32[]{:S(2)}) async-start(), calls=%async_computation.3 | async-start | bytes 4456448 | tf_op jit(solution)/shard_map/all_gather | solution.py:63
  68.1 58.6 %copy-start.3 = (bf16[1,1024]{1,0:T(2,128)(2,1)S(1)}, bf16[1,1024]{1,0:T(2,128)(2,1)}, u32[]{:S(2)}) copy-start(bf16[1,1024]{1,0:T(2,128)(2,1)} %param.14) | copy-start | bytes 6148
  126.6 783.9 %copy-start.4 = (bf16[1,16384]{1,0:T(2,128)(2,1)S(1)}, bf16[1,16384]{1,0:T(2,128)(2,1)}, u32[]{:S(2)}) copy-start(bf16[1,16384]{1,0:T(2,128)(2,1)} %param.15) | copy-start | bytes 98308
  126.6 52.4 %all-gather.5.cloned.1.call-start = ((), (), s32[]{:S(2)}) async-start(), calls=%async_computation.5 | async-start | bytes 4456448 | tf_op jit(solution)/shard_map/while/body/eval_jaxpr/all_gather | solution.py:63
  126.6 2.6 collective-permute-start
  129.2 0.7 copy-start
  182.1 1.0 copy-start.1
  185.0 112.0 %all-gather.5.cloned.1.call-start = ((), (), s32[]{:S(2)}) async-start(), calls=%async_computation.5 | async-start | bytes 4456448 | tf_op jit(solution)/shard_map/while/body/eval_jaxpr/all_gather | solution.py:63
  185.0 58.3 %collective-permute-start = (bf16[128,1024]{1,0:T(8,128)(2,1)S(1)}, bf16[128,1024]{1,0:T(8,128)(2,1)S(1)}, u32[]{:S(2)}, u32[]{:S(2)}) collective-permute-start(bf16[128,1024]{1,0:T(8,128)(2,1)S(1)} %get-tuple-element.292), channel_id=1, source_target_pairs={{0,16},{16,32},{32,48},{48,64},{64,80},{80,96},{96,112},{1,17},{17... | collective-permute-start | bytes 786440 | tf_op jit(solution)/shard_map/while/body/eval_jaxpr/ppermute | solution.py:20
  243.3 0.7 copy-start
  300.2 1.0 copy-start.1
  303.1 113.8 %all-gather.5.cloned.1.call-start = ((), (), s32[]{:S(2)}) async-start(), calls=%async_computation.5 | async-start | bytes 4456448 | tf_op jit(solution)/shard_map/while/body/eval_jaxpr/all_gather | solution.py:63
  303.1 2.9 collective-permute-start
  306.0 0.7 copy-start
  420.0 1.0 copy-start.1
  422.9 113.5 %all-gather.5.cloned.1.call-start = ((), (), s32[]{:S(2)}) async-start(), calls=%async_computation.5 | async-start | bytes 4456448 | tf_op jit(solution)/shard_map/while/body/eval_jaxpr/all_gather | solution.py:63
  422.9 2.9 collective-permute-start
  539.6 1.0 copy-start.1
  542.5 115.3 %all-gather.5.cloned.1.call-start = ((), (), s32[]{:S(2)}) async-start(), calls=%async_computation.5 | async-start | bytes 4456448 | tf_op jit(solution)/shard_map/while/body/eval_jaxpr/all_gather | solution.py:63
  542.5 2.9 collective-permute-start
  660.9 1.0 copy-start.1
  663.9 113.6 %all-gather.5.cloned.1.call-start = ((), (), s32[]{:S(2)}) async-start(), calls=%async_computation.5 | async-start | bytes 4456448 | tf_op jit(solution)/shard_map/while/body/eval_jaxpr/all_gather | solution.py:63
  663.9 2.9 collective-permute-start
  666.8 0.7 copy-start
  780.6 1.0 copy-start.1
  783.5 115.0 %all-gather.5.cloned.1.call-start = ((), (), s32[]{:S(2)}) async-start(), calls=%async_computation.5 | async-start | bytes 4456448 | tf_op jit(solution)/shard_map/while/body/eval_jaxpr/all_gather | solution.py:63
  783.5 2.9 collective-permute-start
  901.6 1.0 copy-start.1
  904.6 14.0 %all-to-all-start = ((bf16[16,8,1024]{2,1,0:T(8,128)(2,1)}), bf16[16,8,1024]{2,1,0:T(8,128)(2,1)S(1)}, u32[]{:S(2)}, u32[]{:S(2)}) async-start(bf16[16,8,1024]{2,1,0:T(8,128)(2,1)} %bitcast.3), calls=%async_computation | async-start | bytes 524288 | tf_op jit(solution)/shard_map/all_to_all | solution.py:104
  918.6 25.3 %all-to-all-start.1 = ((bf16[16,8,1024]{2,1,0:T(8,128)(2,1)}), bf16[16,8,1024]{2,1,0:T(8,128)(2,1)S(1)}, u32[]{:S(2)}, u32[]{:S(2)}) async-start(bf16[16,8,1024]{2,1,0:T(8,128)(2,1)} %bitcast.9), calls=%async_computation.1 | async-start | bytes 524288 | tf_op jit(solution)/shard_map/all_to_all | solution.py:105
  922.1 222.4 %reduce-scatter.2.cloned.1.call-start = ((), (), s32[]{:S(2)}) async-start(), calls=%async_computation.4 | async-start | bytes 17825792 | tf_op jit(solution)/shard_map/reduce_scatter | solution.py:133
  969.7 3.4 copy-start.2
  (3 other events, 2.1 us)
Sparse Core Ops, SparseCore 0:
  10.7 54.2 all-gather.2
  130.0 48.8 all-gather.4
  244.2 52.8 all-gather.4
  306.8 110.0 all-gather.4
  426.7 109.7 all-gather.4
  546.3 111.5 all-gather.4
  667.6 109.8 all-gather.4
  787.3 111.2 all-gather.4
  979.4 165.1 reduce-scatter.1
where the time goes:
time: 1170 us; the launch traced here: 1160 us
  waiting for transfers between devices  662 us (57%)
  blocking collectives  230 us (20%)
  matrix products  93.7 us (8%)
  starting transfers between devices  87.5 us (7%)
  other arithmetic  47.7 us (4%)
  local copies, waits for them, and re-layouts  17.4 us (1%)
  between operations  16.7 us (1%)
    all_gather x8, waiting for transfers between devices, teacher(): stream_piece = lax.all_gather(layer_in, 'mp', axis=1, tiled=True)  523 us
    all_gather x8, blocking collectives, teacher(): gain_piece = lax.all_gather(teacher_gain, 'mp', axis=1, tiled=True)  189 us
    reduce_scatter x1, waiting for transfers between devices, local(): lax.psum_scatter(jnp.concatenate([up_part, down_part], axis=1), 'mp', sca...  123 us
    ppermute x7, starting transfers between devices, shifted(): lax.ppermute(value, axis, [(source, source + steps) for source in range(l...  67.3 us
    dot_general x1, matrix products, multiply(): return jnp.dot(scaled_in, weight, preferred_element_type=jnp.float32)  56.5 us
    psum x1, blocking collectives, local(): total_error = lax.psum(jnp.sum(error * error), 'mp')  41.3 us
    reduce_sum x8, other arithmetic, teacher(): jnp.sum(jnp.square(stream_piece.astype(jnp.float32)), axis=1, keepdims=True)  24.6 us
  transfers between devices with their start and end apart: 18, of which 17 were waited for; matrix products, arithmetic and copies ran while one was open for 1% of the time, Pallas kernels for 0%

commit v1 on v0

v1 whole, which is shorter than its diff:
```python
import math

import jax
import jax.numpy as jnp
import numpy as np
from jax import lax
from jax.experimental import pallas as pl
from jax.experimental.pallas import tpu as pltpu
from jax.sharding import PartitionSpec as P

D = 16384
R = 128
TOK = 128
LAYERS = 8
SEG = 8
MP = 16
WIDTH = D // MP
PIECE = WIDTH // SEG
ROWS = TOK + 16
EPSILON = 1e-05
EMBED_KEY = 7919
BF = jnp.bfloat16
F32 = jnp.float32


def wrapped(value):
    value &= 0xFFFFFFFF
    return np.int32(value - (1 << 32) if value >> 31 else value)


MULT = wrapped(73244475)
MULT_SQ = wrapped(73244475 * 73244475)


def fold(bits):
    return jnp.bitwise_xor(bits, lax.shift_right_logical(bits, jnp.int32(16)))


def uniform_bits(mixed_bits):
    mixed_bits = fold(mixed_bits) * MULT
    mixed_bits = fold(mixed_bits) * MULT_SQ
    mixed_bits = fold(mixed_bits) * MULT
    return lax.shift_right_logical(fold(mixed_bits), jnp.int32(8))


def hashed(mixed_bits, magnitude):
    return uniform_bits(mixed_bits).astype(F32) * np.float32(magnitude * 2.0 / 16777216.0) - np.float32(magnitude)


def ternary(mixed_bits, magnitude):
    bits = uniform_bits(mixed_bits)
    return (lax.rem(bits, jnp.int32(3)) - jnp.int32(1)).astype(F32) * np.float32(magnitude)


def split_row(row):
    high = row.astype(BF).astype(F32)
    index = lax.broadcasted_iota(jnp.int32, (16, row.shape[1]), 0)
    tile = jnp.where(index == 0, high, jnp.where(index == 1, row - high, 0.0))
    return tile.astype(BF)


def joined_row(tile):
    return jnp.sum(tile.astype(F32), axis=0, keepdims=True)


SMEM = pl.BlockSpec(memory_space=pltpu.SMEM)
VMEM = pl.BlockSpec(memory_space=pltpu.VMEM)


def call(body, name, out_shape, in_specs, flops=0, nbytes=0, limit=48 << 20):
    single = not isinstance(out_shape, (tuple, list))
    return pl.pallas_call(
        body,
        out_shape=out_shape,
        in_specs=in_specs,
        out_specs=VMEM if single else tuple(VMEM for _ in out_shape),
        name=name,
        cost_estimate=pl.CostEstimate(flops=flops, bytes_accessed=nbytes, transcendentals=0),
        compiler_params=pltpu.CompilerParams(vmem_limit_bytes=limit),
    )


def sds(shape, dtype):
    return jax.ShapeDtypeStruct(shape, dtype)


def weight_kernel(place, out):
    chunk = 32
    row = lax.broadcasted_iota(jnp.int32, (chunk, WIDTH), 0)
    col = lax.broadcasted_iota(jnp.int32, (chunk, WIDTH), 1)
    base = row * 16411 + col + (place[0] * 1000003 + place[1] * (PIECE * 16411) + place[2] * WIDTH)
    per = PIECE // chunk

    def step(index, carry):
        first = (index // per) * WIDTH + (index % per) * chunk
        start = pl.multiple_of(index * chunk, chunk)
        out[pl.ds(start, chunk), :] = hashed(base + first * 16411, math.sqrt(3.0 / D)).astype(BF)
        return carry

    lax.fori_loop(0, MP * per, step, 0)


def teacher_weight(seed, segment, block):
    return call(
        weight_kernel,
        "weight",
        sds((MP * PIECE, WIDTH), BF),
        [SMEM],
        flops=20 * MP * PIECE * WIDTH,
        nbytes=2 * MP * PIECE * WIDTH,
    )(jnp.stack([seed, segment, block]))


def message(out, stream, gain):
    wide = stream.astype(F32)
    scaled = (wide * gain).astype(BF)
    squares = jnp.sum(wide * wide, axis=1, keepdims=True)
    tile = split_row(jnp.transpose(jnp.broadcast_to(squares, (TOK, TOK)))[:1])
    for index in range(MP):
        out[index, :TOK, :] = scaled
        out[index, TOK:, :] = tile


def first_kernel(place, token, gain, stream_out, message_out):
    col = lax.broadcasted_iota(jnp.int32, (TOK, PIECE), 1) + place[0]
    mixed = token[...] * 16411 + col + jnp.int32((EMBED_KEY * 1000003) % (1 << 32) - (1 << 32))
    stream = hashed(mixed, math.sqrt(3.0)).astype(BF)
    stream_out[...] = stream
    message(message_out, stream, gain[...])


def update_kernel(own, part_a, part_b, part_c, stream, gain, stream_out, mean_out, message_out):
    total = own[...]
    for part in (part_a, part_b, part_c):
        total = total + part[...].astype(F32)
    squares = joined_row(total[TOK:])
    mean = jnp.transpose(jnp.broadcast_to(squares, (TOK, TOK))) * np.float32(1.0 / D)
    mean_out[...] = mean
    result = (stream[...].astype(F32) + total[:TOK] * lax.rsqrt(mean + EPSILON)).astype(BF)
    stream_out[...] = result
    message(message_out, result, gain[...])


def contract_kernel(place, gathered, weight, own_out, other_out):
    scaled = jnp.concatenate([gathered[index, :TOK, :] for index in range(MP)], axis=1)
    squares = joined_row(gathered[0, TOK:, :])
    for index in range(1, MP):
        squares = squares + joined_row(gathered[index, TOK:, :])
    tile = split_row(squares)
    first = place[0] == 0
    for chunk in range(4):
        part = jnp.dot(scaled, weight[:, chunk * 256 : (chunk + 1) * 256], preferred_element_type=F32)
        left, right = part[:, :PIECE], part[:, PIECE:]
        own_out[chunk, :TOK, :] = jnp.where(first, left, right)
        other_out[chunk, :TOK, :] = jnp.where(first, right, left).astype(BF)
        own_out[chunk, TOK:, :] = tile.astype(F32)
        other_out[chunk, TOK:, :] = tile


def pair_kernel(place, own, other, kept, send_a, send_b, send_c):
    def total(chunk):
        return own[chunk] + other[chunk].astype(F32)

    def packed(chunk):
        both = total(chunk)
        return both[:TOK].astype(BF), split_row(joined_row(both[TOK:]))

    here = place[0]
    kept[...] = total(here)
    for shift, out in ((1, send_a), (2, send_b), (3, send_c)):
        body, tile = packed(lax.rem(here + shift, 4))
        out[:TOK, :] = body
        out[TOK:, :] = tile


CORE = [(i, i ^ 1) for i in range(SEG)]


def along_x(shift):
    return [(i, (i + 2 * shift) % SEG) for i in range(SEG)]


def along_y(shift):
    return [(i, i // 4 * 4 + (i + shift) % 4) for i in range(MP)]


def along_z(shift):
    return [(i, (i + 4 * shift) % MP) for i in range(MP)]


def sum_mp(value):
    for along in (along_y, along_z):
        parts = [lax.ppermute(value, "mp", along(shift)) for shift in (1, 2, 3)]
        value = (value + parts[1]) + (parts[0] + parts[2])
    return value


def student_up_kernel(place, pieces, mean, gain, normed_out, pre_out):
    row = lax.broadcasted_iota(jnp.int32, (PIECE, R), 0)
    rank = lax.broadcasted_iota(jnp.int32, (PIECE, R), 1)
    base = row * 16411 + rank + (place[0] * 1000003 + place[1] * (WIDTH * 16411))
    scale = lax.rsqrt(mean[...] + EPSILON)
    total = jnp.zeros((TOK, R), F32)
    for index in range(SEG):
        up_weight = ternary(base + index * PIECE * 16411, math.sqrt(1.5 / D)).astype(BF)
        columns = slice(index * PIECE, (index + 1) * PIECE)
        normed = (pieces[index, 0].astype(F32) * scale * gain[:, columns].astype(F32)).astype(BF)
        normed_out[:, columns] = normed
        total = total + jnp.dot(normed, up_weight, preferred_element_type=F32)
    pre_out[...] = total


def student_error_kernel(place, pieces, pre, back_out, scaled_out, squared_out):
    row = lax.broadcasted_iota(jnp.int32, (PIECE, R), 0)
    rank = lax.broadcasted_iota(jnp.int32, (PIECE, R), 1)
    base = row * 16411 + rank + (place[0] * 1000003 + place[1] * (WIDTH * 16411) + R)
    rectified = jnp.maximum(pre[...], 0.0)
    squared = (rectified * rectified).astype(BF)
    squared_out[...] = squared
    back = jnp.zeros((TOK, R), F32)
    squares = jnp.zeros((TOK, PIECE), F32)
    for index in range(SEG):
        down_weight = ternary(base + index * PIECE * 16411, math.sqrt(1.5 / R)).astype(BF)
        student = lax.dot_general(squared, down_weight, (((1,), (1,)), ((), ())), preferred_element_type=F32)
        error = pieces[index, 0].astype(F32) + student - pieces[index, 1].astype(F32)
        squares = squares + error * error
        scaled = (error * np.float32(1.0 / TOK)).astype(BF)
        scaled_out[:, index * PIECE : (index + 1) * PIECE] = scaled
        back = back + jnp.dot(scaled, down_weight, preferred_element_type=F32)
    back_out[:TOK, :] = back
    back_out[TOK:, :] = jnp.sum(squares.reshape(TOK // 8, 8, PIECE), axis=0)


def student_grad_kernel(normed, scaled, squared, pre, back, up_out, down_out):
    rectified = jnp.maximum(pre[...], 0.0)
    back_pre = (back[:TOK, :] * 2.0 * rectified).astype(BF)
    over_tokens = (((0,), (0,)), ((), ()))
    up_out[...] = lax.dot_general(normed[...], back_pre, over_tokens, preferred_element_type=F32)
    down_out[...] = lax.dot_general(scaled[...], squared[...], over_tokens, preferred_element_type=F32)


def local(token_ids, teacher_seeds, student_seeds, teacher_gain, student_gain):
    block = lax.axis_index("mp")
    segment = lax.axis_index("segment")
    core = lax.rem(segment, 2)
    column = segment // 2

    gains = teacher_gain.astype(F32).reshape(SEG, 1, PIECE)
    seeds = jnp.broadcast_to(teacher_seeds.astype(F32).reshape(1, 1, 1), (SEG, 1, PIECE))
    layer_facts = lax.all_to_all(
        jnp.concatenate([gains, seeds], axis=1), "segment", split_axis=0, concat_axis=0, tiled=True
    )
    layer_gains = layer_facts[:, 0]
    layer_seeds = layer_facts[:, 1, 0].astype(jnp.int32)

    message_shape = sds((MP, ROWS, PIECE), BF)
    piece_shape = sds((TOK, PIECE), BF)
    stream, outgoing = call(first_kernel, "first", (piece_shape, message_shape), [SMEM, VMEM, VMEM])(
        (block * WIDTH + segment * PIECE).reshape(1), token_ids.reshape(TOK, 1), layer_gains[:1]
    )
    streams, means = [stream], []
    for layer in range(LAYERS):
        weight = teacher_weight(layer_seeds[layer], segment, block)
        gathered = lax.all_to_all(outgoing, "mp", split_axis=0, concat_axis=0, tiled=True)
        own, other = call(
            contract_kernel,
            "contract",
            (sds((4, ROWS, PIECE), F32), sds((4, ROWS, PIECE), BF)),
            [SMEM, VMEM, VMEM],
            flops=2 * TOK * MP * PIECE * WIDTH,
            nbytes=2 * MP * PIECE * WIDTH,
        )(core.reshape(1), gathered, weight)
        other = lax.ppermute(other, "segment", CORE)
        kept, *sends = call(
            pair_kernel,
            "pair",
            (sds((ROWS, PIECE), F32),) + tuple(sds((ROWS, PIECE), BF) for _ in range(3)),
            [SMEM, VMEM, VMEM],
        )(column.reshape(1), own, other)
        parts = [lax.ppermute(send, "segment", along_x(shift)) for shift, send in zip((1, 2, 3), sends)]
        next_gain = layer_gains[min(layer + 1, LAYERS - 1)].reshape(1, PIECE)
        stream, mean, outgoing = call(
            update_kernel, "update", (piece_shape, sds((TOK, PIECE), F32), message_shape), [VMEM] * 6
        )(kept, *parts, stream, next_gain)
        streams.append(stream)
        means.append(mean)

    pairs = jnp.stack([jnp.stack([streams[layer], streams[layer + 1]]) for layer in range(LAYERS)])
    pieces = lax.all_to_all(pairs, "segment", split_axis=0, concat_axis=0, tiled=True)
    mean = lax.dynamic_index_in_dim(jnp.stack(means), segment, 0, False)
    place = jnp.stack([student_seeds[0], block])
    gain = lax.dynamic_slice_in_dim(student_gain, block * WIDTH, WIDTH, 1)
    normed, pre = call(
        student_up_kernel, "student_up", (sds((TOK, WIDTH), BF), sds((TOK, R), F32)), [SMEM, VMEM, VMEM, VMEM]
    )(place, pieces, mean, gain)
    pre = sum_mp(pre)
    back, scaled, squared = call(
        student_error_kernel,
        "student_error",
        (sds((TOK + 8, R), F32), sds((TOK, WIDTH), BF), sds((TOK, R), BF)),
        [SMEM, VMEM, VMEM],
    )(place, pieces, pre)
    back = sum_mp(back)
    grad_up, grad_down = call(
        student_grad_kernel, "student_grad", (sds((WIDTH, R), F32), sds((WIDTH, R), F32)), [VMEM] * 5
    )(normed, scaled, squared, pre, back)
    loss = (jnp.sum(back[TOK:]) / (TOK * D)).reshape(1)
    return loss, grad_up[None], grad_down[None]


def solution(mesh):
    in_specs = (P(), P("segment"), P("segment"), P("segment", "mp"), P("segment", None))
    out_specs = (P("segment"), P("segment", "mp", None), P("segment", "mp", None))
    return jax.shard_map(local, mesh=mesh, in_specs=in_specs, out_specs=out_specs, check_vma=False)
```

time: 1170 us -> 316 us (0.27); the launches traced: 1160 us -> 315 us
  waiting for transfers between devices: 662 us -> 94.5 us
  blocking collectives: 230 us -> 0 us
  matrix products: 93.7 us -> 0 us
  Pallas kernels: 0 us -> 65.7 us
  other arithmetic: 47.7 us -> 12.1 us
  local copies, waits for them, and re-layouts: 17.4 us -> 36.6 us
  starting transfers between devices: 87.5 us -> 102 us
  between operations: 16.7 us -> 4.23 us
    all_gather x8 -> x0, waiting for transfers between devices: 523 us -> none  [teacher(): stream_piece = lax.all_gather(layer_in, 'mp', axis=1, tiled=True)]
    all_gather x8 -> x0, blocking collectives: 189 us -> none  [teacher(): gain_piece = lax.all_gather(teacher_gain, 'mp', axis=1, tiled=True)]
    reduce_scatter x1 -> x0, waiting for transfers between devices: 123 us -> none  [local(): lax.psum_scatter(jnp.concatenate([up_part, down_part], axis=1), 'mp', sca...]
    dot_general x5 -> x0, matrix products: 93.7 us -> none  [the longest x1 56.5 us: multiply(): return jnp.dot(scaled_in, weight, preferred_element_type=jnp.float32)]
    pallas_call x0 -> x35, Pallas kernels: none -> 65.7 us  [the longest x8 46.7 us: teacher_weight(): call(weight_kernel, 'weight', sds((MP * PIECE, WIDTH), BF), [SMEM], flops...]
    all_to_all x2 -> x10, waiting for transfers between devices: 7.93 us -> 49.3 us  [the longest x8 35.2 us: local(): lax.all_to_all(outgoing, 'mp', split_axis=0, concat_axis=0, tiled=True)]
    psum x1 -> x0, blocking collectives: 41.3 us -> none  [local(): total_error = lax.psum(jnp.sum(error * error), 'mp')]
    all_to_all x2 -> x10, starting transfers between devices: 8.82 us -> 49.6 us  [the longest x8 41.7 us: local(): lax.all_to_all(outgoing, 'mp', split_axis=0, concat_axis=0, tiled=True)]
  transfers between devices with their start and end apart: 18 -> 54, of which waited for: 17 -> 50; matrix products, arithmetic and copies ran while one was open for 1% -> 4% of each run, Pallas kernels for 0% -> 15%
where the time goes in v1:
time: 316 us; the launch traced here: 315 us
  starting transfers between devices  102 us (32%)
  waiting for transfers between devices  94.5 us (30%)
  Pallas kernels  65.7 us (21%)
  local copies, waits for them, and re-layouts  36.6 us (12%)
  other arithmetic  12.1 us (4%)
  between operations  4.23 us (1%)
    pallas_call x8, Pallas kernels, teacher_weight(): call(weight_kernel, 'weight', sds((MP * PIECE, WIDTH), BF), [SMEM], flops...  46.7 us
    all_to_all x8, starting transfers between devices, local(): lax.all_to_all(outgoing, 'mp', split_axis=0, concat_axis=0, tiled=True)  41.7 us
    all_to_all x8, waiting for transfers between devices, local(): lax.all_to_all(outgoing, 'mp', split_axis=0, concat_axis=0, tiled=True)  35.2 us
    unnamed x41, local copies, waits for them, and re-layouts  33.6 us
    ppermute x24, starting transfers between devices, local(): lax.ppermute(send, 'segment', along_x(shift))  31.9 us
    ppermute x24, waiting for transfers between devices, local(): lax.ppermute(send, 'segment', along_x(shift))  24.6 us
    ppermute x12, starting transfers between devices, sum_mp(): parts = [lax.ppermute(value, 'mp', along(shift)) for shift in (1, 2, 3)]  19.4 us
    ppermute x12, waiting for transfers between devices, sum_mp(): parts = [lax.ppermute(value, 'mp', along(shift)) for shift in (1, 2, 3)]  11 us
  transfers between devices with their start and end apart: 54, of which 50 were waited for; matrix products, arithmetic and copies ran while one was open for 4% of the time, Pallas kernels for 15%

profile of v1, /device:TPU:0, one launch (start us, length us, event | category | flops | bytes accessed | tf_op | source)
XLA Modules:
  0.0 314.7 jit_solution(13655695573130245920)
XLA Ops:
  2.6 4.4 %all-to-all-start = ((f32[8,2,128]{2,1,0:T(2,128)}), f32[8,2,128]{2,1,0:T(2,128)S(1)}, u32[]{:S(2)}, u32[]{:S(2)}) async-start(f32[8,2,128]{2,1,0:T(2,128)} %concatenate.3), calls=%async_computation | async-start | bytes 16384 | tf_op jit(solution)/shard_map/all_to_all | solution.py:250
  7.8 4.5 %all-to-all-done = f32[8,2,128]{2,1,0:T(2,128)S(1)} async-done(((f32[8,2,128]{2,1,0:T(2,128)}), f32[8,2,128]{2,1,0:T(2,128)S(1)}, u32[]{:S(2)}, u32[]{:S(2)}) %all-to-all-start) | async-done | bytes 8224 | tf_op jit(solution)/shard_map/all_to_all | solution.py:250
  13.4 8.0 %all-to-all-start.1 = ((bf16[16,144,128]{2,1,0:T(8,128)(2,1)}), bf16[16,144,128]{2,1,0:T(8,128)(2,1)S(1)}, u32[]{:S(2)}, u32[]{:S(2)}) async-start(bf16[16,144,128]{2,1,0:T(8,128)(2,1)} %get-tuple-element.84), calls=%async_computation.1 | async-start | bytes 1179648 | tf_op jit(solution)/shard_map/all_to_all | solution.py:264
  22.8 5.8 %weight.8 = bf16[2048,1024]{1,0:T(8,128)(2,1)S(1)} custom-call(s32[3]{0:T(128)S(1)} %add_add_fusion.4.place), custom_call_target="tpu_custom_call" | custom-call | flops 41943040 | bytes 4194304 | tf_op jit(solution)/shard_map/weight/pallas_call | solution.py:104
  30.6 3.1 all-to-all-done.1.gathered
  45.8 4.1 %all-to-all-start.2 = ((bf16[16,144,128]{2,1,0:T(8,128)(2,1)}), bf16[16,144,128]{2,1,0:T(8,128)(2,1)S(1)}, u32[]{:S(2)}, u32[]{:S(2)}) async-start(bf16[16,144,128]{2,1,0:T(8,128)(2,1)} %get-tuple-element.92), calls=%async_computation.2 | async-start | bytes 1179648 | tf_op jit(solution)/shard_map/all_to_all | solution.py:264
  50.6 5.8 %weight.9 = bf16[2048,1024]{1,0:T(8,128)(2,1)S(1)} custom-call(s32[3]{0:T(128)S(1)} %add_add_fusion.5.place), custom_call_target="tpu_custom_call" | custom-call | flops 41943040 | bytes 4194304 | tf_op jit(solution)/shard_map/weight/pallas_call | solution.py:104
  58.5 2.8 all-to-all-done.2.gathered
  74.7 4.6 %all-to-all-start.3 = ((bf16[16,144,128]{2,1,0:T(8,128)(2,1)}), bf16[16,144,128]{2,1,0:T(8,128)(2,1)S(1)}, u32[]{:S(2)}, u32[]{:S(2)}) async-start(bf16[16,144,128]{2,1,0:T(8,128)(2,1)} %get-tuple-element.100), calls=%async_computation.3 | async-start | bytes 1179648 | tf_op jit(solution)/shard_map/all_to_all | solution.py:264
  80.0 5.8 %weight.10 = bf16[2048,1024]{1,0:T(8,128)(2,1)S(1)} custom-call(s32[3]{0:T(128)S(1)} %add_add_fusion.6.place), custom_call_target="tpu_custom_call" | custom-call | flops 41943040 | bytes 4194304 | tf_op jit(solution)/shard_map/weight/pallas_call | solution.py:104
  87.8 2.6 all-to-all-done.3.gathered
  100.4 2.5 collective-permute-done.9.part_a
  104.0 4.6 %all-to-all-start.4 = ((bf16[16,144,128]{2,1,0:T(8,128)(2,1)}), bf16[16,144,128]{2,1,0:T(8,128)(2,1)S(1)}, u32[]{:S(2)}, u32[]{:S(2)}) async-start(bf16[16,144,128]{2,1,0:T(8,128)(2,1)} %get-tuple-element.108), calls=%async_computation.4 | async-start | bytes 1179648 | tf_op jit(solution)/shard_map/all_to_all | solution.py:264
  109.3 5.8 %weight.11 = bf16[2048,1024]{1,0:T(8,128)(2,1)S(1)} custom-call(s32[3]{0:T(128)S(1)} %add_add_fusion.7.place), custom_call_target="tpu_custom_call" | custom-call | flops 41943040 | bytes 4194304 | tf_op jit(solution)/shard_map/weight/pallas_call | solution.py:104
  131.5 4.9 %all-to-all-start.5 = ((bf16[16,144,128]{2,1,0:T(8,128)(2,1)}), bf16[16,144,128]{2,1,0:T(8,128)(2,1)S(1)}, u32[]{:S(2)}, u32[]{:S(2)}) async-start(bf16[16,144,128]{2,1,0:T(8,128)(2,1)} %get-tuple-element.116), calls=%async_computation.5 | async-start | bytes 1179648 | tf_op jit(solution)/shard_map/all_to_all | solution.py:264
  137.1 5.8 %weight.12 = bf16[2048,1024]{1,0:T(8,128)(2,1)S(1)} custom-call(s32[3]{0:T(128)S(1)} %add_add_fusion.8.place), custom_call_target="tpu_custom_call" | custom-call | flops 41943040 | bytes 4194304 | tf_op jit(solution)/shard_map/weight/pallas_call | solution.py:104
  145.0 2.8 all-to-all-done.5.gathered
  153.6 2.5 collective-permute-start.18
  161.1 4.6 %all-to-all-start.6 = ((bf16[16,144,128]{2,1,0:T(8,128)(2,1)}), bf16[16,144,128]{2,1,0:T(8,128)(2,1)S(1)}, u32[]{:S(2)}, u32[]{:S(2)}) async-start(bf16[16,144,128]{2,1,0:T(8,128)(2,1)} %get-tuple-element.124), calls=%async_computation.6 | async-start | bytes 1179648 | tf_op jit(solution)/shard_map/all_to_all | solution.py:264
  166.4 5.8 %weight.13 = bf16[2048,1024]{1,0:T(8,128)(2,1)S(1)} custom-call(s32[3]{0:T(128)S(1)} %add_add_fusion.9.place), custom_call_target="tpu_custom_call" | custom-call | flops 41943040 | bytes 4194304 | tf_op jit(solution)/shard_map/weight/pallas_call | solution.py:104
  175.0 5.8 %weight.14 = bf16[2048,1024]{1,0:T(8,128)(2,1)S(1)} custom-call(s32[3]{0:T(128)S(1)} %add_add_fusion.10.place), custom_call_target="tpu_custom_call" | custom-call | flops 41943040 | bytes 4194304 | tf_op jit(solution)/shard_map/weight/pallas_call | solution.py:104
  183.6 5.8 %weight.15 = bf16[2048,1024]{1,0:T(8,128)(2,1)S(1)} custom-call(s32[3]{0:T(128)S(1)} %add_add_fusion.11.place), custom_call_target="tpu_custom_call" | custom-call | flops 41943040 | bytes 4194304 | tf_op jit(solution)/shard_map/weight/pallas_call | solution.py:104
  196.2 3.0 collective-permute-start.22
  204.2 7.2 %all-to-all-start.7 = ((bf16[16,144,128]{2,1,0:T(8,128)(2,1)}), bf16[16,144,128]{2,1,0:T(8,128)(2,1)S(1)}, u32[]{:S(2)}, u32[]{:S(2)}) async-start(bf16[16,144,128]{2,1,0:T(8,128)(2,1)} %get-tuple-element.132), calls=%async_computation.7 | async-start | bytes 1179648 | tf_op jit(solution)/shard_map/all_to_all | solution.py:264
  212.1 10.4 %all-to-all-done.7.gathered = bf16[16,144,128]{2,1,0:T(8,128)(2,1)S(1)} async-done(((bf16[16,144,128]{2,1,0:T(8,128)(2,1)}), bf16[16,144,128]{2,1,0:T(8,128)(2,1)S(1)}, u32[]{:S(2)}, u32[]{:S(2)}) %all-to-all-start.7) | async-done | bytes 589856 | tf_op jit(solution)/shard_map/all_to_all | solution.py:264
  235.6 3.6 %all-to-all-start.8 = ((bf16[16,144,128]{2,1,0:T(8,128)(2,1)}), bf16[16,144,128]{2,1,0:T(8,128)(2,1)S(1)}, u32[]{:S(2)}, u32[]{:S(2)}) async-start(bf16[16,144,128]{2,1,0:T(8,128)(2,1)} %get-tuple-element.140), calls=%async_computation.8 | async-start | bytes 1179648 | tf_op jit(solution)/shard_map/all_to_all | solution.py:264
  239.8 11.1 %all-to-all-done.8.gathered = bf16[16,144,128]{2,1,0:T(8,128)(2,1)S(1)} async-done(((bf16[16,144,128]{2,1,0:T(8,128)(2,1)}), bf16[16,144,128]{2,1,0:T(8,128)(2,1)S(1)}, u32[]{:S(2)}, u32[]{:S(2)}) %all-to-all-start.8) | async-done | bytes 589856 | tf_op jit(solution)/shard_map/all_to_all | solution.py:264
  255.7 2.5 collective-permute-start.30
  263.9 3.6 %all-to-all-start.9 = ((bf16[8,2,128,128]{3,2,1,0:T(8,128)(2,1)}), bf16[8,2,128,128]{3,2,1,0:T(8,128)(2,1)S(1)}, u32[]{:S(2)}, u32[]{:S(2)}) async-start(bf16[8,2,128,128]{3,2,1,0:T(8,128)(2,1)} %fusion.7), calls=%async_computation.9 | async-start | bytes 1048576 | tf_op jit(solution)/shard_map/all_to_all | solution.py:289
  268.3 9.6 %all-to-all-done.9.pieces = bf16[8,2,128,128]{3,2,1,0:T(8,128)(2,1)S(1)} async-done(((bf16[8,2,128,128]{3,2,1,0:T(8,128)(2,1)}), bf16[8,2,128,128]{3,2,1,0:T(8,128)(2,1)S(1)}, u32[]{:S(2)}, u32[]{:S(2)}) %all-to-all-start.9) | async-done | bytes 524320 | tf_op jit(solution)/shard_map/all_to_all | solution.py:289
  280.5 2.7 collective-permute-start.34
  287.7 2.7 collective-permute-start.37
  (183 shorter events, 151.3 us)
Async XLA Ops:
  2.6 9.7 %all-to-all-start = ((f32[8,2,128]{2,1,0:T(2,128)}), f32[8,2,128]{2,1,0:T(2,128)S(1)}, u32[]{:S(2)}, u32[]{:S(2)}) async-start(f32[8,2,128]{2,1,0:T(2,128)} %concatenate.3), calls=%async_computation | async-start | bytes 16384 | tf_op jit(solution)/shard_map/all_to_all | solution.py:250
  13.4 20.3 %all-to-all-start.1 = ((bf16[16,144,128]{2,1,0:T(8,128)(2,1)}), bf16[16,144,128]{2,1,0:T(8,128)(2,1)S(1)}, u32[]{:S(2)}, u32[]{:S(2)}) async-start(bf16[16,144,128]{2,1,0:T(8,128)(2,1)} %get-tuple-element.84), calls=%async_computation.1 | async-start | bytes 1179648 | tf_op jit(solution)/shard_map/all_to_all | solution.py:264
  38.1 5.4 %collective-permute-start.1 = (bf16[144,128]{1,0:T(8,128)(2,1)S(1)}, bf16[144,128]{1,0:T(8,128)(2,1)S(1)}, u32[]{:S(2)}, u32[]{:S(2)}) collective-permute-start(bf16[144,128]{1,0:T(8,128)(2,1)S(1)} %get-tuple-element.88), channel_id=1, source_target_pairs={{0,32},{16,48},{32,64},{48,80},{64,96},{80,112},{96,0},{112,16},{1... | collective-permute-start | bytes 110600 | tf_op jit(solution)/shard_map/ppermute | solution.py:280
  38.7 5.5 %collective-permute-start.2 = (bf16[144,128]{1,0:T(8,128)(2,1)S(1)}, bf16[144,128]{1,0:T(8,128)(2,1)S(1)}, u32[]{:S(2)}, u32[]{:S(2)}) collective-permute-start(bf16[144,128]{1,0:T(8,128)(2,1)S(1)} %get-tuple-element.89), channel_id=1, source_target_pairs={{0,64},{16,80},{32,96},{48,112},{64,0},{80,16},{96,32},{112,48},{1... | collective-permute-start | bytes 110600 | tf_op jit(solution)/shard_map/ppermute | solution.py:280
  45.8 15.4 %all-to-all-start.2 = ((bf16[16,144,128]{2,1,0:T(8,128)(2,1)}), bf16[16,144,128]{2,1,0:T(8,128)(2,1)S(1)}, u32[]{:S(2)}, u32[]{:S(2)}) async-start(bf16[16,144,128]{2,1,0:T(8,128)(2,1)} %get-tuple-element.92), calls=%async_computation.2 | async-start | bytes 1179648 | tf_op jit(solution)/shard_map/all_to_all | solution.py:264
  65.7 5.2 %collective-permute-start.5 = (bf16[144,128]{1,0:T(8,128)(2,1)S(1)}, bf16[144,128]{1,0:T(8,128)(2,1)S(1)}, u32[]{:S(2)}, u32[]{:S(2)}) collective-permute-start(bf16[144,128]{1,0:T(8,128)(2,1)S(1)} %get-tuple-element.96), channel_id=1, source_target_pairs={{0,32},{16,48},{32,64},{48,80},{64,96},{80,112},{96,0},{112,16},{1... | collective-permute-start | bytes 110600 | tf_op jit(solution)/shard_map/ppermute | solution.py:280
  67.2 5.5 %collective-permute-start.6 = (bf16[144,128]{1,0:T(8,128)(2,1)S(1)}, bf16[144,128]{1,0:T(8,128)(2,1)S(1)}, u32[]{:S(2)}, u32[]{:S(2)}) collective-permute-start(bf16[144,128]{1,0:T(8,128)(2,1)S(1)} %get-tuple-element.97), channel_id=1, source_target_pairs={{0,64},{16,80},{32,96},{48,112},{64,0},{80,16},{96,32},{112,48},{1... | collective-permute-start | bytes 110600 | tf_op jit(solution)/shard_map/ppermute | solution.py:280
  74.7 15.8 %all-to-all-start.3 = ((bf16[16,144,128]{2,1,0:T(8,128)(2,1)}), bf16[16,144,128]{2,1,0:T(8,128)(2,1)S(1)}, u32[]{:S(2)}, u32[]{:S(2)}) async-start(bf16[16,144,128]{2,1,0:T(8,128)(2,1)} %get-tuple-element.100), calls=%async_computation.3 | async-start | bytes 1179648 | tf_op jit(solution)/shard_map/all_to_all | solution.py:264
  94.9 5.5 %collective-permute-start.10 = (bf16[144,128]{1,0:T(8,128)(2,1)S(1)}, bf16[144,128]{1,0:T(8,128)(2,1)S(1)}, u32[]{:S(2)}, u32[]{:S(2)}) collective-permute-start(bf16[144,128]{1,0:T(8,128)(2,1)S(1)} %get-tuple-element.105), channel_id=1, source_target_pairs={{0,64},{16,80},{32,96},{48,112},{64,0},{80,16},{96,32},{112,48},{1... | collective-permute-start | bytes 110600 | tf_op jit(solution)/shard_map/ppermute | solution.py:280
  104.0 15.5 %all-to-all-start.4 = ((bf16[16,144,128]{2,1,0:T(8,128)(2,1)}), bf16[16,144,128]{2,1,0:T(8,128)(2,1)S(1)}, u32[]{:S(2)}, u32[]{:S(2)}) async-start(bf16[16,144,128]{2,1,0:T(8,128)(2,1)} %get-tuple-element.108), calls=%async_computation.4 | async-start | bytes 1179648 | tf_op jit(solution)/shard_map/all_to_all | solution.py:264
  123.9 5.3 %collective-permute-start.13 = (bf16[144,128]{1,0:T(8,128)(2,1)S(1)}, bf16[144,128]{1,0:T(8,128)(2,1)S(1)}, u32[]{:S(2)}, u32[]{:S(2)}) collective-permute-start(bf16[144,128]{1,0:T(8,128)(2,1)S(1)} %get-tuple-element.112), channel_id=1, source_target_pairs={{0,32},{16,48},{32,64},{48,80},{64,96},{80,112},{96,0},{112,16},{1... | collective-permute-start | bytes 110600 | tf_op jit(solution)/shard_map/ppermute | solution.py:280
  124.0 5.5 %collective-permute-start.14 = (bf16[144,128]{1,0:T(8,128)(2,1)S(1)}, bf16[144,128]{1,0:T(8,128)(2,1)S(1)}, u32[]{:S(2)}, u32[]{:S(2)}) collective-permute-start(bf16[144,128]{1,0:T(8,128)(2,1)S(1)} %get-tuple-element.113), channel_id=1, source_target_pairs={{0,64},{16,80},{32,96},{48,112},{64,0},{80,16},{96,32},{112,48},{1... | collective-permute-start | bytes 110600 | tf_op jit(solution)/shard_map/ppermute | solution.py:280
  131.5 16.3 %all-to-all-start.5 = ((bf16[16,144,128]{2,1,0:T(8,128)(2,1)}), bf16[16,144,128]{2,1,0:T(8,128)(2,1)S(1)}, u32[]{:S(2)}, u32[]{:S(2)}) async-start(bf16[16,144,128]{2,1,0:T(8,128)(2,1)} %get-tuple-element.116), calls=%async_computation.5 | async-start | bytes 1179648 | tf_op jit(solution)/shard_map/all_to_all | solution.py:264
  152.3 5.5 %collective-permute-start.17 = (bf16[144,128]{1,0:T(8,128)(2,1)S(1)}, bf16[144,128]{1,0:T(8,128)(2,1)S(1)}, u32[]{:S(2)}, u32[]{:S(2)}) collective-permute-start(bf16[144,128]{1,0:T(8,128)(2,1)S(1)} %get-tuple-element.120), channel_id=1, source_target_pairs={{0,32},{16,48},{32,64},{48,80},{64,96},{80,112},{96,0},{112,16},{1... | collective-permute-start | bytes 110600 | tf_op jit(solution)/shard_map/ppermute | solution.py:280
  153.6 5.5 %collective-permute-start.18 = (bf16[144,128]{1,0:T(8,128)(2,1)S(1)}, bf16[144,128]{1,0:T(8,128)(2,1)S(1)}, u32[]{:S(2)}, u32[]{:S(2)}) collective-permute-start(bf16[144,128]{1,0:T(8,128)(2,1)S(1)} %get-tuple-element.121), channel_id=1, source_target_pairs={{0,64},{16,80},{32,96},{48,112},{64,0},{80,16},{96,32},{112,48},{1... | collective-permute-start | bytes 110600 | tf_op jit(solution)/shard_map/ppermute | solution.py:280
  161.1 30.3 %all-to-all-start.6 = ((bf16[16,144,128]{2,1,0:T(8,128)(2,1)}), bf16[16,144,128]{2,1,0:T(8,128)(2,1)S(1)}, u32[]{:S(2)}, u32[]{:S(2)}) async-start(bf16[16,144,128]{2,1,0:T(8,128)(2,1)} %get-tuple-element.124), calls=%async_computation.6 | async-start | bytes 1179648 | tf_op jit(solution)/shard_map/all_to_all | solution.py:264
  196.2 5.5 %collective-permute-start.22 = (bf16[144,128]{1,0:T(8,128)(2,1)S(1)}, bf16[144,128]{1,0:T(8,128)(2,1)S(1)}, u32[]{:S(2)}, u32[]{:S(2)}) collective-permute-start(bf16[144,128]{1,0:T(8,128)(2,1)S(1)} %get-tuple-element.129), channel_id=1, source_target_pairs={{0,64},{16,80},{32,96},{48,112},{64,0},{80,16},{96,32},{112,48},{1... | collective-permute-start | bytes 110600 | tf_op jit(solution)/shard_map/ppermute | solution.py:280
  204.2 18.3 %all-to-all-start.7 = ((bf16[16,144,128]{2,1,0:T(8,128)(2,1)}), bf16[16,144,128]{2,1,0:T(8,128)(2,1)S(1)}, u32[]{:S(2)}, u32[]{:S(2)}) async-start(bf16[16,144,128]{2,1,0:T(8,128)(2,1)} %get-tuple-element.132), calls=%async_computation.7 | async-start | bytes 1179648 | tf_op jit(solution)/shard_map/all_to_all | solution.py:264
  228.3 5.5 %collective-permute-start.26 = (bf16[144,128]{1,0:T(8,128)(2,1)S(1)}, bf16[144,128]{1,0:T(8,128)(2,1)S(1)}, u32[]{:S(2)}, u32[]{:S(2)}) collective-permute-start(bf16[144,128]{1,0:T(8,128)(2,1)S(1)} %get-tuple-element.137), channel_id=1, source_target_pairs={{0,64},{16,80},{32,96},{48,112},{64,0},{80,16},{96,32},{112,48},{1... | collective-permute-start | bytes 110600 | tf_op jit(solution)/shard_map/ppermute | solution.py:280
  235.6 15.3 %all-to-all-start.8 = ((bf16[16,144,128]{2,1,0:T(8,128)(2,1)}), bf16[16,144,128]{2,1,0:T(8,128)(2,1)S(1)}, u32[]{:S(2)}, u32[]{:S(2)}) async-start(bf16[16,144,128]{2,1,0:T(8,128)(2,1)} %get-tuple-element.140), calls=%async_computation.8 | async-start | bytes 1179648 | tf_op jit(solution)/shard_map/all_to_all | solution.py:264
  255.3 5.4 %collective-permute-start.29 = (bf16[144,128]{1,0:T(8,128)(2,1)S(1)}, bf16[144,128]{1,0:T(8,128)(2,1)S(1)}, u32[]{:S(2)}, u32[]{:S(2)}) collective-permute-start(bf16[144,128]{1,0:T(8,128)(2,1)S(1)} %get-tuple-element.144), channel_id=1, source_target_pairs={{0,32},{16,48},{32,64},{48,80},{64,96},{80,112},{96,0},{112,16},{1... | collective-permute-start | bytes 110600 | tf_op jit(solution)/shard_map/ppermute | solution.py:280
  255.7 5.5 %collective-permute-start.30 = (bf16[144,128]{1,0:T(8,128)(2,1)S(1)}, bf16[144,128]{1,0:T(8,128)(2,1)S(1)}, u32[]{:S(2)}, u32[]{:S(2)}) collective-permute-start(bf16[144,128]{1,0:T(8,128)(2,1)S(1)} %get-tuple-element.145), channel_id=1, source_target_pairs={{0,64},{16,80},{32,96},{48,112},{64,0},{80,16},{96,32},{112,48},{1... | collective-permute-start | bytes 110600 | tf_op jit(solution)/shard_map/ppermute | solution.py:280
  263.9 13.9 %all-to-all-start.9 = ((bf16[8,2,128,128]{3,2,1,0:T(8,128)(2,1)}), bf16[8,2,128,128]{3,2,1,0:T(8,128)(2,1)S(1)}, u32[]{:S(2)}, u32[]{:S(2)}) async-start(bf16[8,2,128,128]{3,2,1,0:T(8,128)(2,1)} %fusion.7), calls=%async_computation.9 | async-start | bytes 1048576 | tf_op jit(solution)/shard_map/all_to_all | solution.py:289
  279.1 6.2 %collective-permute-start.32 = (f32[128,128]{1,0:T(8,128)S(1)}, f32[128,128]{1,0:T(8,128)S(1)}, u32[]{:S(2)}, u32[]{:S(2)}) collective-permute-start(f32[128,128]{1,0:T(8,128)S(1)} %get-tuple-element.156), channel_id=1, source_target_pairs={{0,2},{1,3},{2,0},{3,1},{4,6},{5,7},{6,4},{7,5},{8,10},{9,11},{10,... | collective-permute-start | bytes 196616 | tf_op jit(solution)/shard_map/ppermute | solution.py:193
  279.9 5.9 %collective-permute-start.33 = (f32[128,128]{1,0:T(8,128)S(1)}, f32[128,128]{1,0:T(8,128)S(1)}, u32[]{:S(2)}, u32[]{:S(2)}) collective-permute-start(f32[128,128]{1,0:T(8,128)S(1)} %get-tuple-element.156), channel_id=1, source_target_pairs={{0,1},{1,2},{2,3},{3,0},{4,5},{5,6},{6,7},{7,4},{8,9},{9,10},{10,1... | collective-permute-start | bytes 196616 | tf_op jit(solution)/shard_map/ppermute | solution.py:193
  280.5 5.3 %collective-permute-start.34 = (f32[128,128]{1,0:T(8,128)S(1)}, f32[128,128]{1,0:T(8,128)S(1)}, u32[]{:S(2)}, u32[]{:S(2)}) collective-permute-start(f32[128,128]{1,0:T(8,128)S(1)} %get-tuple-element.156), channel_id=1, source_target_pairs={{0,3},{1,0},{2,1},{3,2},{4,7},{5,4},{6,5},{7,6},{8,11},{9,8},{10,9... | collective-permute-start | bytes 196616 | tf_op jit(solution)/shard_map/ppermute | solution.py:193
  285.8 5.8 %collective-permute-start.35 = (f32[128,128]{1,0:T(8,128)S(1)}, f32[128,128]{1,0:T(8,128)S(1)}, u32[]{:S(2)}, u32[]{:S(2)}) collective-permute-start(f32[128,128]{1,0:T(8,128)S(1)} %add_add_fusion.3), channel_id=1, source_target_pairs={{0,8},{1,9},{2,10},{3,11},{4,12},{5,13},{6,14},{7,15},{8,0},{9,1},... | collective-permute-start | bytes 196616 | tf_op jit(solution)/shard_map/ppermute | solution.py:193
  287.1 5.5 %collective-permute-start.36 = (f32[128,128]{1,0:T(8,128)S(1)}, f32[128,128]{1,0:T(8,128)S(1)}, u32[]{:S(2)}, u32[]{:S(2)}) collective-permute-start(f32[128,128]{1,0:T(8,128)S(1)} %add_add_fusion.3), channel_id=1, source_target_pairs={{0,4},{1,5},{2,6},{3,7},{4,8},{5,9},{6,10},{7,11},{8,12},{9,13},{1... | collective-permute-start | bytes 196616 | tf_op jit(solution)/shard_map/ppermute | solution.py:193
  294.0 5.9 %collective-permute-start.38 = (f32[136,128]{1,0:T(8,128)S(1)}, f32[136,128]{1,0:T(8,128)S(1)}, u32[]{:S(2)}, u32[]{:S(2)}) collective-permute-start(f32[136,128]{1,0:T(8,128)S(1)} %get-tuple-element.157), channel_id=1, source_target_pairs={{0,2},{1,3},{2,0},{3,1},{4,6},{5,7},{6,4},{7,5},{8,10},{9,11},{10,... | collective-permute-start | bytes 208904 | tf_op jit(solution)/shard_map/ppermute | solution.py:193
  296.2 5.5 %collective-permute-start.39 = (f32[136,128]{1,0:T(8,128)S(1)}, f32[136,128]{1,0:T(8,128)S(1)}, u32[]{:S(2)}, u32[]{:S(2)}) collective-permute-start(f32[136,128]{1,0:T(8,128)S(1)} %get-tuple-element.157), channel_id=1, source_target_pairs={{0,1},{1,2},{2,3},{3,0},{4,5},{5,6},{6,7},{7,4},{8,9},{9,10},{10,1... | collective-permute-start | bytes 208904 | tf_op jit(solution)/shard_map/ppermute | solution.py:193
  302.5 5.9 %collective-permute-start.41 = (f32[136,128]{1,0:T(8,128)S(1)}, f32[136,128]{1,0:T(8,128)S(1)}, u32[]{:S(2)}, u32[]{:S(2)}) collective-permute-start(f32[136,128]{1,0:T(8,128)S(1)} %add_add_fusion.1), channel_id=1, source_target_pairs={{0,8},{1,9},{2,10},{3,11},{4,12},{5,13},{6,14},{7,15},{8,0},{9,1},... | collective-permute-start | bytes 208904 | tf_op jit(solution)/shard_map/ppermute | solution.py:193
  304.7 5.5 %collective-permute-start.42 = (f32[136,128]{1,0:T(8,128)S(1)}, f32[136,128]{1,0:T(8,128)S(1)}, u32[]{:S(2)}, u32[]{:S(2)}) collective-permute-start(f32[136,128]{1,0:T(8,128)S(1)} %add_add_fusion.1), channel_id=1, source_target_pairs={{0,4},{1,5},{2,6},{3,7},{4,8},{5,9},{6,10},{7,11},{8,12},{9,13},{1... | collective-permute-start | bytes 208904 | tf_op jit(solution)/shard_map/ppermute | solution.py:193
  (39 other events, 373.7 us)

commit v2 on v1

v2 whole, which is shorter than its diff:
```python
import functools
import math

import jax
import jax.numpy as jnp
import numpy as np
from jax import lax
from jax.experimental import pallas as pl
from jax.experimental.pallas import tpu as pltpu
from jax.sharding import PartitionSpec as P

D = 16384
R = 128
TOK = 128
LAYERS = 8
SEG = 8
MP = 16
WIDTH = D // MP
PIECE = WIDTH // SEG
ROWS = TOK + 16
EPSILON = 1e-05
EMBED_KEY = 7919
BF = jnp.bfloat16
F32 = jnp.float32


def wrapped(value):
    value &= 0xFFFFFFFF
    return np.int32(value - (1 << 32) if value >> 31 else value)


MULT = wrapped(73244475)
MULT_SQ = wrapped(73244475 * 73244475)


def fold(bits):
    return jnp.bitwise_xor(bits, lax.shift_right_logical(bits, jnp.int32(16)))


def uniform_bits(mixed_bits):
    mixed_bits = fold(mixed_bits) * MULT
    mixed_bits = fold(mixed_bits) * MULT_SQ
    mixed_bits = fold(mixed_bits) * MULT
    return lax.shift_right_logical(fold(mixed_bits), jnp.int32(8))


def hashed(mixed_bits, magnitude):
    return uniform_bits(mixed_bits).astype(F32) * np.float32(magnitude * 2.0 / 16777216.0) - np.float32(magnitude)


def ternary(mixed_bits, magnitude):
    bits = uniform_bits(mixed_bits)
    return (lax.rem(bits, jnp.int32(3)) - jnp.int32(1)).astype(F32) * np.float32(magnitude)


def split_row(row):
    high = row.astype(BF).astype(F32)
    index = lax.broadcasted_iota(jnp.int32, (16, row.shape[1]), 0)
    tile = jnp.where(index == 0, high, jnp.where(index == 1, row - high, 0.0))
    return tile.astype(BF)


def joined_row(tile):
    return jnp.sum(tile.astype(F32), axis=0, keepdims=True)


SMEM = pl.BlockSpec(memory_space=pltpu.SMEM)
VMEM = pl.BlockSpec(memory_space=pltpu.VMEM)
HBM = pl.BlockSpec(memory_space=pltpu.HBM)


def call(body, name, out_shape, in_specs, flops=0, nbytes=0, limit=8 << 20, out_specs=None, scratch=(), aliases={}):
    single = not isinstance(out_shape, (tuple, list))
    return pl.pallas_call(
        body,
        out_shape=out_shape,
        in_specs=in_specs,
        out_specs=out_specs or (VMEM if single else tuple(VMEM for _ in out_shape)),
        scratch_shapes=scratch,
        input_output_aliases=aliases,
        name=name,
        cost_estimate=pl.CostEstimate(flops=flops, bytes_accessed=nbytes, transcendentals=0),
        compiler_params=pltpu.CompilerParams(vmem_limit_bytes=limit),
    )


def sds(shape, dtype):
    return jax.ShapeDtypeStruct(shape, dtype)


def gate(value, *others):
    return lax.optimization_barrier((value, *others))[0]


def pack_kernel(seed, gain, out):
    row = jnp.full((1, PIECE), seed[0], jnp.int32).astype(F32)
    for index in range(SEG):
        part = gain[:, index * PIECE : (index + 1) * PIECE].astype(F32)
        for target in range(SEG):
            out[target, index : index + 1, :] = part
    for target in range(SEG):
        out[target, SEG:, :] = jnp.broadcast_to(row, (SEG, PIECE))


def embed_kernel(place, token, stream_out, piece_out, tile_out):
    tokens = jnp.broadcast_to(token[...], (TOK, PIECE)) * 16411 + wrapped(EMBED_KEY * 1000003)
    tokens = tokens + lax.broadcasted_iota(jnp.int32, (TOK, PIECE), 1)
    squares = jnp.zeros((TOK, PIECE), F32)
    for index in range(SEG):
        part = hashed(tokens + (place[0] + index * PIECE), math.sqrt(3.0)).astype(BF)
        stream_out[:, index * PIECE : (index + 1) * PIECE] = part
        wide = part.astype(F32)
        squares = squares + wide * wide
    piece_out[...] = hashed(tokens + (place[0] + place[1] * PIECE), math.sqrt(3.0)).astype(BF)
    tile_out[...] = split_row(jnp.sum(jnp.transpose(squares), axis=0, keepdims=True))


def first_weight_kernel(place, out):
    chunk = 16
    shape = (chunk, MP * PIECE)
    row = lax.broadcasted_iota(jnp.int32, shape, 0)
    col = lax.broadcasted_iota(jnp.int32, shape, 1)
    base = row * 16411 + (col // PIECE) * WIDTH + col % PIECE + place[0]

    def step(index, carry):
        start = pl.multiple_of(index * chunk, chunk)
        out[pl.ds(start, chunk), :] = hashed(base + index * (chunk * 16411), math.sqrt(3.0 / D)).astype(BF)
        return carry

    lax.fori_loop(0, WIDTH // chunk, step, 0, unroll=2)


WIDE = 256
PARTS = WIDTH // WIDE


def weight_kernel(layer, place, *refs):
    out, slots, sems = refs[-3:]
    chunk, tall, depth = 64, 256, 4
    row = lax.broadcasted_iota(jnp.int32, (chunk, WIDTH), 0)
    col = lax.broadcasted_iota(jnp.int32, (chunk, WIDTH), 1)
    base = row * 16411 + col + place[layer]

    def copy(index, slot):
        start = pl.multiple_of(index * tall, tall)
        return pltpu.make_async_copy(slots.at[slot], out.at[layer - 1, :, pl.ds(start, tall), :], sems.at[slot])

    def fill(index, slot):
        def step(part, carry):
            first = (2 * index + part // 2) * (WIDTH * 16411) + (part % 2) * (chunk * 16411)
            made = hashed(base + first, math.sqrt(3.0 / D)).astype(BF)
            start = pl.multiple_of(part * chunk, chunk)
            for wide in range(PARTS):
                slots[slot, wide, pl.ds(start, chunk), :] = made[:, wide * WIDE : (wide + 1) * WIDE]
            return carry

        lax.fori_loop(0, tall // chunk, step, 0, unroll=2)
        copy(index, slot).start()

    def first_round(slot, carry):
        fill(slot, slot)
        return carry

    def second_round(slot, carry):
        copy(slot, slot).wait()
        fill(depth + slot, slot)
        return carry

    lax.fori_loop(0, depth, first_round, 0)
    lax.fori_loop(0, depth, second_round, 0)
    for slot in range(depth):
        copy(depth + slot, slot).wait()


WEIGHTS = MP * PIECE * WIDTH


def teacher_weight(layer, place, stored=None):
    cost = dict(flops=20 * WEIGHTS, nbytes=2 * WEIGHTS)
    if layer == 0:
        return call(first_weight_kernel, "first_weight", sds((WIDTH, MP * PIECE), BF), [SMEM], **cost)(place)
    return call(
        functools.partial(weight_kernel, layer),
        "weight",
        sds((LAYERS - 1, PARTS, MP * PIECE, WIDE), BF),
        [SMEM] + [HBM] * (layer > 1),
        out_specs=HBM,
        scratch=(pltpu.VMEM((4, PARTS, 256, WIDE), BF), pltpu.SemaphoreType.DMA((4,))),
        limit=40 << 20,
        aliases={1: 0} if layer > 1 else {},
        **cost,
    )(place, *([stored] if layer > 1 else []))


def first_contract_kernel(stream, tile, facts, weight, out):
    parts = []
    for index in range(SEG):
        part = stream[:, index * PIECE : (index + 1) * PIECE].astype(F32)
        parts.append((part * facts[0, index : index + 1, :]).astype(BF))
    scaled = jnp.concatenate(parts, axis=1)
    squares = tile[...]
    for index in range(MP // 2):
        part = jnp.dot(scaled, weight[:, index * 256 : (index + 1) * 256], preferred_element_type=F32)
        for half in range(2):
            out[2 * index + half, :TOK, :] = part[:, half * PIECE : (half + 1) * PIECE].astype(BF)
            out[2 * index + half, TOK:, :] = squares


def message(out, sems, held, stream, gain):
    wide = stream.astype(F32)
    scaled = (wide * gain).astype(BF)
    tile = split_row(jnp.sum(jnp.transpose(wide * wide), axis=0, keepdims=True))
    for index in range(4):
        held[index, :TOK, :] = scaled
        held[index, TOK:, :] = tile
    copies = [pltpu.make_async_copy(held, out.at[pl.ds(4 * index, 4)], sems.at[index]) for index in range(MP // 4)]
    for copy in copies:
        copy.start()
    for copy in copies:
        copy.wait()


def advance(layer, total, stream, gains, stream_out, mean_out, message_out, held, sems):
    squares = joined_row(total[TOK:])
    mean = jnp.transpose(jnp.broadcast_to(squares, (TOK, TOK))) * np.float32(1.0 / D)
    mean_out[...] = mean
    result = (stream[...].astype(F32) + total[:TOK] * lax.rsqrt(mean + EPSILON)).astype(BF)
    stream_out[...] = result
    message(message_out, sems, held, result, gains[layer + 1 : layer + 2, :])


def first_update_kernel(parts, stream, gains, stream_out, mean_out, message_out, held, sems):
    total = parts[0].astype(F32)
    for index in range(1, MP):
        total = total + parts[index].astype(F32)
    advance(0, total, stream, gains, stream_out, mean_out, message_out, held, sems)


def update_kernel(layer, own, part_a, part_b, part_c, stream, gains, stream_out, mean_out, message_out, held, sems):
    total = own[...]
    for part in (part_a, part_b, part_c):
        total = total + part[...].astype(F32)
    advance(layer, total, stream, gains, stream_out, mean_out, message_out, held, sems)


def contract_kernel(layer, place, gathered, weight, own_out, other_out, held, sems):
    half = MP * PIECE // 2
    copies = []
    for part in range(PARTS):
        for rows in range(2):
            where = (part, pl.ds(rows * half, half))
            copies.append(pltpu.make_async_copy(weight.at[(layer - 1, *where)], held.at[where], sems.at[part, rows]))
    for copy in copies:
        copy.start()
    scaled = jnp.concatenate([gathered[index, :TOK, :] for index in range(MP)], axis=1)
    squares = joined_row(gathered[0, TOK:, :])
    for index in range(1, MP):
        squares = squares + joined_row(gathered[index, TOK:, :])
    tile = split_row(squares)
    first = place[0] == 0
    for chunk in range(4):
        copies[2 * chunk].wait()
        copies[2 * chunk + 1].wait()
        part = jnp.dot(scaled, held[chunk], preferred_element_type=F32)
        left, right = part[:, :PIECE], part[:, PIECE:]
        own_out[chunk, :TOK, :] = jnp.where(first, left, right)
        other_out[chunk, :TOK, :] = jnp.where(first, right, left).astype(BF)
        own_out[chunk, TOK:, :] = tile.astype(F32)
        other_out[chunk, TOK:, :] = tile


def packed(both, out):
    out[:TOK, :] = both[:TOK].astype(BF)
    out[TOK:, :] = split_row(joined_row(both[TOK:]))


def pair_kernel(place, own, other, kept, send_a, send_b, send_c):
    here = place[0]
    kept[...] = own[here] + other[here].astype(F32)
    for shift, out in ((1, send_a), (2, send_b), (3, send_c)):
        chunk = lax.rem(here + shift, 4)
        packed(own[chunk] + other[chunk].astype(F32), out)


def last_pair_kernel(own, other, kept, send):
    for chunk in range(4):
        both = own[chunk] + other[chunk].astype(F32)
        kept[chunk] = both
        packed(both, send.at[chunk])


def last_update_kernel(place, kept, part_a, part_b, part_c, pieces, stream_out, mean_out):
    core = place[1]
    last = place[0] == SEG - 1
    for chunk in range(4):
        total = kept[chunk]
        for part in (part_a, part_b, part_c):
            total = total + part[chunk].astype(F32)
        if chunk == 0:
            squares = joined_row(total[TOK:])
            mean = jnp.transpose(jnp.broadcast_to(squares, (TOK, TOK))) * np.float32(1.0 / D)
            mean_out[...] = mean
            scale = lax.rsqrt(mean + EPSILON)
        before = pieces[2 * chunk + core].astype(F32)
        stream = jnp.where(last, before[0], before[1])
        stream_out[chunk] = (stream + total[:TOK] * scale).astype(BF)


def gather_kernel(place, *refs):
    streams, means = refs[:LAYERS], refs[LAYERS : 2 * LAYERS - 1]
    outs, mean_out, held = refs[2 * LAYERS - 1 : -2], refs[-2], refs[-1]
    for layer in range(LAYERS):
        held[layer] = streams[layer][...]
    held[LAYERS] = streams[LAYERS - 1][...]
    for partner in range(SEG):
        outs[partner][...] = held[pl.ds(jnp.bitwise_xor(place[0], partner), 2)]
    mean = means[0][...]
    for layer in range(1, LAYERS - 1):
        mean = jnp.where(place[0] == layer, means[layer][...], mean)
    mean_out[...] = mean


def partners(partner):
    return [(i, i ^ partner) for i in range(SEG)]


CORE = [(i, i ^ 1) for i in range(SEG)]


def along_x(shift):
    return [(i, (i + 2 * shift) % SEG) for i in range(SEG)]


def to_last(column):
    return [(2 * column + core, SEG - 2 + core) for core in range(2)]


def along_y(shift):
    return [(i, i // 4 * 4 + (i + shift) % 4) for i in range(MP)]


def along_z(shift):
    return [(i, (i + 4 * shift) % MP) for i in range(MP)]


def sum_mp(value):
    for along in (along_y, along_z):
        parts = [lax.ppermute(value, "mp", along(shift)) for shift in (1, 2, 3)]
        value = (value + parts[1]) + (parts[0] + parts[2])
    return value


def ternary_base(place):
    row = lax.broadcasted_iota(jnp.int32, (PIECE, R), 0)
    rank = lax.broadcasted_iota(jnp.int32, (PIECE, R), 1)
    return row * 16411 + rank + place


def student_up_kernel(place, gain, *refs):
    parts, pieces, pre_out = refs[:SEG], refs[SEG], refs[SEG + 1]
    for partner in range(SEG):
        pieces[jnp.bitwise_xor(place[0], partner)] = parts[partner][...]
    base = ternary_base(place[2])
    total = jnp.zeros((TOK, R), F32)
    for index in range(SEG):
        up_weight = ternary(base + index * PIECE * 16411, math.sqrt(1.5 / D)).astype(BF)
        scaled = (pieces[index, 0].astype(F32) * gain[:, index * PIECE : (index + 1) * PIECE].astype(F32)).astype(BF)
        total = total + jnp.dot(scaled, up_weight, preferred_element_type=F32)
    pre_out[...] = total


def student_error_kernel(place, pieces, own, other, pre, mean, last_mean, back_out, scaled_out, squared_out, pre_out):
    last = place[0] == SEG - 1
    first = place[1] == 0
    base = ternary_base(place[2] + R)
    scale = lax.rsqrt(jnp.where(last, last_mean[...], mean[...]) + EPSILON)
    rectified = jnp.maximum(pre[...] * scale, 0.0)
    pre_out[...] = rectified
    squared = (rectified * rectified).astype(BF)
    squared_out[...] = squared
    back = jnp.zeros((TOK, R), F32)
    squares = jnp.zeros((TOK, PIECE), F32)
    for index in range(SEG):
        down_weight = ternary(base + index * PIECE * 16411, math.sqrt(1.5 / R)).astype(BF)
        student = lax.dot_general(squared, down_weight, (((1,), (1,)), ((), ())), preferred_element_type=F32)
        mine, theirs = own[index // 2].astype(F32), other[index // 2].astype(F32)
        final = jnp.where(first, mine, theirs) if index % 2 == 0 else jnp.where(first, theirs, mine)
        target = jnp.where(last, final, pieces[index, 1].astype(F32))
        error = pieces[index, 0].astype(F32) + student - target
        squares = squares + error * error
        scaled = (error * np.float32(1.0 / TOK)).astype(BF)
        scaled_out[:, index * PIECE : (index + 1) * PIECE] = scaled
        back = back + jnp.dot(scaled, down_weight, preferred_element_type=F32)
    back_out[:TOK, :] = back
    back_out[TOK:, :] = jnp.sum(squares.reshape(TOK // 8, 8, PIECE), axis=0)


OVER_TOKENS = (((0,), (0,)), ((), ()))


def student_down_kernel(place, pieces, gain, mean, last_mean, scaled, squared, normed_out, down_out):
    scale = lax.rsqrt(jnp.where(place[0] == SEG - 1, last_mean[...], mean[...]) + EPSILON)
    for index in range(SEG):
        columns = slice(index * PIECE, (index + 1) * PIECE)
        normed = pieces[index, 0].astype(F32) * scale * gain[:, columns].astype(F32)
        normed_out[:, columns] = normed.astype(BF)
    down_out[...] = lax.dot_general(scaled[...], squared[...], OVER_TOKENS, preferred_element_type=F32)


def student_grad_kernel(normed, rectified, back, up_out, loss_out):
    back_pre = (back[:TOK, :] * 2.0 * rectified[...]).astype(BF)
    up_out[...] = lax.dot_general(normed[...], back_pre, OVER_TOKENS, preferred_element_type=F32)
    total = jnp.sum(jnp.sum(back[TOK:, :], axis=0, keepdims=True), axis=1, keepdims=True)
    loss_out[...] = total * np.float32(1.0 / (TOK * D))


def local(token_ids, teacher_seeds, student_seeds, teacher_gain, student_gain):
    block = lax.axis_index("mp")
    segment = lax.axis_index("segment")
    core = lax.rem(segment, 2)
    column = segment // 2
    piece_shape = sds((TOK, PIECE), BF)
    mean_shape = sds((TOK, TOK), F32)
    message_shape = sds((MP, ROWS, PIECE), BF)

    facts = call(pack_kernel, "pack", sds((SEG, 2 * SEG, PIECE), F32), [SMEM, VMEM])(teacher_seeds, teacher_gain)
    facts = lax.all_to_all(facts, "segment", split_axis=0, concat_axis=0, tiled=True)
    embedded, stream, tile = call(
        embed_kernel, "embed", (sds((TOK, WIDTH), BF), piece_shape, sds((16, TOK), BF)), [SMEM, VMEM]
    )(jnp.stack([block * WIDTH, segment]), token_ids.reshape(TOK, 1))
    here = segment * PIECE * 16411 + block * WIDTH
    first_here = block * (WIDTH * 16411) + segment * PIECE
    at_start = jnp.arange(LAYERS, dtype=jnp.int32) == 0
    places = facts[:, SEG, 0].astype(jnp.int32) * 1000003 + jnp.where(at_start, first_here, here)
    gains = lax.dynamic_index_in_dim(facts, segment, 1, False)

    weight = teacher_weight(0, places)
    outgoing = call(
        first_contract_kernel, "first_contract", message_shape, [VMEM] * 4, flops=2 * TOK * WEIGHTS, nbytes=2 * WEIGHTS
    )(embedded, tile, facts, weight)
    parts = lax.all_to_all(outgoing, "mp", split_axis=0, concat_axis=0, tiled=True)
    weight = teacher_weight(1, gate(places, outgoing))
    parts, weight = lax.optimization_barrier((parts, weight))
    advance_out = dict(
        out_shape=(piece_shape, mean_shape, message_shape),
        out_specs=(VMEM, VMEM, HBM),
        scratch=(pltpu.VMEM((4, ROWS, PIECE), BF), pltpu.SemaphoreType.DMA((MP // 4,))),
    )
    stream_new, mean, outgoing = call(first_update_kernel, "first_update", in_specs=[VMEM] * 3, **advance_out)(
        parts, stream, gains
    )
    streams, means = [stream, stream_new], [mean]
    for layer in range(1, LAYERS):
        gathered = lax.all_to_all(outgoing, "mp", split_axis=0, concat_axis=0, tiled=True)
        if layer + 1 < LAYERS:
            weight = teacher_weight(layer + 1, gate(places, outgoing), weight)
            gathered, weight = lax.optimization_barrier((gathered, weight))
        else:
            place = jnp.stack([segment, core, student_seeds[0] * 1000003 + block * (WIDTH * 16411)])
            *pairs, mean = call(
                gather_kernel,
                "gather",
                tuple(sds((2, TOK, PIECE), BF) for _ in range(SEG)) + (mean_shape,),
                [SMEM] + [VMEM] * (2 * LAYERS - 1),
                scratch=(pltpu.VMEM((LAYERS + 1, TOK, PIECE), BF),),
            )(place, *streams, *means)
            pairs[1:] = [lax.ppermute(pairs[partner], "segment", partners(partner)) for partner in range(1, SEG)]
            gathered = gate(gathered, *pairs)
        own, other = call(
            functools.partial(contract_kernel, layer),
            "contract",
            (sds((4, ROWS, PIECE), F32), sds((4, ROWS, PIECE), BF)),
            [SMEM, VMEM, HBM],
            flops=2 * TOK * WEIGHTS,
            nbytes=2 * WEIGHTS,
            limit=40 << 20,
            scratch=(pltpu.VMEM((PARTS, MP * PIECE, WIDE), BF), pltpu.SemaphoreType.DMA((PARTS, 2))),
        )(core.reshape(1), gathered, weight)
        other = lax.ppermute(other, "segment", CORE)
        if layer + 1 == LAYERS:
            break
        kept, *sends = call(
            pair_kernel,
            "pair",
            (sds((ROWS, PIECE), F32),) + tuple(sds((ROWS, PIECE), BF) for _ in range(3)),
            [SMEM, VMEM, VMEM],
        )(column.reshape(1), own, other)
        parts = [lax.ppermute(send, "segment", along_x(shift)) for shift, send in zip((1, 2, 3), sends)]
        stream, mean, outgoing = call(
            functools.partial(update_kernel, layer), "update", in_specs=[VMEM] * 6, **advance_out
        )(kept, *parts, streams[-1], gains)
        streams.append(stream)
        means.append(mean)

    kept, send = call(
        last_pair_kernel, "last_pair", (sds((4, ROWS, PIECE), F32), sds((4, ROWS, PIECE), BF)), [VMEM] * 2
    )(own, other)
    parts = [lax.ppermute(send, "segment", to_last(source)) for source in range(3)]
    student_columns = lax.dynamic_slice_in_dim(student_gain, block * WIDTH, WIDTH, 1)
    pieces, pre = call(
        student_up_kernel,
        "student_up",
        (sds((SEG, 2, TOK, PIECE), BF), sds((TOK, R), F32)),
        [SMEM] + [VMEM] * (SEG + 1),
    )(place, student_columns, gate(pairs[0], send), *pairs[1:])
    pre = sum_mp(pre)
    last_own, last_mean = call(
        last_update_kernel, "last_update", (sds((4, TOK, PIECE), BF), mean_shape), [SMEM] + [VMEM] * 5
    )(place, kept, *parts, pieces)
    last_other = lax.ppermute(last_own, "segment", CORE)

    back, scaled, squared, rectified = call(
        student_error_kernel,
        "student_error",
        (sds((TOK + 8, R), F32), sds((TOK, WIDTH), BF), sds((TOK, R), BF), sds((TOK, R), F32)),
        [SMEM] + [VMEM] * 6,
    )(place, pieces, last_own, last_other, pre, mean, last_mean)
    normed, grad_down = call(
        student_down_kernel, "student_down", (sds((TOK, WIDTH), BF), sds((WIDTH, R), F32)), [SMEM] + [VMEM] * 6
    )(place, pieces, student_columns, mean, last_mean, scaled, squared)
    back = sum_mp(back)
    grad_up, loss = call(
        student_grad_kernel, "student_grad", (sds((WIDTH, R), F32), sds((1, 1), F32)), [VMEM] * 3
    )(normed, rectified, back)
    return loss.reshape(1), grad_up[None], grad_down[None]


def solution(mesh):
    in_specs = (P(), P("segment"), P("segment"), P("segment", "mp"), P("segment", None))
    out_specs = (P("segment"), P("segment", "mp", None), P("segment", "mp", None))
    return jax.shard_map(local, mesh=mesh, in_specs=in_specs, out_specs=out_specs, check_vma=False)
```

time: 316 us -> 272 us (0.86)
  local copies, waits for them, and re-layouts: 36.6 us -> 1.48 us
  Pallas kernels: 65.7 us -> 86.4 us
  other arithmetic: 12.1 us -> 0.48 us
  waiting for transfers between devices: 94.5 us -> 84 us
  starting transfers between devices: 102 us -> 94.9 us
    unnamed x41 -> x8, local copies, waits for them, and re-layouts: 33.6 us -> 0.7 us
    pallas_call x26 -> x31, Pallas kernels: 63.8 us -> 84.6 us  [the longest x7 42.8 us: teacher_weight(): call(functools.partial(weight_kernel, layer), 'weight', sds((LAYERS - 1,...]
    ppermute x0 -> x11, starting transfers between devices: none -> 12.5 us  [the longest x7 8.17 us: local(): lax.ppermute(pairs[partner], 'segment', partners(partner))]
    all_to_all x2 -> x1, waiting for transfers between devices: 14.1 us -> 3.69 us  [local(): lax.all_to_all(facts, 'segment', split_axis=0, concat_axis=0, tiled=True)]
    ppermute x24 -> x18, starting transfers between devices: 31.9 us -> 22.6 us  [local(): lax.ppermute(send, 'segment', along_x(shift))]
    all_to_all x8, starting transfers between devices: 41.7 us -> 33.2 us  [local(): lax.all_to_all(outgoing, 'mp', split_axis=0, concat_axis=0, tiled=True)]
    another operation x10 -> x2, other arithmetic: 6.21 us -> 0.15 us  [the longest x1 0.08 us: local(): jnp.stack([segment, core, student_seeds[0] * 1000003 + block * (WIDTH * 1...]
    ppermute x0 -> x11, waiting for transfers between devices: none -> 5.96 us  [the longest x7 5.09 us: local(): lax.ppermute(pairs[partner], 'segment', partners(partner))]
  transfers between devices with their start and end apart: 54 -> 57, of which waited for: 50 -> 44; matrix products, arithmetic and copies ran while one was open for 4% -> 0% of each run, Pallas kernels for 15% -> 17%
where the time goes in v2:
time: 272 us; the launch traced here: 270 us
  starting transfers between devices  94.9 us (35%)
  Pallas kernels  86.4 us (32%)
  waiting for transfers between devices  84 us (31%)
    pallas_call x7, Pallas kernels, teacher_weight(): call(functools.partial(weight_kernel, layer), 'weight', sds((LAYERS - 1,...  42.8 us
    all_to_all x8, waiting for transfers between devices, local(): lax.all_to_all(outgoing, 'mp', split_axis=0, concat_axis=0, tiled=True)  37.7 us
    all_to_all x8, starting transfers between devices, local(): lax.all_to_all(outgoing, 'mp', split_axis=0, concat_axis=0, tiled=True)  33.2 us
    ppermute x18, starting transfers between devices, local(): lax.ppermute(send, 'segment', along_x(shift))  22.6 us
    ppermute x12, starting transfers between devices, sum_mp(): parts = [lax.ppermute(value, 'mp', along(shift)) for shift in (1, 2, 3)]  21.6 us
    ppermute x18, waiting for transfers between devices, local(): lax.ppermute(send, 'segment', along_x(shift))  21.2 us
    pallas_call x7, Pallas kernels, local(): call(functools.partial(contract_kernel, layer), 'contract', (sds((4, ROWS...  20.7 us
    ppermute x7, waiting for transfers between devices, local(): other = lax.ppermute(other, 'segment', CORE)  9.38 us
  transfers between devices with their start and end apart: 57, of which 44 were waited for; matrix products, arithmetic and copies ran while one was open for 0% of the time, Pallas kernels for 17%

profile of v2, /device:TPU:0, one launch (start us, length us, event | category | flops | bytes accessed | tf_op | source)
XLA Modules:
  0.0 269.8 jit_solution(1518846742013656232)
XLA Ops:
  2.7 4.4 %all-to-all-start = ((f32[8,16,128]{2,1,0:T(8,128)}), f32[8,16,128]{2,1,0:T(8,128)S(1)}, u32[]{:S(2)}, u32[]{:S(2)}) async-start(f32[8,16,128]{2,1,0:T(8,128)} %pack.1), calls=%async_computation | async-start | bytes 131072 | tf_op jit(solution)/shard_map/all_to_all | solution.py:427
  9.0 3.7 %all-to-all-done.facts = f32[8,16,128]{2,1,0:T(8,128)S(1)} async-done(((f32[8,16,128]{2,1,0:T(8,128)}), f32[8,16,128]{2,1,0:T(8,128)S(1)}, u32[]{:S(2)}, u32[]{:S(2)}) %all-to-all-start) | async-done | bytes 65568 | tf_op jit(solution)/shard_map/all_to_all | solution.py:427
  12.9 5.2 %first_weight.1.weight = bf16[1024,2048]{1,0:T(8,128)(2,1)S(1)} custom-call(s32[8]{0:T(128)S(1)} %fusion.2.place), custom_call_target="tpu_custom_call" | custom-call | flops 41943040 | bytes 4194304 | tf_op jit(solution)/shard_map/first_weight/pallas_call | solution.py:181
  19.7 8.0 %all-to-all-start.1 = ((bf16[16,144,128]{2,1,0:T(8,128)(2,1)}), bf16[16,144,128]{2,1,0:T(8,128)(2,1)S(1)}, u32[]{:S(2)}, u32[]{:S(2)}) async-start(bf16[16,144,128]{2,1,0:T(8,128)(2,1)} %first_contract.1), calls=%async_computation.1 | async-start | bytes 1179648 | tf_op jit(solution)/shard_map/all_to_all | solution.py:441
  27.8 6.1 %weight.7.refs_0_ = bf16[7,4,2048,256]{3,2,1,0:T(8,128)(2,1)} custom-call(s32[8]{0:T(128)S(1)} %fusion.2.place), custom_call_target="tpu_custom_call" | custom-call | flops 41943040 | bytes 4194304 | tf_op jit(solution)/shard_map/weight/pallas_call | solution.py:182
  33.9 6.0 %all-to-all-done.1.parts = bf16[16,144,128]{2,1,0:T(8,128)(2,1)S(1)} async-done(((bf16[16,144,128]{2,1,0:T(8,128)(2,1)}), bf16[16,144,128]{2,1,0:T(8,128)(2,1)S(1)}, u32[]{:S(2)}, u32[]{:S(2)}) %all-to-all-start.1) | async-done | bytes 589856 | tf_op jit(solution)/shard_map/all_to_all | solution.py:441
  41.0 3.6 %all-to-all-start.2 = ((bf16[16,144,128]{2,1,0:T(8,128)(2,1)}), bf16[16,144,128]{2,1,0:T(8,128)(2,1)S(1)}, u32[]{:S(2)}, u32[]{:S(2)}) async-start(bf16[16,144,128]{2,1,0:T(8,128)(2,1)} %get-tuple-element.117), calls=%async_computation.2 | async-start | bytes 1179648 | tf_op jit(solution)/shard_map/all_to_all | solution.py:454
  44.6 6.1 %weight.8.refs_0_ = bf16[7,4,2048,256]{3,2,1,0:T(8,128)(2,1)} custom-call(s32[8]{0:T(128)S(1)} %fusion.2.place, bf16[7,4,2048,256]{3,2,1,0:T(8,128)(2,1)} %weight.7.refs_0_), custom_call_target="tpu_custom_call", output_to_operand_aliasing={{}: (1, {})} | custom-call | flops 41943040 | bytes 4194304 | tf_op jit(solution)/shard_map/weight/pallas_call | solution.py:182
  50.7 4.9 %all-to-all-done.2.gathered = bf16[16,144,128]{2,1,0:T(8,128)(2,1)S(1)} async-done(((bf16[16,144,128]{2,1,0:T(8,128)(2,1)}), bf16[16,144,128]{2,1,0:T(8,128)(2,1)S(1)}, u32[]{:S(2)}, u32[]{:S(2)}) %all-to-all-start.2) | async-done | bytes 589856 | tf_op jit(solution)/shard_map/all_to_all | solution.py:454
  67.8 3.6 %all-to-all-start.3 = ((bf16[16,144,128]{2,1,0:T(8,128)(2,1)}), bf16[16,144,128]{2,1,0:T(8,128)(2,1)S(1)}, u32[]{:S(2)}, u32[]{:S(2)}) async-start(bf16[16,144,128]{2,1,0:T(8,128)(2,1)} %get-tuple-element.129), calls=%async_computation.3 | async-start | bytes 1179648 | tf_op jit(solution)/shard_map/all_to_all | solution.py:454
  71.4 6.1 %weight.9.refs_0_ = bf16[7,4,2048,256]{3,2,1,0:T(8,128)(2,1)} custom-call(s32[8]{0:T(128)S(1)} %fusion.2.place, bf16[7,4,2048,256]{3,2,1,0:T(8,128)(2,1)} %weight.8.refs_0_), custom_call_target="tpu_custom_call", output_to_operand_aliasing={{}: (1, {})} | custom-call | flops 41943040 | bytes 4194304 | tf_op jit(solution)/shard_map/weight/pallas_call | solution.py:182
  77.5 5.4 %all-to-all-done.3.gathered = bf16[16,144,128]{2,1,0:T(8,128)(2,1)S(1)} async-done(((bf16[16,144,128]{2,1,0:T(8,128)(2,1)}), bf16[16,144,128]{2,1,0:T(8,128)(2,1)S(1)}, u32[]{:S(2)}, u32[]{:S(2)}) %all-to-all-start.3) | async-done | bytes 589856 | tf_op jit(solution)/shard_map/all_to_all | solution.py:454
  96.1 3.6 %all-to-all-start.4 = ((bf16[16,144,128]{2,1,0:T(8,128)(2,1)}), bf16[16,144,128]{2,1,0:T(8,128)(2,1)S(1)}, u32[]{:S(2)}, u32[]{:S(2)}) async-start(bf16[16,144,128]{2,1,0:T(8,128)(2,1)} %get-tuple-element.140), calls=%async_computation.4 | async-start | bytes 1179648 | tf_op jit(solution)/shard_map/all_to_all | solution.py:454
  99.7 6.1 %weight.10.refs_0_ = bf16[7,4,2048,256]{3,2,1,0:T(8,128)(2,1)} custom-call(s32[8]{0:T(128)S(1)} %fusion.2.place, bf16[7,4,2048,256]{3,2,1,0:T(8,128)(2,1)} %weight.9.refs_0_), custom_call_target="tpu_custom_call", output_to_operand_aliasing={{}: (1, {})} | custom-call | flops 41943040 | bytes 4194304 | tf_op jit(solution)/shard_map/weight/pallas_call | solution.py:182
  105.9 5.4 %all-to-all-done.4.gathered = bf16[16,144,128]{2,1,0:T(8,128)(2,1)S(1)} async-done(((bf16[16,144,128]{2,1,0:T(8,128)(2,1)}), bf16[16,144,128]{2,1,0:T(8,128)(2,1)S(1)}, u32[]{:S(2)}, u32[]{:S(2)}) %all-to-all-start.4) | async-done | bytes 589856 | tf_op jit(solution)/shard_map/all_to_all | solution.py:454
  111.2 3.0 %contract.9 = (f32[4,144,128]{2,1,0:T(8,128)S(1)}, bf16[4,144,128]{2,1,0:T(8,128)(2,1)S(1)}) custom-call(s32[1]{0:T(128)} %bitcast.1.place, bf16[16,144,128]{2,1,0:T(8,128)(2,1)S(1)} %all-to-all-done.4.gathered, bf16[7,4,2048,256]{3,2,1,0:T(8,128)(2,1)} %weight.10.refs_0_), custom_call_target="tpu_custom_call" | custom-call | flops 536870912 | bytes 4194304 | tf_op jit(solution)/shard_map/contract/pallas_call | solution.py:469
  125.3 3.6 %all-to-all-start.5 = ((bf16[16,144,128]{2,1,0:T(8,128)(2,1)}), bf16[16,144,128]{2,1,0:T(8,128)(2,1)S(1)}, u32[]{:S(2)}, u32[]{:S(2)}) async-start(bf16[16,144,128]{2,1,0:T(8,128)(2,1)} %get-tuple-element.151), calls=%async_computation.5 | async-start | bytes 1179648 | tf_op jit(solution)/shard_map/all_to_all | solution.py:454
  128.9 6.1 %weight.11.refs_0_ = bf16[7,4,2048,256]{3,2,1,0:T(8,128)(2,1)} custom-call(s32[8]{0:T(128)S(1)} %fusion.2.place, bf16[7,4,2048,256]{3,2,1,0:T(8,128)(2,1)} %weight.10.refs_0_), custom_call_target="tpu_custom_call", output_to_operand_aliasing={{}: (1, {})} | custom-call | flops 41943040 | bytes 4194304 | tf_op jit(solution)/shard_map/weight/pallas_call | solution.py:182
  135.1 5.0 %all-to-all-done.5.gathered = bf16[16,144,128]{2,1,0:T(8,128)(2,1)S(1)} async-done(((bf16[16,144,128]{2,1,0:T(8,128)(2,1)}), bf16[16,144,128]{2,1,0:T(8,128)(2,1)S(1)}, u32[]{:S(2)}, u32[]{:S(2)}) %all-to-all-start.5) | async-done | bytes 589856 | tf_op jit(solution)/shard_map/all_to_all | solution.py:454
  140.1 3.0 %contract.10 = (f32[4,144,128]{2,1,0:T(8,128)S(1)}, bf16[4,144,128]{2,1,0:T(8,128)(2,1)S(1)}) custom-call(s32[1]{0:T(128)} %bitcast.1.place, bf16[16,144,128]{2,1,0:T(8,128)(2,1)S(1)} %all-to-all-done.5.gathered, bf16[7,4,2048,256]{3,2,1,0:T(8,128)(2,1)} %weight.11.refs_0_), custom_call_target="tpu_custom_call" | custom-call | flops 536870912 | bytes 4194304 | tf_op jit(solution)/shard_map/contract/pallas_call | solution.py:469
  152.1 3.6 %all-to-all-start.6 = ((bf16[16,144,128]{2,1,0:T(8,128)(2,1)}), bf16[16,144,128]{2,1,0:T(8,128)(2,1)S(1)}, u32[]{:S(2)}, u32[]{:S(2)}) async-start(bf16[16,144,128]{2,1,0:T(8,128)(2,1)} %get-tuple-element.162), calls=%async_computation.6 | async-start | bytes 1179648 | tf_op jit(solution)/shard_map/all_to_all | solution.py:454
  155.7 6.1 %weight.12.refs_0_ = bf16[7,4,2048,256]{3,2,1,0:T(8,128)(2,1)} custom-call(s32[8]{0:T(128)S(1)} %fusion.2.place, bf16[7,4,2048,256]{3,2,1,0:T(8,128)(2,1)} %weight.11.refs_0_), custom_call_target="tpu_custom_call", output_to_operand_aliasing={{}: (1, {})} | custom-call | flops 41943040 | bytes 4194304 | tf_op jit(solution)/shard_map/weight/pallas_call | solution.py:182
  161.8 5.5 %all-to-all-done.6.gathered = bf16[16,144,128]{2,1,0:T(8,128)(2,1)S(1)} async-done(((bf16[16,144,128]{2,1,0:T(8,128)(2,1)}), bf16[16,144,128]{2,1,0:T(8,128)(2,1)S(1)}, u32[]{:S(2)}, u32[]{:S(2)}) %all-to-all-start.6) | async-done | bytes 589856 | tf_op jit(solution)/shard_map/all_to_all | solution.py:454
  167.3 3.0 %contract.11 = (f32[4,144,128]{2,1,0:T(8,128)S(1)}, bf16[4,144,128]{2,1,0:T(8,128)(2,1)S(1)}) custom-call(s32[1]{0:T(128)} %bitcast.1.place, bf16[16,144,128]{2,1,0:T(8,128)(2,1)S(1)} %all-to-all-done.6.gathered, bf16[7,4,2048,256]{3,2,1,0:T(8,128)(2,1)} %weight.12.refs_0_), custom_call_target="tpu_custom_call" | custom-call | flops 536870912 | bytes 4194304 | tf_op jit(solution)/shard_map/contract/pallas_call | solution.py:469
  180.4 3.6 %all-to-all-start.7 = ((bf16[16,144,128]{2,1,0:T(8,128)(2,1)}), bf16[16,144,128]{2,1,0:T(8,128)(2,1)S(1)}, u32[]{:S(2)}, u32[]{:S(2)}) async-start(bf16[16,144,128]{2,1,0:T(8,128)(2,1)} %get-tuple-element.173), calls=%async_computation.7 | async-start | bytes 1179648 | tf_op jit(solution)/shard_map/all_to_all | solution.py:454
  184.0 6.1 %weight.13 = bf16[7,4,2048,256]{3,2,1,0:T(8,128)(2,1)} custom-call(s32[8]{0:T(128)S(1)} %fusion.2.place, bf16[7,4,2048,256]{3,2,1,0:T(8,128)(2,1)} %weight.12.refs_0_), custom_call_target="tpu_custom_call", output_to_operand_aliasing={{}: (1, {})} | custom-call | flops 41943040 | bytes 4194304 | tf_op jit(solution)/shard_map/weight/pallas_call | solution.py:182
  190.2 5.5 %all-to-all-done.7.gathered = bf16[16,144,128]{2,1,0:T(8,128)(2,1)S(1)} async-done(((bf16[16,144,128]{2,1,0:T(8,128)(2,1)}), bf16[16,144,128]{2,1,0:T(8,128)(2,1)S(1)}, u32[]{:S(2)}, u32[]{:S(2)}) %all-to-all-start.7) | async-done | bytes 589856 | tf_op jit(solution)/shard_map/all_to_all | solution.py:454
  208.0 3.6 %all-to-all-start.8 = ((bf16[16,144,128]{2,1,0:T(8,128)(2,1)}), bf16[16,144,128]{2,1,0:T(8,128)(2,1)S(1)}, u32[]{:S(2)}, u32[]{:S(2)}) async-start(bf16[16,144,128]{2,1,0:T(8,128)(2,1)} %get-tuple-element.192), calls=%async_computation.8 | async-start | bytes 1179648 | tf_op jit(solution)/shard_map/all_to_all | solution.py:454
  226.3 3.0 %contract.13 = (f32[4,144,128]{2,1,0:T(8,128)S(1)}, bf16[4,144,128]{2,1,0:T(8,128)(2,1)S(1)}) custom-call(s32[1]{0:T(128)} %bitcast.1.place, bf16[16,144,128]{2,1,0:T(8,128)(2,1)S(1)} %all-to-all-done.8.gathered, bf16[7,4,2048,256]{3,2,1,0:T(8,128)(2,1)} %weight.13), custom_call_target="tpu_custom_call" | custom-call | flops 536870912 | bytes 4194304 | tf_op jit(solution)/shard_map/contract/pallas_call | solution.py:469
  231.9 3.4 %collective-permute-start.36 = (f32[128,128]{1,0:T(8,128)S(1)}, f32[128,128]{1,0:T(8,128)S(1)}, u32[]{:S(2)}, u32[]{:S(2)}) collective-permute-start(f32[128,128]{1,0:T(8,128)S(1)} %get-tuple-element.210), channel_id=1, source_target_pairs={{0,2},{1,3},{2,0},{3,1},{4,6},{5,7},{6,4},{7,5},{8,10},{9,11},{10,... | collective-permute-start | bytes 196616 | tf_op jit(solution)/shard_map/ppermute | solution.py:348
  242.9 3.1 %collective-permute-start.39 = (f32[128,128]{1,0:T(8,128)S(1)}, f32[128,128]{1,0:T(8,128)S(1)}, u32[]{:S(2)}, u32[]{:S(2)}) collective-permute-start(f32[128,128]{1,0:T(8,128)S(1)} %add_add_fusion.3), channel_id=1, source_target_pairs={{0,8},{1,9},{2,10},{3,11},{4,12},{5,13},{6,14},{7,15},{8,0},{9,1},... | collective-permute-start | bytes 196616 | tf_op jit(solution)/shard_map/ppermute | solution.py:348
  257.0 3.2 %collective-permute-done.42 = f32[136,128]{1,0:T(8,128)S(1)} collective-permute-done((f32[136,128]{1,0:T(8,128)S(1)}, f32[136,128]{1,0:T(8,128)S(1)}, u32[]{:S(2)}, u32[]{:S(2)}) %collective-permute-start.42) | collective-permute-done | bytes 69664 | tf_op jit(solution)/shard_map/ppermute | solution.py:348
  (139 shorter events, 118.7 us)
Async XLA Ops:
  2.7 10.0 %all-to-all-start = ((f32[8,16,128]{2,1,0:T(8,128)}), f32[8,16,128]{2,1,0:T(8,128)S(1)}, u32[]{:S(2)}, u32[]{:S(2)}) async-start(f32[8,16,128]{2,1,0:T(8,128)} %pack.1), calls=%async_computation | async-start | bytes 131072 | tf_op jit(solution)/shard_map/all_to_all | solution.py:427
  19.7 20.2 %all-to-all-start.1 = ((bf16[16,144,128]{2,1,0:T(8,128)(2,1)}), bf16[16,144,128]{2,1,0:T(8,128)(2,1)S(1)}, u32[]{:S(2)}, u32[]{:S(2)}) async-start(bf16[16,144,128]{2,1,0:T(8,128)(2,1)} %first_contract.1), calls=%async_computation.1 | async-start | bytes 1179648 | tf_op jit(solution)/shard_map/all_to_all | solution.py:441
  41.0 14.6 %all-to-all-start.2 = ((bf16[16,144,128]{2,1,0:T(8,128)(2,1)}), bf16[16,144,128]{2,1,0:T(8,128)(2,1)S(1)}, u32[]{:S(2)}, u32[]{:S(2)}) async-start(bf16[16,144,128]{2,1,0:T(8,128)(2,1)} %get-tuple-element.117), calls=%async_computation.2 | async-start | bytes 1179648 | tf_op jit(solution)/shard_map/all_to_all | solution.py:454
  60.7 5.5 %collective-permute-start.2 = (bf16[144,128]{1,0:T(8,128)(2,1)S(1)}, bf16[144,128]{1,0:T(8,128)(2,1)S(1)}, u32[]{:S(2)}, u32[]{:S(2)}) collective-permute-start(bf16[144,128]{1,0:T(8,128)(2,1)S(1)} %get-tuple-element.126), channel_id=1, source_target_pairs={{0,64},{16,80},{32,96},{48,112},{64,0},{80,16},{96,32},{112,48},{1... | collective-permute-start | bytes 110600 | tf_op jit(solution)/shard_map/ppermute | solution.py:488
  67.8 15.1 %all-to-all-start.3 = ((bf16[16,144,128]{2,1,0:T(8,128)(2,1)}), bf16[16,144,128]{2,1,0:T(8,128)(2,1)S(1)}, u32[]{:S(2)}, u32[]{:S(2)}) async-start(bf16[16,144,128]{2,1,0:T(8,128)(2,1)} %get-tuple-element.129), calls=%async_computation.3 | async-start | bytes 1179648 | tf_op jit(solution)/shard_map/all_to_all | solution.py:454
  96.1 15.1 %all-to-all-start.4 = ((bf16[16,144,128]{2,1,0:T(8,128)(2,1)}), bf16[16,144,128]{2,1,0:T(8,128)(2,1)S(1)}, u32[]{:S(2)}, u32[]{:S(2)}) async-start(bf16[16,144,128]{2,1,0:T(8,128)(2,1)} %get-tuple-element.140), calls=%async_computation.4 | async-start | bytes 1179648 | tf_op jit(solution)/shard_map/all_to_all | solution.py:454
  115.7 5.7 %collective-permute-start.10 = (bf16[144,128]{1,0:T(8,128)(2,1)S(1)}, bf16[144,128]{1,0:T(8,128)(2,1)S(1)}, u32[]{:S(2)}, u32[]{:S(2)}) collective-permute-start(bf16[144,128]{1,0:T(8,128)(2,1)S(1)} %get-tuple-element.148), channel_id=1, source_target_pairs={{0,64},{16,80},{32,96},{48,112},{64,0},{80,16},{96,32},{112,48},{1... | collective-permute-start | bytes 110600 | tf_op jit(solution)/shard_map/ppermute | solution.py:488
  125.3 14.7 %all-to-all-start.5 = ((bf16[16,144,128]{2,1,0:T(8,128)(2,1)}), bf16[16,144,128]{2,1,0:T(8,128)(2,1)S(1)}, u32[]{:S(2)}, u32[]{:S(2)}) async-start(bf16[16,144,128]{2,1,0:T(8,128)(2,1)} %get-tuple-element.151), calls=%async_computation.5 | async-start | bytes 1179648 | tf_op jit(solution)/shard_map/all_to_all | solution.py:454
  144.6 5.5 %collective-permute-start.14 = (bf16[144,128]{1,0:T(8,128)(2,1)S(1)}, bf16[144,128]{1,0:T(8,128)(2,1)S(1)}, u32[]{:S(2)}, u32[]{:S(2)}) collective-permute-start(bf16[144,128]{1,0:T(8,128)(2,1)S(1)} %get-tuple-element.159), channel_id=1, source_target_pairs={{0,64},{16,80},{32,96},{48,112},{64,0},{80,16},{96,32},{112,48},{1... | collective-permute-start | bytes 110600 | tf_op jit(solution)/shard_map/ppermute | solution.py:488
  152.1 15.3 %all-to-all-start.6 = ((bf16[16,144,128]{2,1,0:T(8,128)(2,1)}), bf16[16,144,128]{2,1,0:T(8,128)(2,1)S(1)}, u32[]{:S(2)}, u32[]{:S(2)}) async-start(bf16[16,144,128]{2,1,0:T(8,128)(2,1)} %get-tuple-element.162), calls=%async_computation.6 | async-start | bytes 1179648 | tf_op jit(solution)/shard_map/all_to_all | solution.py:454
  180.4 15.3 %all-to-all-start.7 = ((bf16[16,144,128]{2,1,0:T(8,128)(2,1)}), bf16[16,144,128]{2,1,0:T(8,128)(2,1)S(1)}, u32[]{:S(2)}, u32[]{:S(2)}) async-start(bf16[16,144,128]{2,1,0:T(8,128)(2,1)} %get-tuple-element.173), calls=%async_computation.7 | async-start | bytes 1179648 | tf_op jit(solution)/shard_map/all_to_all | solution.py:454
  200.2 5.5 %collective-permute-start.21 = (bf16[144,128]{1,0:T(8,128)(2,1)S(1)}, bf16[144,128]{1,0:T(8,128)(2,1)S(1)}, u32[]{:S(2)}, u32[]{:S(2)}) collective-permute-start(bf16[144,128]{1,0:T(8,128)(2,1)S(1)} %get-tuple-element.180), channel_id=1, source_target_pairs={{0,32},{16,48},{32,64},{48,80},{64,96},{80,112},{96,0},{112,16},{1... | collective-permute-start | bytes 110600 | tf_op jit(solution)/shard_map/ppermute | solution.py:488
  208.0 18.2 %all-to-all-start.8 = ((bf16[16,144,128]{2,1,0:T(8,128)(2,1)}), bf16[16,144,128]{2,1,0:T(8,128)(2,1)S(1)}, u32[]{:S(2)}, u32[]{:S(2)}) async-start(bf16[16,144,128]{2,1,0:T(8,128)(2,1)} %get-tuple-element.192), calls=%async_computation.8 | async-start | bytes 1179648 | tf_op jit(solution)/shard_map/all_to_all | solution.py:454
  213.1 7.4 %collective-permute-start.25 = (bf16[2,128,128]{2,1,0:T(8,128)(2,1)S(1)}, bf16[2,128,128]{2,1,0:T(8,128)(2,1)S(1)}, u32[]{:S(2)}, u32[]{:S(2)}) collective-permute-start(bf16[2,128,128]{2,1,0:T(8,128)(2,1)S(1)} %get-tuple-element.194), channel_id=1, source_target_pairs={{0,32},{16,48},{32,0},{48,16},{64,96},{80,112},{96,64},{112,80},{1... | collective-permute-start | bytes 196616 | tf_op jit(solution)/shard_map/ppermute | solution.py:467
  214.5 6.7 %collective-permute-start.26 = (bf16[2,128,128]{2,1,0:T(8,128)(2,1)S(1)}, bf16[2,128,128]{2,1,0:T(8,128)(2,1)S(1)}, u32[]{:S(2)}, u32[]{:S(2)}) collective-permute-start(bf16[2,128,128]{2,1,0:T(8,128)(2,1)S(1)} %get-tuple-element.195), channel_id=1, source_target_pairs={{0,48},{16,32},{32,16},{48,0},{64,112},{80,96},{96,80},{112,64},{1... | collective-permute-start | bytes 196616 | tf_op jit(solution)/shard_map/ppermute | solution.py:467
  214.9 7.7 %collective-permute-start.27 = (bf16[2,128,128]{2,1,0:T(8,128)(2,1)S(1)}, bf16[2,128,128]{2,1,0:T(8,128)(2,1)S(1)}, u32[]{:S(2)}, u32[]{:S(2)}) collective-permute-start(bf16[2,128,128]{2,1,0:T(8,128)(2,1)S(1)} %get-tuple-element.196), channel_id=1, source_target_pairs={{0,64},{16,80},{32,96},{48,112},{64,0},{80,16},{96,32},{112,48},{1... | collective-permute-start | bytes 196616 | tf_op jit(solution)/shard_map/ppermute | solution.py:467
  217.1 6.1 %collective-permute-start.28 = (bf16[2,128,128]{2,1,0:T(8,128)(2,1)S(1)}, bf16[2,128,128]{2,1,0:T(8,128)(2,1)S(1)}, u32[]{:S(2)}, u32[]{:S(2)}) collective-permute-start(bf16[2,128,128]{2,1,0:T(8,128)(2,1)S(1)} %get-tuple-element.197), channel_id=1, source_target_pairs={{0,80},{16,64},{32,112},{48,96},{64,16},{80,0},{96,48},{112,32},{1... | collective-permute-start | bytes 196616 | tf_op jit(solution)/shard_map/ppermute | solution.py:467
  218.2 6.9 %collective-permute-start.29 = (bf16[2,128,128]{2,1,0:T(8,128)(2,1)S(1)}, bf16[2,128,128]{2,1,0:T(8,128)(2,1)S(1)}, u32[]{:S(2)}, u32[]{:S(2)}) collective-permute-start(bf16[2,128,128]{2,1,0:T(8,128)(2,1)S(1)} %get-tuple-element.198), channel_id=1, source_target_pairs={{0,96},{16,112},{32,64},{48,80},{64,32},{80,48},{96,0},{112,16},{1... | collective-permute-start | bytes 196616 | tf_op jit(solution)/shard_map/ppermute | solution.py:467
  220.5 5.7 %collective-permute-start.30 = (bf16[2,128,128]{2,1,0:T(8,128)(2,1)S(1)}, bf16[2,128,128]{2,1,0:T(8,128)(2,1)S(1)}, u32[]{:S(2)}, u32[]{:S(2)}) collective-permute-start(bf16[2,128,128]{2,1,0:T(8,128)(2,1)S(1)} %get-tuple-element.199), channel_id=1, source_target_pairs={{0,112},{16,96},{32,80},{48,64},{64,48},{80,32},{96,16},{112,0},{1... | collective-permute-start | bytes 196616 | tf_op jit(solution)/shard_map/ppermute | solution.py:467
  231.9 10.2 %collective-permute-start.36 = (f32[128,128]{1,0:T(8,128)S(1)}, f32[128,128]{1,0:T(8,128)S(1)}, u32[]{:S(2)}, u32[]{:S(2)}) collective-permute-start(f32[128,128]{1,0:T(8,128)S(1)} %get-tuple-element.210), channel_id=1, source_target_pairs={{0,2},{1,3},{2,0},{3,1},{4,6},{5,7},{6,4},{7,5},{8,10},{9,11},{10,... | collective-permute-start | bytes 196616 | tf_op jit(solution)/shard_map/ppermute | solution.py:348
  235.3 7.5 %collective-permute-start.37 = (f32[128,128]{1,0:T(8,128)S(1)}, f32[128,128]{1,0:T(8,128)S(1)}, u32[]{:S(2)}, u32[]{:S(2)}) collective-permute-start(f32[128,128]{1,0:T(8,128)S(1)} %get-tuple-element.210), channel_id=1, source_target_pairs={{0,1},{1,2},{2,3},{3,0},{4,5},{5,6},{6,7},{7,4},{8,9},{9,10},{10,1... | collective-permute-start | bytes 196616 | tf_op jit(solution)/shard_map/ppermute | solution.py:348
  235.9 7.0 %collective-permute-start.38 = (f32[128,128]{1,0:T(8,128)S(1)}, f32[128,128]{1,0:T(8,128)S(1)}, u32[]{:S(2)}, u32[]{:S(2)}) collective-permute-start(f32[128,128]{1,0:T(8,128)S(1)} %get-tuple-element.210), channel_id=1, source_target_pairs={{0,3},{1,0},{2,1},{3,2},{4,7},{5,4},{6,5},{7,6},{8,11},{9,8},{10,9... | collective-permute-start | bytes 196616 | tf_op jit(solution)/shard_map/ppermute | solution.py:348
  238.6 8.7 %collective-permute-start.32 = (bf16[4,144,128]{2,1,0:T(8,128)(2,1)S(1)}, bf16[4,144,128]{2,1,0:T(8,128)(2,1)S(1)}, u32[]{:S(2)}, u32[]{:S(2)}) collective-permute-start(bf16[4,144,128]{2,1,0:T(8,128)(2,1)S(1)} %get-tuple-element.203), channel_id=1, source_target_pairs={{0,96},{16,112},{1,97},{17,113},{2,98},{18,114},{3,99},{19,115},{4... | collective-permute-start | bytes 442376 | tf_op jit(solution)/shard_map/ppermute | solution.py:498
  241.5 8.5 %collective-permute-start.33 = (bf16[4,144,128]{2,1,0:T(8,128)(2,1)S(1)}, bf16[4,144,128]{2,1,0:T(8,128)(2,1)S(1)}, u32[]{:S(2)}, u32[]{:S(2)}) collective-permute-start(bf16[4,144,128]{2,1,0:T(8,128)(2,1)S(1)} %get-tuple-element.203), channel_id=1, source_target_pairs={{32,96},{48,112},{33,97},{49,113},{34,98},{50,114},{35,99},{51,115... | collective-permute-start | bytes 442376 | tf_op jit(solution)/shard_map/ppermute | solution.py:498
  242.2 7.9 %collective-permute-start.34 = (bf16[4,144,128]{2,1,0:T(8,128)(2,1)S(1)}, bf16[4,144,128]{2,1,0:T(8,128)(2,1)S(1)}, u32[]{:S(2)}, u32[]{:S(2)}) collective-permute-start(bf16[4,144,128]{2,1,0:T(8,128)(2,1)S(1)} %get-tuple-element.203), channel_id=1, source_target_pairs={{64,96},{80,112},{65,97},{81,113},{66,98},{82,114},{67,99},{83,115... | collective-permute-start | bytes 442376 | tf_op jit(solution)/shard_map/ppermute | solution.py:498
  242.9 7.9 %collective-permute-start.39 = (f32[128,128]{1,0:T(8,128)S(1)}, f32[128,128]{1,0:T(8,128)S(1)}, u32[]{:S(2)}, u32[]{:S(2)}) collective-permute-start(f32[128,128]{1,0:T(8,128)S(1)} %add_add_fusion.3), channel_id=1, source_target_pairs={{0,8},{1,9},{2,10},{3,11},{4,12},{5,13},{6,14},{7,15},{8,0},{9,1},... | collective-permute-start | bytes 196616 | tf_op jit(solution)/shard_map/ppermute | solution.py:348
  246.0 5.5 %collective-permute-start.40 = (f32[128,128]{1,0:T(8,128)S(1)}, f32[128,128]{1,0:T(8,128)S(1)}, u32[]{:S(2)}, u32[]{:S(2)}) collective-permute-start(f32[128,128]{1,0:T(8,128)S(1)} %add_add_fusion.3), channel_id=1, source_target_pairs={{0,4},{1,5},{2,6},{3,7},{4,8},{5,9},{6,10},{7,11},{8,12},{9,13},{1... | collective-permute-start | bytes 196616 | tf_op jit(solution)/shard_map/ppermute | solution.py:348
  253.6 6.6 %collective-permute-start.42 = (f32[136,128]{1,0:T(8,128)S(1)}, f32[136,128]{1,0:T(8,128)S(1)}, u32[]{:S(2)}, u32[]{:S(2)}) collective-permute-start(f32[136,128]{1,0:T(8,128)S(1)} %get-tuple-element.215), channel_id=1, source_target_pairs={{0,2},{1,3},{2,0},{3,1},{4,6},{5,7},{6,4},{7,5},{8,10},{9,11},{10,... | collective-permute-start | bytes 208904 | tf_op jit(solution)/shard_map/ppermute | solution.py:348
  253.7 7.0 %collective-permute-start.43 = (f32[136,128]{1,0:T(8,128)S(1)}, f32[136,128]{1,0:T(8,128)S(1)}, u32[]{:S(2)}, u32[]{:S(2)}) collective-permute-start(f32[136,128]{1,0:T(8,128)S(1)} %get-tuple-element.215), channel_id=1, source_target_pairs={{0,1},{1,2},{2,3},{3,0},{4,5},{5,6},{6,7},{7,4},{8,9},{9,10},{10,1... | collective-permute-start | bytes 208904 | tf_op jit(solution)/shard_map/ppermute | solution.py:348
  255.1 5.6 %collective-permute-start.44 = (f32[136,128]{1,0:T(8,128)S(1)}, f32[136,128]{1,0:T(8,128)S(1)}, u32[]{:S(2)}, u32[]{:S(2)}) collective-permute-start(f32[136,128]{1,0:T(8,128)S(1)} %get-tuple-element.215), channel_id=1, source_target_pairs={{0,3},{1,0},{2,1},{3,2},{4,7},{5,4},{6,5},{7,6},{8,11},{9,8},{10,9... | collective-permute-start | bytes 208904 | tf_op jit(solution)/shard_map/ppermute | solution.py:348
  260.7 6.8 %collective-permute-start.45 = (f32[136,128]{1,0:T(8,128)S(1)}, f32[136,128]{1,0:T(8,128)S(1)}, u32[]{:S(2)}, u32[]{:S(2)}) collective-permute-start(f32[136,128]{1,0:T(8,128)S(1)} %add_add_fusion.1), channel_id=1, source_target_pairs={{0,8},{1,9},{2,10},{3,11},{4,12},{5,13},{6,14},{7,15},{8,0},{9,1},... | collective-permute-start | bytes 208904 | tf_op jit(solution)/shard_map/ppermute | solution.py:348
  262.6 5.5 %collective-permute-start.46 = (f32[136,128]{1,0:T(8,128)S(1)}, f32[136,128]{1,0:T(8,128)S(1)}, u32[]{:S(2)}, u32[]{:S(2)}) collective-permute-start(f32[136,128]{1,0:T(8,128)S(1)} %add_add_fusion.1), channel_id=1, source_target_pairs={{0,4},{1,5},{2,6},{3,7},{4,8},{5,9},{6,10},{7,11},{8,12},{9,13},{1... | collective-permute-start | bytes 208904 | tf_op jit(solution)/shard_map/ppermute | solution.py:348
  (29 other events, 386.2 us)

commit v3 on v1

v3 whole, which is shorter than its diff:
```python
import functools
import math

import jax
import jax.numpy as jnp
import numpy as np
from jax import lax
from jax.experimental import pallas as pl
from jax.experimental.pallas import tpu as pltpu
from jax.sharding import PartitionSpec as P

D = 16384
R = 128
TOK = 128
LAYERS = 8
SEG = 8
MP = 16
WIDTH = D // MP
PIECE = WIDTH // SEG
STATE = 4 * TOK
GATHER = STATE + 16
SUM = STATE + TOK + 16
STEP_Q, STEP_P, STEP_R, STEP_C = 4096, 1024, 256, 128
EPSILON = 1e-05
EMBED_KEY = 7919
BF = jnp.bfloat16
F32 = jnp.float32


def wrapped(value):
    value &= 0xFFFFFFFF
    return np.int32(value - (1 << 32) if value >> 31 else value)


MULT = wrapped(73244475)
MULT_SQ = wrapped(73244475 * 73244475)


def fold(bits):
    return jnp.bitwise_xor(bits, lax.shift_right_logical(bits, jnp.int32(16)))


def uniform_bits(mixed_bits):
    mixed_bits = fold(mixed_bits) * MULT
    mixed_bits = fold(mixed_bits) * MULT_SQ
    mixed_bits = fold(mixed_bits) * MULT
    return lax.shift_right_logical(fold(mixed_bits), jnp.int32(8))


def hashed(mixed_bits, magnitude):
    return uniform_bits(mixed_bits).astype(F32) * np.float32(magnitude * 2.0 / 16777216.0) - np.float32(magnitude)


def ternary(mixed_bits, magnitude):
    bits = uniform_bits(mixed_bits)
    return (lax.rem(bits, jnp.int32(3)) - jnp.int32(1)).astype(F32) * np.float32(magnitude)


def split_row(row):
    high = row.astype(BF).astype(F32)
    index = lax.broadcasted_iota(jnp.int32, (16, row.shape[1]), 0)
    tile = jnp.where(index == 0, high, jnp.where(index == 1, row - high, 0.0))
    return tile.astype(BF)


def joined_row(tile):
    return jnp.sum(tile.astype(F32), axis=0, keepdims=True)


SMEM = pl.BlockSpec(memory_space=pltpu.SMEM)
VMEM = pl.BlockSpec(memory_space=pltpu.VMEM)
HBM = pl.BlockSpec(memory_space=pltpu.HBM)


def call(body, name, out_shape, in_specs, flops=0, nbytes=0, limit=8 << 20, out_specs=None, scratch=(), aliases={}):
    single = not isinstance(out_shape, (tuple, list))
    return pl.pallas_call(
        body,
        out_shape=out_shape,
        in_specs=in_specs,
        out_specs=out_specs or (VMEM if single else tuple(VMEM for _ in out_shape)),
        scratch_shapes=scratch,
        input_output_aliases=aliases,
        name=name,
        cost_estimate=pl.CostEstimate(flops=flops, bytes_accessed=nbytes, transcendentals=0),
        compiler_params=pltpu.CompilerParams(vmem_limit_bytes=limit),
    )


def sds(shape, dtype):
    return jax.ShapeDtypeStruct(shape, dtype)


def gate(value, *others):
    return lax.optimization_barrier((value, *others))[0]


def pack_kernel(seed, gain, out):
    row = jnp.full((1, PIECE), seed[0], jnp.int32).astype(F32)
    for index in range(SEG):
        part = gain[:, index * PIECE : (index + 1) * PIECE].astype(F32)
        for target in range(SEG):
            out[target, index : index + 1, :] = part
    for target in range(SEG):
        out[target, SEG:, :] = jnp.broadcast_to(row, (SEG, PIECE))


def facts_kernel(place, student_seed, facts, along_z_out, along_y_out, even_out, place_out, student_out):
    core, column, row, plane = place[1], place[2], place[3], place[4]
    for digit in range(4):
        along_z_out[digit] = facts[0, pl.ds(2 * digit + core, 1), :]
        along_y_out[digit] = facts[2 * digit + 1, pl.ds(2 * column + core, 1), :]
        for pair in range(4):
            even_out[pair, digit] = facts[2 * pair, pl.ds(2 * digit + core, 1), :]
    even = (row * STEP_P + core * STEP_C) * 16411 + plane * STEP_Q + column * STEP_R
    odd = (column * STEP_R + core * STEP_C) * 16411 + plane * STEP_Q + row * STEP_P
    for layer in range(LAYERS):
        seed = facts[layer, SEG : SEG + 1, :].astype(jnp.int32)
        place_out[layer : layer + 1, :] = seed * 1000003 + (even if layer % 2 == 0 else odd)
    block = plane * 4 + row
    student_out[...] = jnp.full((SEG, PIECE), student_seed[0] * 1000003 + block * (WIDTH * 16411), jnp.int32)


def odd_gain_kernel(row, *refs):
    parts, out = refs[:4], refs[4]
    for partner, part in zip(PARTNERS, parts):
        for pair in range(4):
            out[pair, jnp.bitwise_xor(row[0], partner)] = part[pair]


def squares_tile(squares):
    return split_row(jnp.sum(jnp.transpose(squares), axis=0, keepdims=True))


def embed_kernel(place, token, out, tile_out):
    tokens = jnp.broadcast_to(token[...], (TOK, PIECE)) * 16411 + wrapped(EMBED_KEY * 1000003)
    tokens = tokens + lax.broadcasted_iota(jnp.int32, (TOK, PIECE), 1)
    tokens = tokens + (place[1] * STEP_C + place[3] * STEP_P)
    squares = jnp.zeros((TOK, PIECE), F32)
    for slot, partner in enumerate(PARTNERS):
        for digit in range(4):
            first = jnp.bitwise_xor(place[4], partner) * STEP_Q + digit * STEP_R
            part = hashed(tokens + first, math.sqrt(3.0)).astype(BF)
            out[slot, digit * TOK : (digit + 1) * TOK, :] = part
            wide = part.astype(F32)
            squares = squares + wide * wide
    tile_out[...] = squares_tile(squares)


def first_scale_kernel(embedded, tile, *refs):
    gains, outs = refs[:4], refs[4:]
    for partner in range(4):
        for digit in range(4):
            rows = slice(digit * TOK, (digit + 1) * TOK)
            outs[partner][rows, :] = (embedded[partner, rows, :].astype(F32) * gains[partner][digit]).astype(BF)
        outs[partner][STATE:, :] = tile[...] if partner == 0 else jnp.zeros((16, TOK), BF)


def weight_kernel(layer, plane, place, out):
    chunk = 64
    row_step, col_step = (STEP_R, STEP_P) if layer % 2 == 0 else (STEP_P, STEP_R)
    row = lax.broadcasted_iota(jnp.int32, (chunk, WIDTH), 0)
    col = lax.broadcasted_iota(jnp.int32, (chunk, WIDTH), 1)
    col = (col // 512) * STEP_C + (col // PIECE % 4) * col_step + col % PIECE
    base = row * 16411 + col + jnp.concatenate([place[layer : layer + 1, :]] * (WIDTH // PIECE), axis=1)

    def step(index, carry):
        piece = index // 2
        slot = piece // 4
        partner = jnp.where(slot == 0, 0, jnp.where(slot == 1, PARTNERS[1], slot - 1))
        first = jnp.bitwise_xor(plane[0], partner) * (STEP_Q * 16411) + (piece % 4) * (row_step * 16411) + (index % 2) * (chunk * 16411)
        start = pl.multiple_of(index * chunk, chunk)
        out[pl.ds(start, chunk), :] = hashed(base + first, math.sqrt(3.0 / D)).astype(BF)
        return carry

    lax.fori_loop(0, 2048 // chunk, step, 0, unroll=2)


WEIGHTS = 2048 * WIDTH


def teacher_weight(layer, plane, place):
    body = functools.partial(weight_kernel, layer)
    return call(body, "weight", sds((2048, WIDTH), BF), [SMEM, VMEM], flops=20 * WEIGHTS, nbytes=2 * WEIGHTS)(
        plane, place
    )


def contract_kernel(core, *refs):
    parts, (weight, own_out, other_out) = refs[:4], refs[4:]
    scaled = [part[digit * TOK : (digit + 1) * TOK, :] for part in parts for digit in range(4)]
    scaled = jnp.concatenate(scaled, axis=1)
    squares = joined_row(parts[0][STATE:, :])
    for part in parts[1:]:
        squares = squares + joined_row(part[STATE:, :])
    tile = split_row(squares)
    own_out[STATE:, :] = tile.astype(F32)
    other_out[STATE:, :] = tile
    first = core[0] == 0
    for pair in range(2):
        low = jnp.dot(scaled, weight[:, pair * 256 : (pair + 1) * 256], preferred_element_type=F32)
        high = jnp.dot(scaled, weight[:, 512 + pair * 256 : 512 + (pair + 1) * 256], preferred_element_type=F32)
        own, other = jnp.where(first, low, high), jnp.where(first, high, low).astype(BF)
        for half in range(2):
            rows = slice((2 * pair + half) * TOK, (2 * pair + half + 1) * TOK)
            columns = slice(half * PIECE, (half + 1) * PIECE)
            own_out[rows, :] = own[:, columns]
            other_out[rows, :] = other[:, columns]


def pair_kernel(digit, own, other, stream, out):
    total = own[...] + other[...].astype(F32)
    out[:STATE, :] = total[:STATE].astype(BF)
    start = pl.multiple_of(digit[0] * TOK, TOK)
    out[STATE : STATE + TOK, :] = stream[pl.ds(start, TOK), :]
    out[STATE + TOK :, :] = split_row(joined_row(total[STATE:]))


def update_kernel(pair, digit, part_a, part_b, part_c, part_d, gains, stream_out, mean_out, message_out):
    parts = (part_a, part_b, part_c, part_d)

    def total(rows):
        wide = [part[rows, :].astype(F32) for part in parts]
        return (wide[0] + wide[2]) + (wide[1] + wide[3])

    squares = joined_row(total(slice(STATE + TOK, SUM)))
    mean = jnp.transpose(jnp.broadcast_to(squares, (TOK, TOK))) * np.float32(1.0 / D)
    mean_out[...] = mean
    scale = lax.rsqrt(mean + EPSILON)
    for partner, part in zip(PARTNERS, parts):
        start = pl.multiple_of(jnp.bitwise_xor(digit[0], partner) * TOK, TOK)
        stream_out[pl.ds(start, TOK), :] = part[STATE : STATE + TOK, :]
    squares = jnp.zeros((TOK, PIECE), F32)
    for index in range(4):
        rows = slice(index * TOK, (index + 1) * TOK)
        result = (stream_out[rows, :].astype(F32) + total(rows) * scale).astype(BF)
        stream_out[rows, :] = result
        wide = result.astype(F32)
        squares = squares + wide * wide
        if pair is not None:
            message_out[rows, :] = (wide * gains[pair, index]).astype(BF)
    if pair is not None:
        message_out[STATE:, :] = squares_tile(squares)


def odd_kernel(column, row, *refs):
    streams, outs, held = refs[:4], refs[4:8], refs[8]
    start = pl.multiple_of(row[0] * TOK, TOK)
    for index in range(4):
        held[index] = streams[index][pl.ds(start, TOK), :]
    for partner in range(4):
        outs[partner][...] = held[jnp.bitwise_xor(column[0], partner)]


def first_swap_kernel(segment, core, column, *refs):
    odd_parts, even, means = refs[:4], refs[4:8], refs[8:15]
    odd_out, here_out, send_out, later_out, mean_out = refs[15:20]
    held = refs[20]
    first = core[0] == 0
    for partner, part in zip(PARTNERS, odd_parts):
        start = pl.multiple_of(jnp.bitwise_xor(column[0], partner) * TOK, TOK)
        odd_out[pl.ds(start, TOK), :] = part[...]
    for index in range(4):
        held[index] = even[index][...]
    held[4] = even[3][...]
    now = held[column[0]].astype(F32)
    odd = odd_out[...].astype(F32)
    here_out[...] = jnp.where(first, now, odd).astype(BF)
    send_out[...] = jnp.where(first, odd, now).astype(BF)
    later_out[...] = held[column[0] + 1]
    mean = means[0][...]
    for layer in range(1, LAYERS - 1):
        mean = jnp.where(segment[0] == layer, means[layer][...], mean)
    mean_out[...] = mean


def second_swap_kernel(core, column, odd, later, last, here_out, send_out):
    first = core[0] == 0
    even = jnp.where(column[0] == 3, last[...].astype(F32), later[...].astype(F32))
    odd = odd[...].astype(F32)
    here_out[...] = jnp.where(first, odd, even).astype(BF)
    send_out[...] = jnp.where(first, even, odd).astype(BF)


CORE = [(i, i ^ 1) for i in range(SEG)]
ALONG = {
    "x": ("segment", 2),
    "y": ("mp", 1),
    "z": ("mp", 4),
}


PARTNERS = (0, 3, 1, 2)


def exchange(values, physical):
    axis, step = ALONG[physical]
    size = SEG if axis == "segment" else MP
    values = values if isinstance(values, (list, tuple)) else [values] * 4
    return [values[0]] + [
        lax.ppermute(values[k], axis, [(i, i ^ (k * step)) for i in range(size)]) for k in PARTNERS[1:]
    ]


def sum_mp(value):
    for physical in ("y", "z"):
        own, third, first, second = exchange(value, physical)
        value = (own + first) + (second + third)
    return value


def ternary_base(place):
    row = lax.broadcasted_iota(jnp.int32, (PIECE, R), 0)
    rank = lax.broadcasted_iota(jnp.int32, (PIECE, R), 1)
    return row * 16411 + rank + place[0:1, :]


def piece_of(core, index, here, there):
    first = core[0] == 0
    rows = slice(index // 2 * TOK, (index // 2 + 1) * TOK)
    here, there = here[rows, :].astype(F32), there[rows, :].astype(F32)
    return jnp.where(first, here, there) if index % 2 == 0 else jnp.where(first, there, here)


def student_up_kernel(core, place, here, there, gain, pre_out):
    base = ternary_base(place)
    total = jnp.zeros((TOK, R), F32)
    for index in range(SEG):
        up_weight = ternary(base + index * PIECE * 16411, math.sqrt(1.5 / D)).astype(BF)
        gains = gain[:, index * PIECE : (index + 1) * PIECE].astype(F32)
        scaled = (piece_of(core, index, here, there) * gains).astype(BF)
        total = total + jnp.dot(scaled, up_weight, preferred_element_type=F32)
    pre_out[...] = total


def student_error_kernel(
    segment, core, place, here, there, target_here, target_there, pre, mean, last_mean, back_out, scaled_out, squared_out, pre_out
):
    base = ternary_base(place) + R
    scale = lax.rsqrt(jnp.where(segment[0] == SEG - 1, last_mean[...], mean[...]) + EPSILON)
    rectified = jnp.maximum(pre[...] * scale, 0.0)
    pre_out[...] = rectified
    squared = (rectified * rectified).astype(BF)
    squared_out[...] = squared
    back = jnp.zeros((TOK, R), F32)
    squares = jnp.zeros((TOK, PIECE), F32)
    for index in range(SEG):
        down_weight = ternary(base + index * PIECE * 16411, math.sqrt(1.5 / R)).astype(BF)
        student = lax.dot_general(squared, down_weight, (((1,), (1,)), ((), ())), preferred_element_type=F32)
        target = piece_of(core, index, target_here, target_there)
        error = piece_of(core, index, here, there) + student - target
        squares = squares + error * error
        scaled = (error * np.float32(1.0 / TOK)).astype(BF)
        scaled_out[:, index * PIECE : (index + 1) * PIECE] = scaled
        back = back + jnp.dot(scaled, down_weight, preferred_element_type=F32)
    back_out[:TOK, :] = back
    back_out[TOK:, :] = jnp.sum(squares.reshape(TOK // 8, 8, PIECE), axis=0)


OVER_TOKENS = (((0,), (0,)), ((), ()))


def student_down_kernel(segment, core, here, there, gain, mean, last_mean, scaled, squared, normed_out, down_out):
    scale = lax.rsqrt(jnp.where(segment[0] == SEG - 1, last_mean[...], mean[...]) + EPSILON)
    for index in range(SEG):
        columns = slice(index * PIECE, (index + 1) * PIECE)
        normed = piece_of(core, index, here, there) * scale * gain[:, columns].astype(F32)
        normed_out[:, columns] = normed.astype(BF)
    down_out[...] = lax.dot_general(scaled[...], squared[...], OVER_TOKENS, preferred_element_type=F32)


def student_grad_kernel(normed, rectified, back, up_out, loss_out):
    back_pre = (back[:TOK, :] * 2.0 * rectified[...]).astype(BF)
    up_out[...] = lax.dot_general(normed[...], back_pre, OVER_TOKENS, preferred_element_type=F32)
    total = jnp.sum(jnp.sum(back[TOK:, :], axis=0, keepdims=True), axis=1, keepdims=True)
    loss_out[...] = total * np.float32(1.0 / (TOK * D))


def local(token_ids, teacher_seeds, student_seeds, teacher_gain, student_gain):
    block = lax.axis_index("mp")
    segment = lax.axis_index("segment")
    core, column = lax.rem(segment, 2), segment // 2
    row, plane = lax.rem(block, 4), block // 4
    place = jnp.stack([segment, core, column, row, plane])
    segment, core, column, row, plane = (part.reshape(1) for part in (segment, core, column, row, plane))
    mean_shape = sds((TOK, TOK), F32)
    state_shape = sds((STATE, PIECE), BF)
    gain_shape = sds((4, 1, PIECE), F32)

    facts = call(pack_kernel, "pack", sds((SEG, 2 * SEG, PIECE), F32), [SMEM, VMEM])(teacher_seeds, teacher_gain)
    facts = lax.all_to_all(facts, "segment", split_axis=0, concat_axis=0, tiled=True)
    embedded, tile = call(
        embed_kernel, "embed", (sds((4, STATE, PIECE), BF), sds((16, TOK), BF)), [SMEM, VMEM]
    )(place, token_ids.reshape(TOK, 1))
    first_gain, odd_gain, even_gains, places, student_place = call(
        facts_kernel,
        "facts",
        (gain_shape, gain_shape, sds((4, 4, 1, PIECE), F32)) + (sds((LAYERS, PIECE), jnp.int32),) * 2,
        [SMEM, SMEM, VMEM],
    )(place, student_seeds, facts)
    first_gains = exchange(first_gain, "z")
    weight = teacher_weight(0, plane, places)
    parts = call(
        first_scale_kernel, "first_scale", tuple(sds((GATHER, PIECE), BF) for _ in range(4)), [VMEM] * 6
    )(embedded, tile, *first_gains)
    odd_gains = call(odd_gain_kernel, "odd_gain", sds((4, 4, 1, PIECE), F32), [SMEM] + [VMEM] * 4)(
        row, *exchange(gate(odd_gain, weight), "y")
    )

    streams, means = [embedded[0]], []
    for layer in range(LAYERS):
        if layer:
            weight = teacher_weight(layer, plane, gate(places, message))
            parts = exchange(message, "z")
        own, other = call(
            contract_kernel,
            "contract",
            (sds((GATHER, PIECE), F32), sds((GATHER, PIECE), BF)),
            [SMEM] + [VMEM] * 5,
            flops=2 * TOK * WEIGHTS,
            nbytes=2 * WEIGHTS,
        )(core, *parts, weight)
        other = lax.ppermute(other, "segment", CORE)
        even = layer % 2 == 0
        summed = call(
            pair_kernel, "pair", sds((SUM, PIECE), BF), [SMEM] + [VMEM] * 3
        )(column if even else row, own, other, streams[-1])
        parts = exchange(summed, "y" if even else "x")
        pair = None if layer + 1 == LAYERS else (layer + 1) // 2
        stream, mean, message = call(
            functools.partial(update_kernel, pair),
            "update",
            (state_shape, mean_shape, sds((GATHER, PIECE), BF)),
            [SMEM] + [VMEM] * 5,
        )(row if even else column, *parts, odd_gains if even else even_gains)
        streams.append(stream)
        means.append(mean)

    odd = call(
        odd_kernel,
        "odd",
        tuple(sds((TOK, PIECE), BF) for _ in range(4)),
        [SMEM] * 2 + [VMEM] * 4,
        scratch=(pltpu.VMEM((4, TOK, PIECE), BF),),
    )(column, row, *streams[1::2])
    odd = exchange(odd, "x")
    odd_half, here, send, later, mean = call(
        first_swap_kernel,
        "first_swap",
        (state_shape,) * 4 + (mean_shape,),
        [SMEM] * 3 + [VMEM] * 15,
        scratch=(pltpu.VMEM((5, STATE, PIECE), BF),),
    )(segment, core, column, *odd, *streams[0:8:2], *means[:7])
    there = lax.ppermute(send, "segment", CORE)
    student_columns = lax.dynamic_slice_in_dim(student_gain, block * WIDTH, WIDTH, 1)
    pre = call(student_up_kernel, "student_up", sds((TOK, R), F32), [SMEM] + [VMEM] * 4)(
        core, student_place, here, there, student_columns
    )
    pre = sum_mp(pre)

    target_here, send = call(second_swap_kernel, "second_swap", (state_shape,) * 2, [SMEM] * 2 + [VMEM] * 3)(
        core, column, odd_half, later, streams[LAYERS]
    )
    target_there = lax.ppermute(send, "segment", CORE)
    back, scaled, squared, rectified = call(
        student_error_kernel,
        "student_error",
        (sds((TOK + 8, R), F32), sds((TOK, WIDTH), BF), sds((TOK, R), BF), sds((TOK, R), F32)),
        [SMEM] * 2 + [VMEM] * 8,
    )(segment, core, student_place, here, there, target_here, target_there, pre, mean, means[LAYERS - 1])
    normed, grad_down = call(
        student_down_kernel, "student_down", (sds((TOK, WIDTH), BF), sds((WIDTH, R), F32)), [SMEM] * 2 + [VMEM] * 7
    )(segment, core, here, there, student_columns, mean, means[LAYERS - 1], scaled, squared)
    back = sum_mp(back)
    grad_up, loss = call(
        student_grad_kernel, "student_grad", (sds((WIDTH, R), F32), sds((1, 1), F32)), [VMEM] * 3
    )(normed, rectified, back)
    return loss.reshape(1), grad_up[None], grad_down[None]


def solution(mesh):
    in_specs = (P(), P("segment"), P("segment"), P("segment", "mp"), P("segment", None))
    out_specs = (P("segment"), P("segment", "mp", None), P("segment", "mp", None))
    return jax.shard_map(local, mesh=mesh, in_specs=in_specs, out_specs=out_specs, check_vma=False)
```

time: 316 us -> 248 us (0.78)
  local copies, waits for them, and re-layouts: 36.6 us -> 1.55 us
  waiting for transfers between devices: 94.5 us -> 81.9 us
  other arithmetic: 12.1 us -> 0.07 us
  Pallas kernels: 65.7 us -> 54.2 us
  starting transfers between devices: 102 us -> 108 us
    ppermute x36 -> x68, starting transfers between devices: 51.3 us -> 102 us  [the longest x66 102 us: exchange(): lax.ppermute(values[k], axis, [(i, i ^ k * step) for i in range(size)])]
    all_to_all x10 -> x1, waiting for transfers between devices: 49.3 us -> 2.77 us  [local(): lax.all_to_all(facts, 'segment', split_axis=0, concat_axis=0, tiled=True)]
    all_to_all x10 -> x1, starting transfers between devices: 49.6 us -> 4.38 us  [local(): lax.all_to_all(facts, 'segment', split_axis=0, concat_axis=0, tiled=True)]
    ppermute x36 -> x68, waiting for transfers between devices: 35.6 us -> 69.8 us  [the longest x66 69.8 us: exchange(): lax.ppermute(values[k], axis, [(i, i ^ k * step) for i in range(size)])]
    unnamed x41 -> x4, local copies, waits for them, and re-layouts: 33.6 us -> 0.69 us
    pallas_call x34 -> x43, Pallas kernels: 64.3 us -> 53.2 us  [the longest x8 38.8 us: teacher_weight(): call(body, 'weight', sds((2048, WIDTH), BF), [SMEM, VMEM], flops=20 * WEI...]
    another operation x10 -> x0, other arithmetic: 6.21 us -> none  [the longest x8 5.5 us: teacher_weight(): jnp.stack([seed, segment, block])]
    unnamed x7 -> x0, other arithmetic: 4.45 us -> none
  transfers between devices with their start and end apart: 54 -> 77, of which waited for: 50 -> 45; matrix products, arithmetic and copies ran while one was open for 4% -> 0% of each run, Pallas kernels for 15% -> 18%
where the time goes in v3:
time: 248 us
  starting transfers between devices  108 us (44%)
  waiting for transfers between devices  81.9 us (33%)
  Pallas kernels  54.2 us (22%)
  between operations  2.55 us (1%)
    ppermute x66, starting transfers between devices, exchange(): lax.ppermute(values[k], axis, [(i, i ^ k * step) for i in range(size)])  102 us
    ppermute x66, waiting for transfers between devices, exchange(): lax.ppermute(values[k], axis, [(i, i ^ k * step) for i in range(size)])  69.8 us
    pallas_call x8, Pallas kernels, teacher_weight(): call(body, 'weight', sds((2048, WIDTH), BF), [SMEM, VMEM], flops=20 * WEI...  38.8 us
    ppermute x8, waiting for transfers between devices, local(): other = lax.ppermute(other, 'segment', CORE)  9.37 us
    pallas_call x8, Pallas kernels, local(): call(contract_kernel, 'contract', (sds((GATHER, PIECE), F32), sds((GATHER...  5.87 us
  transfers between devices with their start and end apart: 77, of which 45 were waited for; matrix products, arithmetic and copies ran while one was open for 0% of the time, Pallas kernels for 18%

profile of v3, /device:TPU:0, one launch (start us, length us, event | category | flops | bytes accessed | tf_op | source)
XLA Modules:
  0.0 248.2 jit_solution(1828537969780193379)
XLA Ops:
  2.7 4.4 %all-to-all-start = ((f32[8,16,128]{2,1,0:T(8,128)}), f32[8,16,128]{2,1,0:T(8,128)S(1)}, u32[]{:S(2)}, u32[]{:S(2)}) async-start(f32[8,16,128]{2,1,0:T(8,128)} %pack.1), calls=%async_computation | async-start | bytes 131072 | tf_op jit(solution)/shard_map/all_to_all | solution.py:391
  13.2 4.1 %collective-permute-start = (f32[4,1,128]{2,1,0:T(1,128)S(1)}, f32[4,1,128]{2,1,0:T(1,128)S(1)}, u32[]{:S(2)}, u32[]{:S(2)}) collective-permute-start(f32[4,1,128]{2,1,0:T(1,128)S(1)} %get-tuple-element.82.refs_0_), channel_id=1, source_target_pairs={{0,12},{1,13},{2,14},{3,15},{4,8},{5,9},{6,10},{7,11},{8,4},{9,5},... | collective-permute-start | bytes 6152 | tf_op jit(solution)/shard_map/ppermute | solution.py:301
  18.9 4.9 %weight.8.refs_4_ = bf16[2048,1024]{1,0:T(8,128)(2,1)S(1)} custom-call(s32[1]{0:T(128)} %bitcast.4.plane, s32[8,128]{1,0:T(8,128)S(1)} %get-tuple-element.139.place), custom_call_target="tpu_custom_call" | custom-call | flops 41943040 | bytes 4194304 | tf_op jit(solution)/shard_map/weight/pallas_call | solution.py:184
  26.1 3.1 %collective-permute-start.4 = (bf16[656,128]{1,0:T(8,128)(2,1)S(1)}, bf16[656,128]{1,0:T(8,128)(2,1)S(1)}, u32[]{:S(2)}, u32[]{:S(2)}) collective-permute-start(bf16[656,128]{1,0:T(8,128)(2,1)S(1)} %pair.8.part_a), channel_id=1, source_target_pairs={{0,3},{1,2},{2,1},{3,0},{4,7},{5,6},{6,5},{7,4},{8,11},{9,10},{10,... | collective-permute-start | bytes 503816 | tf_op jit(solution)/shard_map/ppermute | solution.py:301
  30.9 3.0 %collective-permute-start.7 = (f32[4,1,128]{2,1,0:T(1,128)S(1)}, f32[4,1,128]{2,1,0:T(1,128)S(1)}, u32[]{:S(2)}, u32[]{:S(2)}) collective-permute-start(f32[4,1,128]{2,1,0:T(1,128)S(1)} %get-tuple-element.91.refs_0_), channel_id=1, source_target_pairs={{0,3},{1,2},{2,1},{3,0},{4,7},{5,6},{6,5},{7,4},{8,11},{9,10},{10,... | collective-permute-start | bytes 6152 | tf_op jit(solution)/shard_map/ppermute | solution.py:301
  41.1 3.2 %collective-permute-start.10 = (bf16[528,128]{1,0:T(8,128)(2,1)S(1)}, bf16[528,128]{1,0:T(8,128)(2,1)S(1)}, u32[]{:S(2)}, u32[]{:S(2)}) collective-permute-start(bf16[528,128]{1,0:T(8,128)(2,1)S(1)} %get-tuple-element.93.refs_0_), channel_id=1, source_target_pairs={{0,12},{1,13},{2,14},{3,15},{4,8},{5,9},{6,10},{7,11},{8,4},{9,5},... | collective-permute-start | bytes 405512 | tf_op jit(solution)/shard_map/ppermute | solution.py:301
  45.9 4.9 %weight.9.refs_4_ = bf16[2048,1024]{1,0:T(8,128)(2,1)S(1)} custom-call(s32[1]{0:T(128)} %bitcast.4.plane, s32[8,128]{1,0:T(8,128)S(1)} %get-tuple-element.139.place), custom_call_target="tpu_custom_call" | custom-call | flops 41943040 | bytes 4194304 | tf_op jit(solution)/shard_map/weight/pallas_call | solution.py:184
  54.3 3.5 %collective-permute-start.16 = (bf16[656,128]{1,0:T(8,128)(2,1)S(1)}, bf16[656,128]{1,0:T(8,128)(2,1)S(1)}, u32[]{:S(2)}, u32[]{:S(2)}) collective-permute-start(bf16[656,128]{1,0:T(8,128)(2,1)S(1)} %pair.9.part_a), channel_id=1, source_target_pairs={{0,64},{16,80},{32,96},{48,112},{64,0},{80,16},{96,32},{112,48},{1... | collective-permute-start | bytes 503816 | tf_op jit(solution)/shard_map/ppermute | solution.py:301
  61.5 4.0 %collective-permute-done.16.part_d = bf16[656,128]{1,0:T(8,128)(2,1)S(1)} collective-permute-done((bf16[656,128]{1,0:T(8,128)(2,1)S(1)}, bf16[656,128]{1,0:T(8,128)(2,1)S(1)}, u32[]{:S(2)}, u32[]{:S(2)}) %collective-permute-start.16) | collective-permute-done | bytes 167968 | tf_op jit(solution)/shard_map/ppermute | solution.py:301
  65.7 3.2 %collective-permute-start.17 = (bf16[528,128]{1,0:T(8,128)(2,1)S(1)}, bf16[528,128]{1,0:T(8,128)(2,1)S(1)}, u32[]{:S(2)}, u32[]{:S(2)}) collective-permute-start(bf16[528,128]{1,0:T(8,128)(2,1)S(1)} %get-tuple-element.98.refs_0_), channel_id=1, source_target_pairs={{0,12},{1,13},{2,14},{3,15},{4,8},{5,9},{6,10},{7,11},{8,4},{9,5},... | collective-permute-start | bytes 405512 | tf_op jit(solution)/shard_map/ppermute | solution.py:301
  70.5 4.9 %weight.10.refs_4_ = bf16[2048,1024]{1,0:T(8,128)(2,1)S(1)} custom-call(s32[1]{0:T(128)} %bitcast.4.plane, s32[8,128]{1,0:T(8,128)S(1)} %get-tuple-element.139.place), custom_call_target="tpu_custom_call" | custom-call | flops 41943040 | bytes 4194304 | tf_op jit(solution)/shard_map/weight/pallas_call | solution.py:184
  78.3 3.1 %collective-permute-start.21 = (bf16[656,128]{1,0:T(8,128)(2,1)S(1)}, bf16[656,128]{1,0:T(8,128)(2,1)S(1)}, u32[]{:S(2)}, u32[]{:S(2)}) collective-permute-start(bf16[656,128]{1,0:T(8,128)(2,1)S(1)} %pair.10.part_a), channel_id=1, source_target_pairs={{0,3},{1,2},{2,1},{3,0},{4,7},{5,6},{6,5},{7,4},{8,11},{9,10},{10,... | collective-permute-start | bytes 503816 | tf_op jit(solution)/shard_map/ppermute | solution.py:301
  83.1 2.9 %collective-permute-done.21.part_b = bf16[656,128]{1,0:T(8,128)(2,1)S(1)} collective-permute-done((bf16[656,128]{1,0:T(8,128)(2,1)S(1)}, bf16[656,128]{1,0:T(8,128)(2,1)S(1)}, u32[]{:S(2)}, u32[]{:S(2)}) %collective-permute-start.21) | collective-permute-done | bytes 167968 | tf_op jit(solution)/shard_map/ppermute | solution.py:301
  95.8 4.9 %weight.11.refs_4_ = bf16[2048,1024]{1,0:T(8,128)(2,1)S(1)} custom-call(s32[1]{0:T(128)} %bitcast.4.plane, s32[8,128]{1,0:T(8,128)S(1)} %get-tuple-element.139.place), custom_call_target="tpu_custom_call" | custom-call | flops 41943040 | bytes 4194304 | tf_op jit(solution)/shard_map/weight/pallas_call | solution.py:184
  104.6 3.5 %collective-permute-start.30 = (bf16[656,128]{1,0:T(8,128)(2,1)S(1)}, bf16[656,128]{1,0:T(8,128)(2,1)S(1)}, u32[]{:S(2)}, u32[]{:S(2)}) collective-permute-start(bf16[656,128]{1,0:T(8,128)(2,1)S(1)} %pair.11.part_a), channel_id=1, source_target_pairs={{0,64},{16,80},{32,96},{48,112},{64,0},{80,16},{96,32},{112,48},{1... | collective-permute-start | bytes 503816 | tf_op jit(solution)/shard_map/ppermute | solution.py:301
  108.1 2.8 %collective-permute-done.28.part_b = bf16[656,128]{1,0:T(8,128)(2,1)S(1)} collective-permute-done((bf16[656,128]{1,0:T(8,128)(2,1)S(1)}, bf16[656,128]{1,0:T(8,128)(2,1)S(1)}, u32[]{:S(2)}, u32[]{:S(2)}) %collective-permute-start.28) | collective-permute-done | bytes 167968 | tf_op jit(solution)/shard_map/ppermute | solution.py:301
  111.7 4.0 %collective-permute-done.30.part_d = bf16[656,128]{1,0:T(8,128)(2,1)S(1)} collective-permute-done((bf16[656,128]{1,0:T(8,128)(2,1)S(1)}, bf16[656,128]{1,0:T(8,128)(2,1)S(1)}, u32[]{:S(2)}, u32[]{:S(2)}) %collective-permute-start.30) | collective-permute-done | bytes 167968 | tf_op jit(solution)/shard_map/ppermute | solution.py:301
  120.8 4.9 %weight.12.refs_4_ = bf16[2048,1024]{1,0:T(8,128)(2,1)S(1)} custom-call(s32[1]{0:T(128)} %bitcast.4.plane, s32[8,128]{1,0:T(8,128)S(1)} %get-tuple-element.139.place), custom_call_target="tpu_custom_call" | custom-call | flops 41943040 | bytes 4194304 | tf_op jit(solution)/shard_map/weight/pallas_call | solution.py:184
  132.8 2.8 %collective-permute-done.35.part_b = bf16[656,128]{1,0:T(8,128)(2,1)S(1)} collective-permute-done((bf16[656,128]{1,0:T(8,128)(2,1)S(1)}, bf16[656,128]{1,0:T(8,128)(2,1)S(1)}, u32[]{:S(2)}, u32[]{:S(2)}) %collective-permute-start.35) | collective-permute-done | bytes 167968 | tf_op jit(solution)/shard_map/ppermute | solution.py:301
  145.5 4.9 %weight.13.refs_4_ = bf16[2048,1024]{1,0:T(8,128)(2,1)S(1)} custom-call(s32[1]{0:T(128)} %bitcast.4.plane, s32[8,128]{1,0:T(8,128)S(1)} %get-tuple-element.139.place), custom_call_target="tpu_custom_call" | custom-call | flops 41943040 | bytes 4194304 | tf_op jit(solution)/shard_map/weight/pallas_call | solution.py:184
  154.0 3.5 %collective-permute-start.44 = (bf16[656,128]{1,0:T(8,128)(2,1)S(1)}, bf16[656,128]{1,0:T(8,128)(2,1)S(1)}, u32[]{:S(2)}, u32[]{:S(2)}) collective-permute-start(bf16[656,128]{1,0:T(8,128)(2,1)S(1)} %pair.13.part_a), channel_id=1, source_target_pairs={{0,64},{16,80},{32,96},{48,112},{64,0},{80,16},{96,32},{112,48},{1... | collective-permute-start | bytes 503816 | tf_op jit(solution)/shard_map/ppermute | solution.py:301
  157.6 2.8 %collective-permute-done.42.part_b = bf16[656,128]{1,0:T(8,128)(2,1)S(1)} collective-permute-done((bf16[656,128]{1,0:T(8,128)(2,1)S(1)}, bf16[656,128]{1,0:T(8,128)(2,1)S(1)}, u32[]{:S(2)}, u32[]{:S(2)}) %collective-permute-start.42) | collective-permute-done | bytes 167968 | tf_op jit(solution)/shard_map/ppermute | solution.py:301
  161.2 4.0 %collective-permute-done.44.part_d = bf16[656,128]{1,0:T(8,128)(2,1)S(1)} collective-permute-done((bf16[656,128]{1,0:T(8,128)(2,1)S(1)}, bf16[656,128]{1,0:T(8,128)(2,1)S(1)}, u32[]{:S(2)}, u32[]{:S(2)}) %collective-permute-start.44) | collective-permute-done | bytes 167968 | tf_op jit(solution)/shard_map/ppermute | solution.py:301
  170.2 4.9 %weight.14.refs_4_ = bf16[2048,1024]{1,0:T(8,128)(2,1)S(1)} custom-call(s32[1]{0:T(128)} %bitcast.4.plane, s32[8,128]{1,0:T(8,128)S(1)} %get-tuple-element.139.place), custom_call_target="tpu_custom_call" | custom-call | flops 41943040 | bytes 4194304 | tf_op jit(solution)/shard_map/weight/pallas_call | solution.py:184
  182.3 2.8 %collective-permute-done.49.part_b = bf16[656,128]{1,0:T(8,128)(2,1)S(1)} collective-permute-done((bf16[656,128]{1,0:T(8,128)(2,1)S(1)}, bf16[656,128]{1,0:T(8,128)(2,1)S(1)}, u32[]{:S(2)}, u32[]{:S(2)}) %collective-permute-start.49) | collective-permute-done | bytes 167968 | tf_op jit(solution)/shard_map/ppermute | solution.py:301
  190.2 2.9 %collective-permute-start.56 = (bf16[528,128]{1,0:T(8,128)(2,1)S(1)}, bf16[528,128]{1,0:T(8,128)(2,1)S(1)}, u32[]{:S(2)}, u32[]{:S(2)}) collective-permute-start(bf16[528,128]{1,0:T(8,128)(2,1)S(1)} %get-tuple-element.138.refs_0_), channel_id=1, source_target_pairs={{0,12},{1,13},{2,14},{3,15},{4,8},{5,9},{6,10},{7,11},{8,4},{9,5},... | collective-permute-start | bytes 405512 | tf_op jit(solution)/shard_map/ppermute | solution.py:301
  196.5 4.0 %collective-permute-done.52.refs_1_ = bf16[128,128]{1,0:T(8,128)(2,1)S(1)} collective-permute-done((bf16[128,128]{1,0:T(8,128)(2,1)S(1)}, bf16[128,128]{1,0:T(8,128)(2,1)S(1)}, u32[]{:S(2)}, u32[]{:S(2)}) %collective-permute-start.52) | collective-permute-done | bytes 32800 | tf_op jit(solution)/shard_map/ppermute | solution.py:301
  200.4 4.9 %weight.15.refs_4_ = bf16[2048,1024]{1,0:T(8,128)(2,1)S(1)} custom-call(s32[1]{0:T(128)} %bitcast.4.plane, s32[8,128]{1,0:T(8,128)S(1)} %get-tuple-element.139.place), custom_call_target="tpu_custom_call" | custom-call | flops 41943040 | bytes 4194304 | tf_op jit(solution)/shard_map/weight/pallas_call | solution.py:184
  208.2 4.2 %collective-permute-start.65 = (f32[128,128]{1,0:T(8,128)S(1)}, f32[128,128]{1,0:T(8,128)S(1)}, u32[]{:S(2)}, u32[]{:S(2)}) collective-permute-start(f32[128,128]{1,0:T(8,128)S(1)} %student_up.1), channel_id=1, source_target_pairs={{0,2},{1,3},{2,0},{3,1},{4,6},{5,7},{6,4},{7,5},{8,10},{9,11},{10,... | collective-permute-start | bytes 196616 | tf_op jit(solution)/shard_map/ppermute | solution.py:301
  218.1 3.9 %collective-permute-start.68 = (f32[128,128]{1,0:T(8,128)S(1)}, f32[128,128]{1,0:T(8,128)S(1)}, u32[]{:S(2)}, u32[]{:S(2)}) collective-permute-start(f32[128,128]{1,0:T(8,128)S(1)} %add_add_fusion.3), channel_id=1, source_target_pairs={{0,8},{1,9},{2,10},{3,11},{4,12},{5,13},{6,14},{7,15},{8,0},{9,1},... | collective-permute-start | bytes 196616 | tf_op jit(solution)/shard_map/ppermute | solution.py:301
  228.6 4.0 %collective-permute-start.71 = (f32[136,128]{1,0:T(8,128)S(1)}, f32[136,128]{1,0:T(8,128)S(1)}, u32[]{:S(2)}, u32[]{:S(2)}) collective-permute-start(f32[136,128]{1,0:T(8,128)S(1)} %get-tuple-element.153), channel_id=1, source_target_pairs={{0,2},{1,3},{2,0},{3,1},{4,6},{5,7},{6,4},{7,5},{8,10},{9,11},{10,... | collective-permute-start | bytes 208904 | tf_op jit(solution)/shard_map/ppermute | solution.py:301
  238.3 3.3 %collective-permute-start.74 = (f32[136,128]{1,0:T(8,128)S(1)}, f32[136,128]{1,0:T(8,128)S(1)}, u32[]{:S(2)}, u32[]{:S(2)}) collective-permute-start(f32[136,128]{1,0:T(8,128)S(1)} %add_add_fusion.1), channel_id=1, source_target_pairs={{0,8},{1,9},{2,10},{3,11},{4,12},{5,13},{6,14},{7,15},{8,0},{9,1},... | collective-permute-start | bytes 208904 | tf_op jit(solution)/shard_map/ppermute | solution.py:301
  (178 shorter events, 123.6 us)
Async XLA Ops:
  2.7 10.0 %all-to-all-start = ((f32[8,16,128]{2,1,0:T(8,128)}), f32[8,16,128]{2,1,0:T(8,128)S(1)}, u32[]{:S(2)}, u32[]{:S(2)}) async-start(f32[8,16,128]{2,1,0:T(8,128)} %pack.1), calls=%async_computation | async-start | bytes 131072 | tf_op jit(solution)/shard_map/all_to_all | solution.py:391
  13.2 10.5 %collective-permute-start = (f32[4,1,128]{2,1,0:T(1,128)S(1)}, f32[4,1,128]{2,1,0:T(1,128)S(1)}, u32[]{:S(2)}, u32[]{:S(2)}) collective-permute-start(f32[4,1,128]{2,1,0:T(1,128)S(1)} %get-tuple-element.82.refs_0_), channel_id=1, source_target_pairs={{0,12},{1,13},{2,14},{3,15},{4,8},{5,9},{6,10},{7,11},{8,4},{9,5},... | collective-permute-start | bytes 6152 | tf_op jit(solution)/shard_map/ppermute | solution.py:301
  26.1 14.7 %collective-permute-start.4 = (bf16[656,128]{1,0:T(8,128)(2,1)S(1)}, bf16[656,128]{1,0:T(8,128)(2,1)S(1)}, u32[]{:S(2)}, u32[]{:S(2)}) collective-permute-start(bf16[656,128]{1,0:T(8,128)(2,1)S(1)} %pair.8.part_a), channel_id=1, source_target_pairs={{0,3},{1,2},{2,1},{3,0},{4,7},{5,6},{6,5},{7,4},{8,11},{9,10},{10,... | collective-permute-start | bytes 503816 | tf_op jit(solution)/shard_map/ppermute | solution.py:301
  29.2 11.6 %collective-permute-start.5 = (bf16[656,128]{1,0:T(8,128)(2,1)S(1)}, bf16[656,128]{1,0:T(8,128)(2,1)S(1)}, u32[]{:S(2)}, u32[]{:S(2)}) collective-permute-start(bf16[656,128]{1,0:T(8,128)(2,1)S(1)} %pair.8.part_a), channel_id=1, source_target_pairs={{0,1},{1,0},{2,3},{3,2},{4,5},{5,4},{6,7},{7,6},{8,9},{9,8},{10,11... | collective-permute-start | bytes 503816 | tf_op jit(solution)/shard_map/ppermute | solution.py:301
  29.3 11.5 %collective-permute-start.6 = (bf16[656,128]{1,0:T(8,128)(2,1)S(1)}, bf16[656,128]{1,0:T(8,128)(2,1)S(1)}, u32[]{:S(2)}, u32[]{:S(2)}) collective-permute-start(bf16[656,128]{1,0:T(8,128)(2,1)S(1)} %pair.8.part_a), channel_id=1, source_target_pairs={{0,2},{1,3},{2,0},{3,1},{4,6},{5,7},{6,4},{7,5},{8,10},{9,11},{10,... | collective-permute-start | bytes 503816 | tf_op jit(solution)/shard_map/ppermute | solution.py:301
  41.1 9.6 %collective-permute-start.10 = (bf16[528,128]{1,0:T(8,128)(2,1)S(1)}, bf16[528,128]{1,0:T(8,128)(2,1)S(1)}, u32[]{:S(2)}, u32[]{:S(2)}) collective-permute-start(bf16[528,128]{1,0:T(8,128)(2,1)S(1)} %get-tuple-element.93.refs_0_), channel_id=1, source_target_pairs={{0,12},{1,13},{2,14},{3,15},{4,8},{5,9},{6,10},{7,11},{8,4},{9,5},... | collective-permute-start | bytes 405512 | tf_op jit(solution)/shard_map/ppermute | solution.py:301
  53.1 7.6 %collective-permute-start.14 = (bf16[656,128]{1,0:T(8,128)(2,1)S(1)}, bf16[656,128]{1,0:T(8,128)(2,1)S(1)}, u32[]{:S(2)}, u32[]{:S(2)}) collective-permute-start(bf16[656,128]{1,0:T(8,128)(2,1)S(1)} %pair.9.part_a), channel_id=1, source_target_pairs={{0,96},{16,112},{32,64},{48,80},{64,32},{80,48},{96,0},{112,16},{1... | collective-permute-start | bytes 503816 | tf_op jit(solution)/shard_map/ppermute | solution.py:301
  54.3 11.2 %collective-permute-start.16 = (bf16[656,128]{1,0:T(8,128)(2,1)S(1)}, bf16[656,128]{1,0:T(8,128)(2,1)S(1)}, u32[]{:S(2)}, u32[]{:S(2)}) collective-permute-start(bf16[656,128]{1,0:T(8,128)(2,1)S(1)} %pair.9.part_a), channel_id=1, source_target_pairs={{0,64},{16,80},{32,96},{48,112},{64,0},{80,16},{96,32},{112,48},{1... | collective-permute-start | bytes 503816 | tf_op jit(solution)/shard_map/ppermute | solution.py:301
  65.7 9.6 %collective-permute-start.17 = (bf16[528,128]{1,0:T(8,128)(2,1)S(1)}, bf16[528,128]{1,0:T(8,128)(2,1)S(1)}, u32[]{:S(2)}, u32[]{:S(2)}) collective-permute-start(bf16[528,128]{1,0:T(8,128)(2,1)S(1)} %get-tuple-element.98.refs_0_), channel_id=1, source_target_pairs={{0,12},{1,13},{2,14},{3,15},{4,8},{5,9},{6,10},{7,11},{8,4},{9,5},... | collective-permute-start | bytes 405512 | tf_op jit(solution)/shard_map/ppermute | solution.py:301
  78.3 7.7 %collective-permute-start.21 = (bf16[656,128]{1,0:T(8,128)(2,1)S(1)}, bf16[656,128]{1,0:T(8,128)(2,1)S(1)}, u32[]{:S(2)}, u32[]{:S(2)}) collective-permute-start(bf16[656,128]{1,0:T(8,128)(2,1)S(1)} %pair.10.part_a), channel_id=1, source_target_pairs={{0,3},{1,2},{2,1},{3,0},{4,7},{5,6},{6,5},{7,4},{8,11},{9,10},{10,... | collective-permute-start | bytes 503816 | tf_op jit(solution)/shard_map/ppermute | solution.py:301
  81.4 9.5 %collective-permute-start.23 = (bf16[656,128]{1,0:T(8,128)(2,1)S(1)}, bf16[656,128]{1,0:T(8,128)(2,1)S(1)}, u32[]{:S(2)}, u32[]{:S(2)}) collective-permute-start(bf16[656,128]{1,0:T(8,128)(2,1)S(1)} %pair.10.part_a), channel_id=1, source_target_pairs={{0,2},{1,3},{2,0},{3,1},{4,6},{5,7},{6,4},{7,5},{8,10},{9,11},{10,... | collective-permute-start | bytes 503816 | tf_op jit(solution)/shard_map/ppermute | solution.py:301
  91.1 9.6 %collective-permute-start.24 = (bf16[528,128]{1,0:T(8,128)(2,1)S(1)}, bf16[528,128]{1,0:T(8,128)(2,1)S(1)}, u32[]{:S(2)}, u32[]{:S(2)}) collective-permute-start(bf16[528,128]{1,0:T(8,128)(2,1)S(1)} %get-tuple-element.104.refs_0_), channel_id=1, source_target_pairs={{0,12},{1,13},{2,14},{3,15},{4,8},{5,9},{6,10},{7,11},{8,4},{9,5},... | collective-permute-start | bytes 405512 | tf_op jit(solution)/shard_map/ppermute | solution.py:301
  103.3 7.6 %collective-permute-start.28 = (bf16[656,128]{1,0:T(8,128)(2,1)S(1)}, bf16[656,128]{1,0:T(8,128)(2,1)S(1)}, u32[]{:S(2)}, u32[]{:S(2)}) collective-permute-start(bf16[656,128]{1,0:T(8,128)(2,1)S(1)} %pair.11.part_a), channel_id=1, source_target_pairs={{0,96},{16,112},{32,64},{48,80},{64,32},{80,48},{96,0},{112,16},{1... | collective-permute-start | bytes 503816 | tf_op jit(solution)/shard_map/ppermute | solution.py:301
  104.6 11.2 %collective-permute-start.30 = (bf16[656,128]{1,0:T(8,128)(2,1)S(1)}, bf16[656,128]{1,0:T(8,128)(2,1)S(1)}, u32[]{:S(2)}, u32[]{:S(2)}) collective-permute-start(bf16[656,128]{1,0:T(8,128)(2,1)S(1)} %pair.11.part_a), channel_id=1, source_target_pairs={{0,64},{16,80},{32,96},{48,112},{64,0},{80,16},{96,32},{112,48},{1... | collective-permute-start | bytes 503816 | tf_op jit(solution)/shard_map/ppermute | solution.py:301
  116.0 9.6 %collective-permute-start.31 = (bf16[528,128]{1,0:T(8,128)(2,1)S(1)}, bf16[528,128]{1,0:T(8,128)(2,1)S(1)}, u32[]{:S(2)}, u32[]{:S(2)}) collective-permute-start(bf16[528,128]{1,0:T(8,128)(2,1)S(1)} %get-tuple-element.108.refs_0_), channel_id=1, source_target_pairs={{0,12},{1,13},{2,14},{3,15},{4,8},{5,9},{6,10},{7,11},{8,4},{9,5},... | collective-permute-start | bytes 405512 | tf_op jit(solution)/shard_map/ppermute | solution.py:301
  128.1 7.6 %collective-permute-start.35 = (bf16[656,128]{1,0:T(8,128)(2,1)S(1)}, bf16[656,128]{1,0:T(8,128)(2,1)S(1)}, u32[]{:S(2)}, u32[]{:S(2)}) collective-permute-start(bf16[656,128]{1,0:T(8,128)(2,1)S(1)} %pair.12.part_a), channel_id=1, source_target_pairs={{0,3},{1,2},{2,1},{3,0},{4,7},{5,6},{6,5},{7,4},{8,11},{9,10},{10,... | collective-permute-start | bytes 503816 | tf_op jit(solution)/shard_map/ppermute | solution.py:301
  130.9 9.6 %collective-permute-start.37 = (bf16[656,128]{1,0:T(8,128)(2,1)S(1)}, bf16[656,128]{1,0:T(8,128)(2,1)S(1)}, u32[]{:S(2)}, u32[]{:S(2)}) collective-permute-start(bf16[656,128]{1,0:T(8,128)(2,1)S(1)} %pair.12.part_a), channel_id=1, source_target_pairs={{0,2},{1,3},{2,0},{3,1},{4,6},{5,7},{6,4},{7,5},{8,10},{9,11},{10,... | collective-permute-start | bytes 503816 | tf_op jit(solution)/shard_map/ppermute | solution.py:301
  140.7 9.6 %collective-permute-start.38 = (bf16[528,128]{1,0:T(8,128)(2,1)S(1)}, bf16[528,128]{1,0:T(8,128)(2,1)S(1)}, u32[]{:S(2)}, u32[]{:S(2)}) collective-permute-start(bf16[528,128]{1,0:T(8,128)(2,1)S(1)} %get-tuple-element.114.refs_0_), channel_id=1, source_target_pairs={{0,12},{1,13},{2,14},{3,15},{4,8},{5,9},{6,10},{7,11},{8,4},{9,5},... | collective-permute-start | bytes 405512 | tf_op jit(solution)/shard_map/ppermute | solution.py:301
  152.8 7.6 %collective-permute-start.42 = (bf16[656,128]{1,0:T(8,128)(2,1)S(1)}, bf16[656,128]{1,0:T(8,128)(2,1)S(1)}, u32[]{:S(2)}, u32[]{:S(2)}) collective-permute-start(bf16[656,128]{1,0:T(8,128)(2,1)S(1)} %pair.13.part_a), channel_id=1, source_target_pairs={{0,96},{16,112},{32,64},{48,80},{64,32},{80,48},{96,0},{112,16},{1... | collective-permute-start | bytes 503816 | tf_op jit(solution)/shard_map/ppermute | solution.py:301
  154.0 11.2 %collective-permute-start.44 = (bf16[656,128]{1,0:T(8,128)(2,1)S(1)}, bf16[656,128]{1,0:T(8,128)(2,1)S(1)}, u32[]{:S(2)}, u32[]{:S(2)}) collective-permute-start(bf16[656,128]{1,0:T(8,128)(2,1)S(1)} %pair.13.part_a), channel_id=1, source_target_pairs={{0,64},{16,80},{32,96},{48,112},{64,0},{80,16},{96,32},{112,48},{1... | collective-permute-start | bytes 503816 | tf_op jit(solution)/shard_map/ppermute | solution.py:301
  165.5 9.6 %collective-permute-start.45 = (bf16[528,128]{1,0:T(8,128)(2,1)S(1)}, bf16[528,128]{1,0:T(8,128)(2,1)S(1)}, u32[]{:S(2)}, u32[]{:S(2)}) collective-permute-start(bf16[528,128]{1,0:T(8,128)(2,1)S(1)} %get-tuple-element.118.refs_0_), channel_id=1, source_target_pairs={{0,12},{1,13},{2,14},{3,15},{4,8},{5,9},{6,10},{7,11},{8,4},{9,5},... | collective-permute-start | bytes 405512 | tf_op jit(solution)/shard_map/ppermute | solution.py:301
  177.5 7.6 %collective-permute-start.49 = (bf16[656,128]{1,0:T(8,128)(2,1)S(1)}, bf16[656,128]{1,0:T(8,128)(2,1)S(1)}, u32[]{:S(2)}, u32[]{:S(2)}) collective-permute-start(bf16[656,128]{1,0:T(8,128)(2,1)S(1)} %pair.14.part_a), channel_id=1, source_target_pairs={{0,3},{1,2},{2,1},{3,0},{4,7},{5,6},{6,5},{7,4},{8,11},{9,10},{10,... | collective-permute-start | bytes 503816 | tf_op jit(solution)/shard_map/ppermute | solution.py:301
  180.3 9.6 %collective-permute-start.51 = (bf16[656,128]{1,0:T(8,128)(2,1)S(1)}, bf16[656,128]{1,0:T(8,128)(2,1)S(1)}, u32[]{:S(2)}, u32[]{:S(2)}) collective-permute-start(bf16[656,128]{1,0:T(8,128)(2,1)S(1)} %pair.14.part_a), channel_id=1, source_target_pairs={{0,2},{1,3},{2,0},{3,1},{4,6},{5,7},{6,4},{7,5},{8,10},{9,11},{10,... | collective-permute-start | bytes 503816 | tf_op jit(solution)/shard_map/ppermute | solution.py:301
  190.2 15.9 %collective-permute-start.56 = (bf16[528,128]{1,0:T(8,128)(2,1)S(1)}, bf16[528,128]{1,0:T(8,128)(2,1)S(1)}, u32[]{:S(2)}, u32[]{:S(2)}) collective-permute-start(bf16[528,128]{1,0:T(8,128)(2,1)S(1)} %get-tuple-element.138.refs_0_), channel_id=1, source_target_pairs={{0,12},{1,13},{2,14},{3,15},{4,8},{5,9},{6,10},{7,11},{8,4},{9,5},... | collective-permute-start | bytes 405512 | tf_op jit(solution)/shard_map/ppermute | solution.py:301
  193.1 13.0 %collective-permute-start.57 = (bf16[528,128]{1,0:T(8,128)(2,1)S(1)}, bf16[528,128]{1,0:T(8,128)(2,1)S(1)}, u32[]{:S(2)}, u32[]{:S(2)}) collective-permute-start(bf16[528,128]{1,0:T(8,128)(2,1)S(1)} %get-tuple-element.138.refs_0_), channel_id=1, source_target_pairs={{0,4},{1,5},{2,6},{3,7},{4,0},{5,1},{6,2},{7,3},{8,12},{9,13},{10,... | collective-permute-start | bytes 405512 | tf_op jit(solution)/shard_map/ppermute | solution.py:301
  193.1 13.0 %collective-permute-start.58 = (bf16[528,128]{1,0:T(8,128)(2,1)S(1)}, bf16[528,128]{1,0:T(8,128)(2,1)S(1)}, u32[]{:S(2)}, u32[]{:S(2)}) collective-permute-start(bf16[528,128]{1,0:T(8,128)(2,1)S(1)} %get-tuple-element.138.refs_0_), channel_id=1, source_target_pairs={{0,8},{1,9},{2,10},{3,11},{4,12},{5,13},{6,14},{7,15},{8,0},{9,1},... | collective-permute-start | bytes 405512 | tf_op jit(solution)/shard_map/ppermute | solution.py:301
  196.5 8.8 %collective-permute-start.53 = (bf16[128,128]{1,0:T(8,128)(2,1)S(1)}, bf16[128,128]{1,0:T(8,128)(2,1)S(1)}, u32[]{:S(2)}, u32[]{:S(2)}) collective-permute-start(bf16[128,128]{1,0:T(8,128)(2,1)S(1)} %get-tuple-element.126), channel_id=1, source_target_pairs={{0,32},{16,48},{32,0},{48,16},{64,96},{80,112},{96,64},{112,80},{1... | collective-permute-start | bytes 98312 | tf_op jit(solution)/shard_map/ppermute | solution.py:301
  208.2 7.9 %collective-permute-start.64 = (f32[128,128]{1,0:T(8,128)S(1)}, f32[128,128]{1,0:T(8,128)S(1)}, u32[]{:S(2)}, u32[]{:S(2)}) collective-permute-start(f32[128,128]{1,0:T(8,128)S(1)} %student_up.1), channel_id=1, source_target_pairs={{0,1},{1,0},{2,3},{3,2},{4,5},{5,4},{6,7},{7,6},{8,9},{9,8},{10,11... | collective-permute-start | bytes 196616 | tf_op jit(solution)/shard_map/ppermute | solution.py:301
  208.2 9.5 %collective-permute-start.65 = (f32[128,128]{1,0:T(8,128)S(1)}, f32[128,128]{1,0:T(8,128)S(1)}, u32[]{:S(2)}, u32[]{:S(2)}) collective-permute-start(f32[128,128]{1,0:T(8,128)S(1)} %student_up.1), channel_id=1, source_target_pairs={{0,2},{1,3},{2,0},{3,1},{4,6},{5,7},{6,4},{7,5},{8,10},{9,11},{10,... | collective-permute-start | bytes 196616 | tf_op jit(solution)/shard_map/ppermute | solution.py:301
  213.0 9.1 %collective-permute-start.60 = (bf16[656,128]{1,0:T(8,128)(2,1)S(1)}, bf16[656,128]{1,0:T(8,128)(2,1)S(1)}, u32[]{:S(2)}, u32[]{:S(2)}) collective-permute-start(bf16[656,128]{1,0:T(8,128)(2,1)S(1)} %pair.15.part_a), channel_id=1, source_target_pairs={{0,96},{16,112},{32,64},{48,80},{64,32},{80,48},{96,0},{112,16},{1... | collective-permute-start | bytes 503816 | tf_op jit(solution)/shard_map/ppermute | solution.py:301
  214.2 9.0 %collective-permute-start.61 = (bf16[656,128]{1,0:T(8,128)(2,1)S(1)}, bf16[656,128]{1,0:T(8,128)(2,1)S(1)}, u32[]{:S(2)}, u32[]{:S(2)}) collective-permute-start(bf16[656,128]{1,0:T(8,128)(2,1)S(1)} %pair.15.part_a), channel_id=1, source_target_pairs={{0,32},{16,48},{32,0},{48,16},{64,96},{80,112},{96,64},{112,80},{1... | collective-permute-start | bytes 503816 | tf_op jit(solution)/shard_map/ppermute | solution.py:301
  216.0 8.5 %collective-permute-start.62 = (bf16[656,128]{1,0:T(8,128)(2,1)S(1)}, bf16[656,128]{1,0:T(8,128)(2,1)S(1)}, u32[]{:S(2)}, u32[]{:S(2)}) collective-permute-start(bf16[656,128]{1,0:T(8,128)(2,1)S(1)} %pair.15.part_a), channel_id=1, source_target_pairs={{0,64},{16,80},{32,96},{48,112},{64,0},{80,16},{96,32},{112,48},{1... | collective-permute-start | bytes 503816 | tf_op jit(solution)/shard_map/ppermute | solution.py:301
  (47 other events, 453.3 us)

commit v4 on v3

v4 whole, which is shorter than its diff:
```python
import functools
import math

import jax
import jax.numpy as jnp
import numpy as np
from jax import lax
from jax.experimental import pallas as pl
from jax.experimental.pallas import tpu as pltpu
from jax.sharding import PartitionSpec as P

D = 16384
R = 128
TOK = 128
LAYERS = 8
SEG = 8
MP = 16
WIDTH = D // MP
PIECE = WIDTH // SEG
STATE = 4 * TOK
GATHER = STATE + 16
SUM = STATE + TOK + 16
FACTS = 48
STEP_Q, STEP_P, STEP_R, STEP_C = 4096, 1024, 256, 128
EPSILON = 1e-05
EMBED_KEY = 7919
BF = jnp.bfloat16
F32 = jnp.float32


def wrapped(value):
    value &= 0xFFFFFFFF
    return np.int32(value - (1 << 32) if value >> 31 else value)


MULT = wrapped(73244475)
MULT_SQ = wrapped(73244475 * 73244475)


def fold(bits):
    return jnp.bitwise_xor(bits, lax.shift_right_logical(bits, jnp.int32(16)))


def uniform_bits(mixed_bits):
    mixed_bits = fold(mixed_bits) * MULT
    mixed_bits = fold(mixed_bits) * MULT_SQ
    mixed_bits = fold(mixed_bits) * MULT
    return lax.shift_right_logical(fold(mixed_bits), jnp.int32(8))


def hashed(mixed_bits, magnitude):
    return uniform_bits(mixed_bits).astype(F32) * np.float32(magnitude * 2.0 / 16777216.0) - np.float32(magnitude)


def ternary(mixed_bits, magnitude):
    bits = uniform_bits(mixed_bits)
    return (lax.rem(bits, jnp.int32(3)) - jnp.int32(1)).astype(F32) * np.float32(magnitude)


def split_row(row):
    high = row.astype(BF).astype(F32)
    index = lax.broadcasted_iota(jnp.int32, (16, row.shape[1]), 0)
    tile = jnp.where(index == 0, high, jnp.where(index == 1, row - high, 0.0))
    return tile.astype(BF)


def joined_row(tile):
    return jnp.sum(tile.astype(F32), axis=0, keepdims=True)


SMEM = pl.BlockSpec(memory_space=pltpu.SMEM)
VMEM = pl.BlockSpec(memory_space=pltpu.VMEM)
HBM = pl.BlockSpec(memory_space=pltpu.HBM)


def call(body, name, out_shape, in_specs, flops=0, nbytes=0, limit=8 << 20, out_specs=None, scratch=(), aliases={}):
    single = not isinstance(out_shape, (tuple, list))
    return pl.pallas_call(
        body,
        out_shape=out_shape,
        in_specs=in_specs,
        out_specs=out_specs or (VMEM if single else tuple(VMEM for _ in out_shape)),
        scratch_shapes=scratch,
        input_output_aliases=aliases,
        name=name,
        cost_estimate=pl.CostEstimate(flops=flops, bytes_accessed=nbytes, transcendentals=0),
        compiler_params=pltpu.CompilerParams(vmem_limit_bytes=limit),
    )


def sds(shape, dtype):
    return jax.ShapeDtypeStruct(shape, dtype)


def gate(value, *others):
    return lax.optimization_barrier((value, *others))[0]


def pack_kernel(seed, student_seed, plane, gain, student_gain, out):
    rows = [gain[:, index * PIECE : (index + 1) * PIECE] for index in range(SEG)]
    for value in (seed[0], student_seed[0]):
        for shift in (16, 8, 0):
            byte = jnp.bitwise_and(lax.shift_right_logical(value, jnp.int32(shift)), jnp.int32(255))
            rows.append(jnp.full((1, PIECE), byte, jnp.int32).astype(F32).astype(BF))
    rows += [jnp.zeros((1, PIECE), BF)] * 2
    start = plane[0] * STEP_Q
    for index in range(4 * SEG):
        rows.append(student_gain[:, pl.ds(pl.multiple_of(start + index * PIECE, PIECE), PIECE)])
    for first in range(0, FACTS, 16):
        out[first : first + 16, :] = jnp.concatenate([row.astype(F32) for row in rows[first : first + 16]], axis=0).astype(BF)


def chip_kernel(core, own, other, out):
    out[core[0]] = own[...]
    out[1 - core[0]] = other[...]


def facts_kernel(place, student_seed, *refs):
    parts, (along_z_out, along_y_out, even_out, place_out, student_out) = refs[:4], refs[4:9]
    fold_place_out, fold_gain_out, up_place_out, up_gain_out, facts = refs[9:]
    core, column, row, plane = place[1], place[2], place[3], place[4]
    for partner, part in zip(PARTNERS, parts):
        facts[pl.ds(2 * jnp.bitwise_xor(column, partner), 2)] = part[...].astype(F32)

    def seed(layer, first):
        high, middle, low = (facts[layer, first + index : first + index + 1, :].astype(jnp.int32) for index in range(3))
        return high * 65536 + middle * 256 + low

    for digit in range(4):
        along_z_out[digit] = facts[0, pl.ds(2 * digit + core, 1), :]
        for pair in range(4):
            even_out[pair, digit] = facts[2 * pair, pl.ds(2 * digit + core, 1), :]
    index = lax.broadcasted_iota(jnp.int32, (16, PIECE), 0)
    gains = jnp.zeros((16, PIECE), F32)
    for pair in range(4):
        gains = jnp.where(index == pair, facts[2 * pair + 1, pl.ds(2 * column + core, 1), :], gains)
    along_y_out[...] = gains.astype(BF)
    even = (row * STEP_P + core * STEP_C) * 16411 + plane * STEP_Q + column * STEP_R
    odd = (column * STEP_R + core * STEP_C) * 16411 + plane * STEP_Q + row * STEP_P
    for layer in range(LAYERS):
        place_out[layer : layer + 1, :] = seed(layer, SEG) * 1000003 + (even if layer % 2 == 0 else odd)
    odd_place = (plane * STEP_Q + column * STEP_R + core * STEP_C) * 16411
    fold_place_out[...] = jnp.broadcast_to(seed(LAYERS - 1, SEG + 3) * 1000003 + odd_place, (SEG, PIECE))
    for digit in range(4):
        fold_gain_out[digit] = facts[LAYERS - 1, pl.ds(16 + SEG * digit + place[0], 1), :]
    block = plane * 4 + row
    for half in range(2):
        chip = facts[pl.ds(2 * column + half, 1)][0]
        high, middle, low = (chip[SEG + 3 + index : SEG + 4 + index].astype(jnp.int32) for index in range(3))
        up_seed = high * 65536 + middle * 256 + low
        up_place_out[half] = jnp.broadcast_to(up_seed * 1000003 + block * (WIDTH * 16411), (SEG, PIECE))
        for digit in range(4):
            index = 16 + SEG * row + 2 * digit + core
            up_gain_out[half, digit] = facts[pl.ds(2 * column + half, 1), pl.ds(index, 1), :][0]
    student_out[...] = jnp.full((SEG, PIECE), student_seed[0] * 1000003 + block * (WIDTH * 16411), jnp.int32)


def squares_tile(squares):
    return split_row(jnp.sum(jnp.transpose(squares), axis=0, keepdims=True))


def embed_kernel(place, token, out, tile_out):
    tokens = jnp.broadcast_to(token[...], (TOK, PIECE)) * 16411 + wrapped(EMBED_KEY * 1000003)
    tokens = tokens + lax.broadcasted_iota(jnp.int32, (TOK, PIECE), 1)
    tokens = tokens + (place[1] * STEP_C + place[3] * STEP_P)
    squares = jnp.zeros((TOK, PIECE), F32)
    for slot, partner in enumerate(PARTNERS):
        for digit in range(4):
            first = jnp.bitwise_xor(place[4], partner) * STEP_Q + digit * STEP_R
            part = hashed(tokens + first, math.sqrt(3.0)).astype(BF)
            out[slot, digit * TOK : (digit + 1) * TOK, :] = part
            wide = part.astype(F32)
            squares = squares + wide * wide
    tile_out[...] = squares_tile(squares)


def first_scale_kernel(embedded, tile, *refs):
    gains, outs = refs[:4], refs[4:]
    for partner in range(4):
        for digit in range(4):
            rows = slice(digit * TOK, (digit + 1) * TOK)
            outs[partner][rows, :] = (embedded[partner, rows, :].astype(F32) * gains[partner][digit]).astype(BF)
        outs[partner][STATE:, :] = tile[...] if partner == 0 else jnp.zeros((16, TOK), BF)


def weight_kernel(layer, plane, place, out):
    chunk = 64
    row_step, col_step = (STEP_R, STEP_P) if layer % 2 == 0 else (STEP_P, STEP_R)
    row = lax.broadcasted_iota(jnp.int32, (chunk, WIDTH), 0)
    col = lax.broadcasted_iota(jnp.int32, (chunk, WIDTH), 1)
    col = (col // 512) * STEP_C + (col // PIECE % 4) * col_step + col % PIECE
    base = row * 16411 + col + jnp.concatenate([place[layer : layer + 1, :]] * (WIDTH // PIECE), axis=1)

    def step(index, carry):
        piece = index // 2
        slot = piece // 4
        partner = jnp.where(slot == 1, PARTNERS[1], jnp.where(slot == 2, PARTNERS[2], slot))
        first = jnp.bitwise_xor(plane[0], partner) * (STEP_Q * 16411) + (piece % 4) * (row_step * 16411) + (index % 2) * (chunk * 16411)
        start = pl.multiple_of(index * chunk, chunk)
        out[pl.ds(start, chunk), :] = hashed(base + first, math.sqrt(3.0 / D)).astype(BF)
        return carry

    lax.fori_loop(0, 2048 // chunk, step, 0, unroll=2)


WEIGHTS = 2048 * WIDTH


def teacher_weight(layer, plane, place):
    body = functools.partial(weight_kernel, layer)
    return call(body, "weight", sds((2048, WIDTH), BF), [SMEM, VMEM], flops=20 * WEIGHTS, nbytes=2 * WEIGHTS)(
        plane, place
    )


def contract_kernel(theirs, core, *refs):
    parts, (weight, *more, out) = refs[:4], refs[4:]
    scaled = [part[digit * TOK : (digit + 1) * TOK, :] for part in parts for digit in range(4)]
    scaled = jnp.concatenate(scaled, axis=1)
    squares = joined_row(parts[0][STATE:, :])
    for part in parts[1:]:
        squares = squares + joined_row(part[STATE:, :])
    out[STATE:GATHER, :] = split_row(squares).astype(out.dtype)
    if more:
        out[GATHER:, :] = more[0][...].astype(out.dtype)
    elif out.shape[0] > GATHER:
        folded = parts[0][GATHER : GATHER + TOK, :].astype(F32)
        for part in parts[1:]:
            folded = folded + part[GATHER : GATHER + TOK, :].astype(F32)
        out[GATHER:, :] = folded.astype(out.dtype)
    first = (1 - core[0] if theirs else core[0]) * STATE
    for pair in range(2):
        columns = pl.ds(pl.multiple_of(first + pair * 256, 256), 256)
        part = jnp.dot(scaled, weight[:, columns], preferred_element_type=F32).astype(out.dtype)
        for half in range(2):
            rows = slice((2 * pair + half) * TOK, (2 * pair + half + 1) * TOK)
            out[rows, :] = part[:, half * PIECE : (half + 1) * PIECE]


def pair_kernel(digit, own, other, stream, *refs):
    *more, out = refs
    total = own[...] + other[...].astype(F32)
    out[:STATE, :] = total[:STATE].astype(BF)
    start = pl.multiple_of(digit[0] * TOK, TOK)
    out[STATE : STATE + TOK, :] = stream[pl.ds(start, TOK), :]
    out[STATE + TOK : SUM, :] = split_row(joined_row(total[STATE:GATHER]))
    if more:
        out[SUM:, :] = more[0][...]
    elif total.shape[0] > GATHER:
        out[SUM:, :] = total[GATHER:].astype(BF)


def placed(digit, parts, out):
    for partner, part in zip(PARTNERS, parts):
        start = pl.multiple_of(jnp.bitwise_xor(digit[0], partner) * TOK, TOK)
        out[pl.ds(start, TOK), :] = part[STATE : STATE + TOK, :]


def pre_kernel(part_a, part_b, part_c, part_d, out):
    wide = [part[GATHER + TOK :, :].astype(F32) for part in (part_a, part_b, part_c, part_d)]
    out[...] = (wide[0] + wide[2]) + (wide[1] + wide[3])


def keep_kernel(digit, part_a, part_b, part_c, part_d, out):
    placed(digit, (part_a, part_b, part_c, part_d), out)


def fold_weight_kernel(place, out):
    base = ternary_base(place)
    for digit in range(4):
        made = ternary(base + digit * (STEP_P * 16411), math.sqrt(1.5 / D))
        out[digit * TOK : (digit + 1) * TOK, :] = made.astype(BF)


def update_kernel(layer, digit, part_a, part_b, part_c, part_d, *refs):
    parts = (part_a, part_b, part_c, part_d)
    following = layer + 1 < LAYERS
    fold = layer + 2 == LAYERS
    if layer == 0:
        stream_out, mean_out, message_out, gains = refs
        for partner, part in zip(PARTNERS, parts):
            for index in range(4):
                row = part[SUM : SUM + 16, :][index : index + 1].astype(F32)
                gains[index, jnp.bitwise_xor(digit[0], partner)] = row
    elif fold:
        gains, fold_weight, fold_gain, stream_out, mean_out, message_out = refs
    elif following:
        gains, stream_out, mean_out, message_out = refs
    else:
        stream_out, mean_out, odd_out, pre_out = refs
    placed(digit, parts, stream_out)

    def total(rows):
        wide = [part[rows, :].astype(F32) for part in parts]
        return (wide[0] + wide[2]) + (wide[1] + wide[3])

    if not following:
        odd_out[...] = stream_out[...]
        pre_out[...] = total(slice(SUM, SUM + TOK))
    squares = joined_row(total(slice(STATE + TOK, SUM)))
    mean = jnp.transpose(jnp.broadcast_to(squares, (TOK, TOK))) * np.float32(1.0 / D)
    mean_out[...] = mean
    scale = lax.rsqrt(mean + EPSILON)
    squares = jnp.zeros((TOK, PIECE), F32)
    folded = jnp.zeros((TOK, R), F32)
    for index in range(4):
        rows = slice(index * TOK, (index + 1) * TOK)
        result = (stream_out[rows, :].astype(F32) + total(rows) * scale).astype(BF)
        stream_out[rows, :] = result
        if following:
            wide = result.astype(F32)
            squares = squares + wide * wide
            message_out[rows, :] = (wide * gains[(layer + 1) // 2, index]).astype(BF)
        if fold:
            scaled = (wide * fold_gain[index]).astype(BF)
            folded = folded + jnp.dot(scaled, fold_weight[rows, :], preferred_element_type=F32)
    if following:
        message_out[STATE:GATHER, :] = squares_tile(squares)
    if fold:
        message_out[GATHER : GATHER + TOK, :] = folded.astype(BF)
        message_out[GATHER + TOK :, :] = total(slice(SUM, SUM + TOK)).astype(BF)


def select_kernel(column, *refs):
    odd, even = refs[:3], refs[3:7]
    odd_out, now_out, later_out, held = refs[7:]
    for index in range(4):
        held[index] = even[index][...]
        held[5 + index] = odd[min(index, 2)][...]
    held[4] = even[3][...]
    odd_out[...] = held[5 + column[0]]
    now_out[...] = held[column[0]]
    later_out[...] = held[column[0] + 1]


def mean_kernel(segment, *refs):
    means, out = refs[:-1], refs[-1]
    mean = means[0][...]
    for layer in range(1, LAYERS - 1):
        mean = jnp.where(segment[0] == layer, means[layer][...], mean)
    out[...] = mean


def swap_kernel(core, column, odd, last_odd, now, later, last, near_out, mine_out):
    end, first = column[0] == 3, core[0] == 0
    later = jnp.where(end, last[...].astype(F32), later[...].astype(F32))
    now = now[...].astype(F32)
    near_out[:STATE, :] = jnp.where(end, last_odd[...].astype(F32), odd[...].astype(F32)).astype(BF)
    near_out[STATE:, :] = jnp.where(first, later, now).astype(BF)
    mine_out[...] = jnp.where(first, now, later).astype(BF)


CORE = [(i, i ^ 1) for i in range(SEG)]
ALONG = {
    "x": ("segment", 2),
    "y": ("mp", 1),
    "z": ("mp", 4),
}


PARTNERS = (0, 2, 1, 3)


def exchange(values, physical):
    axis, step = ALONG[physical]
    size = SEG if axis == "segment" else MP
    values = values if isinstance(values, (list, tuple)) else [values] * 4
    return [values[0]] + [
        lax.ppermute(values[k], axis, [(i, i ^ (k * step)) for i in range(size)]) for k in PARTNERS[1:]
    ]


def summed_along(value, physical):
    own, second, first, third = (part.astype(F32) for part in exchange(value.astype(BF), physical))
    return (own + first) + (second + third)


def ternary_base(place):
    row = lax.broadcasted_iota(jnp.int32, (PIECE, R), 0)
    rank = lax.broadcasted_iota(jnp.int32, (PIECE, R), 1)
    return row * 16411 + rank + place[0:1, :]


def pieces_of(core, index, mine, near, far):
    even = piece_of(core, index, mine, far.at[STATE:])
    odd = piece_of(core, index, near.at[:STATE], far.at[:STATE])
    first = core[0] == 0
    return jnp.where(first, even, odd), jnp.where(first, odd, even)


def piece_of(core, index, here, there):
    first = core[0] == 0
    rows = slice(index // 2 * TOK, (index // 2 + 1) * TOK)
    here, there = here[rows, :].astype(F32), there[rows, :].astype(F32)
    return jnp.where(first, here, there) if index % 2 == 0 else jnp.where(first, there, here)


def student_up_kernel(core, place, gain, now, odd, own_out, other_out):
    totals = []
    for half, stream in enumerate((now, odd)):
        base = ternary_base(place[half]) + core[0] * (STEP_C * 16411)
        total = jnp.zeros((TOK, R), F32)
        for digit in range(4):
            up_weight = ternary(base + digit * (STEP_R * 16411), math.sqrt(1.5 / D)).astype(BF)
            scaled = (stream[digit * TOK : (digit + 1) * TOK, :].astype(F32) * gain[half, digit]).astype(BF)
            total = total + jnp.dot(scaled, up_weight, preferred_element_type=F32)
        totals.append(total)
    first = core[0] == 0
    own_out[...] = jnp.where(first, totals[0], totals[1])
    other_out[...] = jnp.where(first, totals[1], totals[0]).astype(BF)


def student_error_kernel(
    segment, core, place, mine, near, far, pre, last_pre, mean, last_mean, back_out, scaled_out, squared_out, pre_out
):
    base = ternary_base(place) + R
    last = segment[0] == SEG - 1
    scale = lax.rsqrt(jnp.where(last, last_mean[...], mean[...]) + EPSILON)
    rectified = jnp.maximum(jnp.where(last, last_pre[...], pre[...]) * scale, 0.0)
    pre_out[...] = rectified
    squared = (rectified * rectified).astype(BF)
    squared_out[...] = squared
    back = jnp.zeros((TOK, R), F32)
    squares = jnp.zeros((TOK, PIECE), F32)
    for index in range(SEG):
        down_weight = ternary(base + index * PIECE * 16411, math.sqrt(1.5 / R)).astype(BF)
        student = lax.dot_general(squared, down_weight, (((1,), (1,)), ((), ())), preferred_element_type=F32)
        given, target = pieces_of(core, index, mine, near, far)
        error = given + student - target
        squares = squares + error * error
        scaled = (error * np.float32(1.0 / TOK)).astype(BF)
        scaled_out[:, index * PIECE : (index + 1) * PIECE] = scaled
        back = back + jnp.dot(scaled, down_weight, preferred_element_type=F32)
    back_out[:TOK, :] = back.astype(BF)
    back_out[TOK:, :] = jnp.sum(squares.reshape(TOK // 16, 16, PIECE), axis=0).astype(BF)


OVER_TOKENS = (((0,), (0,)), ((), ()))


def student_down_kernel(segment, core, mine, near, far, gain, mean, last_mean, scaled, squared, normed_out, down_out):
    scale = lax.rsqrt(jnp.where(segment[0] == SEG - 1, last_mean[...], mean[...]) + EPSILON)
    for index in range(SEG):
        columns = slice(index * PIECE, (index + 1) * PIECE)
        given, _ = pieces_of(core, index, mine, near, far)
        normed = given * scale * gain[:, columns].astype(F32)
        normed_out[:, columns] = normed.astype(BF)
    down_out[...] = lax.dot_general(scaled[...], squared[...], OVER_TOKENS, preferred_element_type=F32)


def student_grad_kernel(normed, rectified, back, up_out, loss_out):
    back_pre = (back[:TOK, :] * 2.0 * rectified[...]).astype(BF)
    up_out[...] = lax.dot_general(normed[...], back_pre, OVER_TOKENS, preferred_element_type=F32)
    total = jnp.sum(jnp.sum(back[TOK:, :], axis=0, keepdims=True), axis=1, keepdims=True)
    loss_out[...] = total * np.float32(1.0 / (TOK * D))


def local(token_ids, teacher_seeds, student_seeds, teacher_gain, student_gain):
    block = lax.axis_index("mp")
    segment = lax.axis_index("segment")
    core, column = lax.rem(segment, 2), segment // 2
    row, plane = lax.rem(block, 4), block // 4
    place = jnp.stack([segment, core, column, row, plane])
    segment, core, column, row, plane = (part.reshape(1) for part in (segment, core, column, row, plane))
    mean_shape = sds((TOK, TOK), F32)
    state_shape = sds((STATE, PIECE), BF)
    gain_shape = sds((4, 1, PIECE), F32)

    facts = call(pack_kernel, "pack", sds((FACTS, PIECE), BF), [SMEM] * 3 + [VMEM] * 2)(
        teacher_seeds, student_seeds, plane, teacher_gain, student_gain
    )
    facts = call(chip_kernel, "chip", sds((2, FACTS, PIECE), BF), [SMEM, VMEM, VMEM])(
        core, facts, lax.ppermute(facts, "segment", CORE)
    )
    facts = exchange(facts, "x")
    embedded, tile = call(
        embed_kernel, "embed", (sds((4, STATE, PIECE), BF), sds((16, TOK), BF)), [SMEM, VMEM]
    )(place, token_ids.reshape(TOK, 1))
    first_gain, odd_gain, even_gains, places, student_place, fold_place, fold_gain, up_place, up_gain = call(
        facts_kernel,
        "facts",
        (gain_shape, sds((16, PIECE), BF), sds((4, 4, 1, PIECE), F32)) + (sds((LAYERS, PIECE), jnp.int32),) * 3
        + (gain_shape, sds((2, SEG, PIECE), jnp.int32), sds((2, 4, 1, PIECE), F32)),
        [SMEM] * 2 + [VMEM] * 4,
        scratch=(pltpu.VMEM((SEG, FACTS, PIECE), F32),),
    )(place, student_seeds, *facts)
    first_gains = exchange(first_gain, "z")
    weight = teacher_weight(0, plane, places)
    parts = call(
        first_scale_kernel, "first_scale", tuple(sds((GATHER, PIECE), BF) for _ in range(4)), [VMEM] * 6
    )(embedded, tile, *first_gains)
    streams, odd_halves, means = [embedded[0]], [], []
    student_columns = lax.dynamic_slice_in_dim(student_gain, block * WIDTH, WIDTH, 1)
    for layer in range(LAYERS):
        even = layer % 2 == 0
        (axis, digit), other_digit = (("y", row), column) if even else (("x", column), row)
        last = layer + 1 == LAYERS
        if layer:
            parts = exchange(message, "z")
        if layer in (2, 4, 6):
            *parts, odd_halves[-1] = lax.optimization_barrier((*parts, odd_halves[-1]))
        if last:
            weight = teacher_weight(layer, plane, gate(places, message))
        if layer + 2 == LAYERS:
            odd_half, now, later = call(
                select_kernel,
                "select",
                (state_shape,) * 3,
                [SMEM] + [VMEM] * 7,
                scratch=(pltpu.VMEM((9, STATE, PIECE), BF),),
            )(column, *odd_halves, *streams[0:8:2])
            pre_own, pre_other = call(
                student_up_kernel,
                "student_up",
                (sds((TOK, R), F32), sds((TOK, R), BF)),
                [SMEM] + [VMEM] * 4,
                flops=1 << 25,
            )(core, up_place, up_gain, now, odd_half)
            *parts, pre_own, pre_other = lax.optimization_barrier((*parts, pre_own, pre_other))
        if last:
            mean = call(mean_kernel, "mean", mean_shape, [SMEM] + [VMEM] * 7)(segment, *means)
            *parts, mean = lax.optimization_barrier((*parts, mean))
            pre = call(pre_kernel, "pre", sds((TOK, R), F32), [VMEM] * 4)(*parts)
        rows = GATHER + (TOK if layer + 2 >= LAYERS else 0)
        extra = ([pre_other], [pre_own]) if layer + 2 == LAYERS else ([], [])
        contract = dict(in_specs=[SMEM] + [VMEM] * (5 + len(extra[0])), flops=TOK * WEIGHTS, nbytes=2 * WEIGHTS)
        other = call(functools.partial(contract_kernel, True), "contract_other", sds((rows, PIECE), BF), **contract)(
            core, *parts, weight, *extra[0]
        )
        own = call(functools.partial(contract_kernel, False), "contract_own", sds((rows, PIECE), F32), **contract)(
            core, *parts, weight, *extra[1]
        )
        other = lax.ppermute(other, "segment", CORE)
        more = [odd_gain] if layer == 0 else []
        rows = SUM + (16 if layer == 0 else TOK if layer + 2 >= LAYERS else 0)
        summed = call(pair_kernel, "pair", sds((rows, PIECE), BF), [SMEM] + [VMEM] * (3 + len(more)))(
            other_digit, own, other, streams[-1], *more
        )
        parts = exchange(summed, axis)
        out = [state_shape, mean_shape]
        given = [] if layer == 0 or last else [odd_gains if even else even_gains]
        if layer + 2 < LAYERS:
            weight = teacher_weight(layer + 1, plane, gate(places, summed))
            *parts, weight = lax.optimization_barrier((*parts, weight))
        if layer + 2 == LAYERS:
            fold_weight = call(fold_weight_kernel, "fold_weight", state_shape, [VMEM])(gate(fold_place, summed))
            *parts, fold_weight = lax.optimization_barrier((*parts, fold_weight))
            given += [fold_weight, fold_gain]
            out.append(sds((GATHER + 2 * TOK, PIECE), BF))
        elif not last:
            out.append(sds((GATHER, PIECE), BF))
        else:
            out += [state_shape, sds((TOK, R), F32)]
        if layer == 0:
            out.append(sds((4, 4, 1, PIECE), F32))
        stream, stream_mean, *results = call(
            functools.partial(update_kernel, layer), "update", tuple(out), [SMEM] + [VMEM] * (4 + len(given))
        )(digit, *parts, *given)
        if layer in (1, 3, 5):
            odd_halves.append(call(keep_kernel, "keep", state_shape, [SMEM] + [VMEM] * 4)(digit, *parts))
        streams.append(stream)
        if last:
            last_mean, (last_odd, last_pre) = stream_mean, results
        else:
            means.append(stream_mean)
            message = results[0]
        if layer == 0:
            odd_gains = results[1]

    near, mine = call(swap_kernel, "swap", (sds((2 * STATE, PIECE), BF), state_shape), [SMEM] * 2 + [VMEM] * 5)(
        core, column, odd_half, last_odd, now, later, streams[LAYERS]
    )
    far = lax.ppermute(near, "segment", CORE)
    back, scaled, squared, rectified = call(
        student_error_kernel,
        "student_error",
        (sds((TOK + 16, R), BF), sds((TOK, WIDTH), BF), sds((TOK, R), BF), sds((TOK, R), F32)),
        [SMEM] * 2 + [VMEM] * 8,
    )(segment, core, student_place, mine, near, far, pre, last_pre, mean, last_mean)
    normed, grad_down = call(
        student_down_kernel, "student_down", (sds((TOK, WIDTH), BF), sds((WIDTH, R), F32)), [SMEM] * 2 + [VMEM] * 8
    )(segment, core, mine, near, far, student_columns, mean, last_mean, scaled, squared)
    back = summed_along(summed_along(back, "y"), "z")
    grad_up, loss = call(
        student_grad_kernel, "student_grad", (sds((WIDTH, R), F32), sds((1, 1), F32)), [VMEM] * 3
    )(normed, rectified, back)
    return loss.reshape(1), grad_up[None], grad_down[None]


def solution(mesh):
    in_specs = (P(), P("segment"), P("segment"), P("segment", "mp"), P("segment", None))
    out_specs = (P("segment"), P("segment", "mp", None), P("segment", "mp", None))
    return jax.shard_map(local, mesh=mesh, in_specs=in_specs, out_specs=out_specs, check_vma=False)
```

time: 248 us -> 234 us (0.944)
  starting transfers between devices: 108 us -> 82.7 us
  waiting for transfers between devices: 81.9 us -> 89.8 us
    ppermute x66 -> x57, starting transfers between devices: 102 us -> 81.8 us  [exchange(): lax.ppermute(values[k], axis, [(i, i ^ k * step) for i in range(size)])]
    ppermute x66 -> x57, waiting for transfers between devices: 69.8 us -> 80.3 us  [exchange(): lax.ppermute(values[k], axis, [(i, i ^ k * step) for i in range(size)])]
    all_to_all x1 -> x0, starting transfers between devices: 4.38 us -> none  [local(): lax.all_to_all(facts, 'segment', split_axis=0, concat_axis=0, tiled=True)]
    all_to_all x1 -> x0, waiting for transfers between devices: 2.77 us -> none  [local(): lax.all_to_all(facts, 'segment', split_axis=0, concat_axis=0, tiled=True)]
    ppermute x2, waiting for transfers between devices: 0.01 us -> 2.65 us  [the longest x1 1.49 us: local(): far = lax.ppermute(near, 'segment', CORE)]
    pallas_call x32 -> x45, Pallas kernels: 11.7 us -> 12.8 us  [the longest x8 3.84 us: local(): call(functools.partial(contract_kernel, False), 'contract_own', sds((rows...]
  transfers between devices with their start and end apart: 77 -> 67, of which waited for: 45 -> 50; matrix products, arithmetic and copies ran while one was open for 0% -> 1% of each run, Pallas kernels for 18% -> 20%
where the time goes in v4:
time: 234 us; the launch traced here: 233 us
  waiting for transfers between devices  89.8 us (38%)
  starting transfers between devices  82.7 us (35%)
  Pallas kernels  55.3 us (24%)
  local copies, waits for them, and re-layouts  3.07 us (1%)
  between operations  2.46 us (1%)
    ppermute x57, starting transfers between devices, exchange(): lax.ppermute(values[k], axis, [(i, i ^ k * step) for i in range(size)])  81.8 us
    ppermute x57, waiting for transfers between devices, exchange(): lax.ppermute(values[k], axis, [(i, i ^ k * step) for i in range(size)])  80.3 us
    pallas_call x8, Pallas kernels, teacher_weight(): call(body, 'weight', sds((2048, WIDTH), BF), [SMEM, VMEM], flops=20 * WEI...  38.8 us
    ppermute x8, waiting for transfers between devices, local(): other = lax.ppermute(other, 'segment', CORE)  6.9 us
  transfers between devices with their start and end apart: 67, of which 50 were waited for; matrix products, arithmetic and copies ran while one was open for 1% of the time, Pallas kernels for 20%

profile of v4, /device:TPU:0, one launch (start us, length us, event | category | flops | bytes accessed | tf_op | source)
XLA Modules:
  0.0 233.4 jit_solution(429084908230349652)
XLA Ops:
  4.8 3.1 %collective-permute-start.1 = (bf16[2,48,128]{2,1,0:T(8,128)(2,1)S(1)}, bf16[2,48,128]{2,1,0:T(8,128)(2,1)S(1)}, u32[]{:S(2)}, u32[]{:S(2)}) collective-permute-start(bf16[2,48,128]{2,1,0:T(8,128)(2,1)S(1)} %chip.1.refs_0_), channel_id=1, source_target_pairs={{0,64},{16,80},{32,96},{48,112},{64,0},{80,16},{96,32},{112,48},{1... | collective-permute-start | bytes 73736 | tf_op jit(solution)/shard_map/ppermute | solution.py:369
  14.1 4.0 %collective-permute-start.4 = (f32[4,1,128]{2,1,0:T(1,128)S(1)}, f32[4,1,128]{2,1,0:T(1,128)S(1)}, u32[]{:S(2)}, u32[]{:S(2)}) collective-permute-start(f32[4,1,128]{2,1,0:T(1,128)S(1)} %get-tuple-element.130.refs_0_), channel_id=1, source_target_pairs={{0,8},{1,9},{2,10},{3,11},{4,12},{5,13},{6,14},{7,15},{8,0},{9,1},... | collective-permute-start | bytes 6152 | tf_op jit(solution)/shard_map/ppermute | solution.py:369
  19.1 4.9 %weight.8.refs_4_ = bf16[2048,1024]{1,0:T(8,128)(2,1)S(1)} custom-call(s32[1]{0:T(128)} %bitcast.4.plane, s32[8,128]{1,0:T(8,128)S(1)} %get-tuple-element.234.place), custom_call_target="tpu_custom_call" | custom-call | flops 41943040 | bytes 4194304 | tf_op jit(solution)/shard_map/weight/pallas_call | solution.py:211
  26.1 3.1 %collective-permute-start.10 = (bf16[672,128]{1,0:T(8,128)(2,1)S(1)}, bf16[672,128]{1,0:T(8,128)(2,1)S(1)}, u32[]{:S(2)}, u32[]{:S(2)}) collective-permute-start(bf16[672,128]{1,0:T(8,128)(2,1)S(1)} %pair.8.part_a), channel_id=1, source_target_pairs={{0,3},{1,2},{2,1},{3,0},{4,7},{5,6},{6,5},{7,4},{8,11},{9,10},{10,... | collective-permute-start | bytes 516104 | tf_op jit(solution)/shard_map/ppermute | solution.py:369
  30.2 4.9 %weight.9.refs_4_ = bf16[2048,1024]{1,0:T(8,128)(2,1)S(1)} custom-call(s32[1]{0:T(128)} %bitcast.4.plane, s32[8,128]{1,0:T(8,128)S(1)} %get-tuple-element.234.place), custom_call_target="tpu_custom_call" | custom-call | flops 41943040 | bytes 4194304 | tf_op jit(solution)/shard_map/weight/pallas_call | solution.py:211
  38.5 3.1 %collective-permute-start.11 = (bf16[528,128]{1,0:T(8,128)(2,1)S(1)}, bf16[528,128]{1,0:T(8,128)(2,1)S(1)}, u32[]{:S(2)}, u32[]{:S(2)}) collective-permute-start(bf16[528,128]{1,0:T(8,128)(2,1)S(1)} %get-tuple-element.142.refs_0_), channel_id=1, source_target_pairs={{0,8},{1,9},{2,10},{3,11},{4,12},{5,13},{6,14},{7,15},{8,0},{9,1},... | collective-permute-start | bytes 405512 | tf_op jit(solution)/shard_map/ppermute | solution.py:369
  42.7 3.6 %collective-permute-done.11.refs_1_ = bf16[528,128]{1,0:T(8,128)(2,1)S(1)} collective-permute-done((bf16[528,128]{1,0:T(8,128)(2,1)S(1)}, bf16[528,128]{1,0:T(8,128)(2,1)S(1)}, u32[]{:S(2)}, u32[]{:S(2)}) %collective-permute-start.11) | collective-permute-done | bytes 135200 | tf_op jit(solution)/shard_map/ppermute | solution.py:369
  52.3 2.7 %collective-permute-start.17 = (bf16[656,128]{1,0:T(8,128)(2,1)S(1)}, bf16[656,128]{1,0:T(8,128)(2,1)S(1)}, u32[]{:S(2)}, u32[]{:S(2)}) collective-permute-start(bf16[656,128]{1,0:T(8,128)(2,1)S(1)} %pair.9.part_a), channel_id=1, source_target_pairs={{0,96},{16,112},{32,64},{48,80},{64,32},{80,48},{96,0},{112,16},{1... | collective-permute-start | bytes 503816 | tf_op jit(solution)/shard_map/ppermute | solution.py:369
  55.0 4.9 %weight.10.refs_4_ = bf16[2048,1024]{1,0:T(8,128)(2,1)S(1)} custom-call(s32[1]{0:T(128)} %bitcast.4.plane, s32[8,128]{1,0:T(8,128)S(1)} %get-tuple-element.234.place), custom_call_target="tpu_custom_call" | custom-call | flops 41943040 | bytes 4194304 | tf_op jit(solution)/shard_map/weight/pallas_call | solution.py:211
  66.8 3.8 %collective-permute-done.18.refs_1_ = bf16[528,128]{1,0:T(8,128)(2,1)S(1)} collective-permute-done((bf16[528,128]{1,0:T(8,128)(2,1)S(1)}, bf16[528,128]{1,0:T(8,128)(2,1)S(1)}, u32[]{:S(2)}, u32[]{:S(2)}) %collective-permute-start.18) | collective-permute-done | bytes 135200 | tf_op jit(solution)/shard_map/ppermute | solution.py:369
  74.6 3.1 %collective-permute-start.22 = (bf16[656,128]{1,0:T(8,128)(2,1)S(1)}, bf16[656,128]{1,0:T(8,128)(2,1)S(1)}, u32[]{:S(2)}, u32[]{:S(2)}) collective-permute-start(bf16[656,128]{1,0:T(8,128)(2,1)S(1)} %pair.10.part_a), channel_id=1, source_target_pairs={{0,2},{1,3},{2,0},{3,1},{4,6},{5,7},{6,4},{7,5},{8,10},{9,11},{10,... | collective-permute-start | bytes 503816 | tf_op jit(solution)/shard_map/ppermute | solution.py:369
  78.7 4.9 %weight.11.refs_4_ = bf16[2048,1024]{1,0:T(8,128)(2,1)S(1)} custom-call(s32[1]{0:T(128)} %bitcast.4.plane, s32[8,128]{1,0:T(8,128)S(1)} %get-tuple-element.234.place), custom_call_target="tpu_custom_call" | custom-call | flops 41943040 | bytes 4194304 | tf_op jit(solution)/shard_map/weight/pallas_call | solution.py:211
  83.6 2.7 %collective-permute-done.23.part_c = bf16[656,128]{1,0:T(8,128)(2,1)S(1)} collective-permute-done((bf16[656,128]{1,0:T(8,128)(2,1)S(1)}, bf16[656,128]{1,0:T(8,128)(2,1)S(1)}, u32[]{:S(2)}, u32[]{:S(2)}) %collective-permute-start.23) | collective-permute-done | bytes 167968 | tf_op jit(solution)/shard_map/ppermute | solution.py:369
  90.7 3.8 %collective-permute-done.25.refs_1_ = bf16[528,128]{1,0:T(8,128)(2,1)S(1)} collective-permute-done((bf16[528,128]{1,0:T(8,128)(2,1)S(1)}, bf16[528,128]{1,0:T(8,128)(2,1)S(1)}, u32[]{:S(2)}, u32[]{:S(2)}) %collective-permute-start.25) | collective-permute-done | bytes 135200 | tf_op jit(solution)/shard_map/ppermute | solution.py:369
  99.1 3.2 %collective-permute-start.31 = (bf16[656,128]{1,0:T(8,128)(2,1)S(1)}, bf16[656,128]{1,0:T(8,128)(2,1)S(1)}, u32[]{:S(2)}, u32[]{:S(2)}) collective-permute-start(bf16[656,128]{1,0:T(8,128)(2,1)S(1)} %pair.11.part_a), channel_id=1, source_target_pairs={{0,96},{16,112},{32,64},{48,80},{64,32},{80,48},{96,0},{112,16},{1... | collective-permute-start | bytes 503816 | tf_op jit(solution)/shard_map/ppermute | solution.py:369
  102.3 4.9 %weight.12.refs_4_ = bf16[2048,1024]{1,0:T(8,128)(2,1)S(1)} custom-call(s32[1]{0:T(128)} %bitcast.4.plane, s32[8,128]{1,0:T(8,128)S(1)} %get-tuple-element.234.place), custom_call_target="tpu_custom_call" | custom-call | flops 41943040 | bytes 4194304 | tf_op jit(solution)/shard_map/weight/pallas_call | solution.py:211
  114.1 3.8 %collective-permute-done.32.refs_1_ = bf16[528,128]{1,0:T(8,128)(2,1)S(1)} collective-permute-done((bf16[528,128]{1,0:T(8,128)(2,1)S(1)}, bf16[528,128]{1,0:T(8,128)(2,1)S(1)}, u32[]{:S(2)}, u32[]{:S(2)}) %collective-permute-start.32) | collective-permute-done | bytes 135200 | tf_op jit(solution)/shard_map/ppermute | solution.py:369
  121.8 3.2 %collective-permute-start.36 = (bf16[656,128]{1,0:T(8,128)(2,1)S(1)}, bf16[656,128]{1,0:T(8,128)(2,1)S(1)}, u32[]{:S(2)}, u32[]{:S(2)}) collective-permute-start(bf16[656,128]{1,0:T(8,128)(2,1)S(1)} %pair.12.part_a), channel_id=1, source_target_pairs={{0,2},{1,3},{2,0},{3,1},{4,6},{5,7},{6,4},{7,5},{8,10},{9,11},{10,... | collective-permute-start | bytes 503816 | tf_op jit(solution)/shard_map/ppermute | solution.py:369
  126.2 4.9 %weight.13.refs_4_ = bf16[2048,1024]{1,0:T(8,128)(2,1)S(1)} custom-call(s32[1]{0:T(128)} %bitcast.4.plane, s32[8,128]{1,0:T(8,128)S(1)} %get-tuple-element.234.place), custom_call_target="tpu_custom_call" | custom-call | flops 41943040 | bytes 4194304 | tf_op jit(solution)/shard_map/weight/pallas_call | solution.py:211
  131.1 2.7 %collective-permute-done.37.part_c = bf16[656,128]{1,0:T(8,128)(2,1)S(1)} collective-permute-done((bf16[656,128]{1,0:T(8,128)(2,1)S(1)}, bf16[656,128]{1,0:T(8,128)(2,1)S(1)}, u32[]{:S(2)}, u32[]{:S(2)}) %collective-permute-start.37) | collective-permute-done | bytes 167968 | tf_op jit(solution)/shard_map/ppermute | solution.py:369
  138.1 3.8 %collective-permute-done.39.refs_1_ = bf16[528,128]{1,0:T(8,128)(2,1)S(1)} collective-permute-done((bf16[528,128]{1,0:T(8,128)(2,1)S(1)}, bf16[528,128]{1,0:T(8,128)(2,1)S(1)}, u32[]{:S(2)}, u32[]{:S(2)}) %collective-permute-start.39) | collective-permute-done | bytes 135200 | tf_op jit(solution)/shard_map/ppermute | solution.py:369
  146.5 3.2 %collective-permute-start.45 = (bf16[656,128]{1,0:T(8,128)(2,1)S(1)}, bf16[656,128]{1,0:T(8,128)(2,1)S(1)}, u32[]{:S(2)}, u32[]{:S(2)}) collective-permute-start(bf16[656,128]{1,0:T(8,128)(2,1)S(1)} %pair.13.part_a), channel_id=1, source_target_pairs={{0,96},{16,112},{32,64},{48,80},{64,32},{80,48},{96,0},{112,16},{1... | collective-permute-start | bytes 503816 | tf_op jit(solution)/shard_map/ppermute | solution.py:369
  149.7 4.9 %weight.14.refs_4_ = bf16[2048,1024]{1,0:T(8,128)(2,1)S(1)} custom-call(s32[1]{0:T(128)} %bitcast.4.plane, s32[8,128]{1,0:T(8,128)S(1)} %get-tuple-element.234.place), custom_call_target="tpu_custom_call" | custom-call | flops 41943040 | bytes 4194304 | tf_op jit(solution)/shard_map/weight/pallas_call | solution.py:211
  161.5 3.8 %collective-permute-done.46.refs_1_ = bf16[528,128]{1,0:T(8,128)(2,1)S(1)} collective-permute-done((bf16[528,128]{1,0:T(8,128)(2,1)S(1)}, bf16[528,128]{1,0:T(8,128)(2,1)S(1)}, u32[]{:S(2)}, u32[]{:S(2)}) %collective-permute-start.46) | collective-permute-done | bytes 135200 | tf_op jit(solution)/shard_map/ppermute | solution.py:369
  170.1 3.2 %collective-permute-start.50 = (bf16[784,128]{1,0:T(8,128)(2,1)S(1)}, bf16[784,128]{1,0:T(8,128)(2,1)S(1)}, u32[]{:S(2)}, u32[]{:S(2)}) collective-permute-start(bf16[784,128]{1,0:T(8,128)(2,1)S(1)} %pair.14.part_a), channel_id=1, source_target_pairs={{0,2},{1,3},{2,0},{3,1},{4,6},{5,7},{6,4},{7,5},{8,10},{9,11},{10,... | collective-permute-start | bytes 602120 | tf_op jit(solution)/shard_map/ppermute | solution.py:369
  174.7 4.8 %collective-permute-done.50.part_b = bf16[784,128]{1,0:T(8,128)(2,1)S(1)} collective-permute-done((bf16[784,128]{1,0:T(8,128)(2,1)S(1)}, bf16[784,128]{1,0:T(8,128)(2,1)S(1)}, u32[]{:S(2)}, u32[]{:S(2)}) %collective-permute-start.50) | collective-permute-done | bytes 200736 | tf_op jit(solution)/shard_map/ppermute | solution.py:369
  179.5 3.8 %collective-permute-done.51.part_c = bf16[784,128]{1,0:T(8,128)(2,1)S(1)} collective-permute-done((bf16[784,128]{1,0:T(8,128)(2,1)S(1)}, bf16[784,128]{1,0:T(8,128)(2,1)S(1)}, u32[]{:S(2)}, u32[]{:S(2)}) %collective-permute-start.51) | collective-permute-done | bytes 200736 | tf_op jit(solution)/shard_map/ppermute | solution.py:369
  187.9 4.9 %weight.15.refs_4_ = bf16[2048,1024]{1,0:T(8,128)(2,1)S(1)} custom-call(s32[1]{0:T(128)} %bitcast.4.plane, s32[8,128]{1,0:T(8,128)S(1)} %get-tuple-element.234.place), custom_call_target="tpu_custom_call" | custom-call | flops 41943040 | bytes 4194304 | tf_op jit(solution)/shard_map/weight/pallas_call | solution.py:211
  199.0 3.0 %collective-permute-start.59 = (bf16[784,128]{1,0:T(8,128)(2,1)S(1)}, bf16[784,128]{1,0:T(8,128)(2,1)S(1)}, u32[]{:S(2)}, u32[]{:S(2)}) collective-permute-start(bf16[784,128]{1,0:T(8,128)(2,1)S(1)} %pair.15.part_a), channel_id=1, source_target_pairs={{0,96},{16,112},{32,64},{48,80},{64,32},{80,48},{96,0},{112,16},{1... | collective-permute-start | bytes 602120 | tf_op jit(solution)/shard_map/ppermute | solution.py:369
  202.0 5.3 %collective-permute-done.57.part_b = bf16[784,128]{1,0:T(8,128)(2,1)S(1)} collective-permute-done((bf16[784,128]{1,0:T(8,128)(2,1)S(1)}, bf16[784,128]{1,0:T(8,128)(2,1)S(1)}, u32[]{:S(2)}, u32[]{:S(2)}) %collective-permute-start.57) | collective-permute-done | bytes 200736 | tf_op jit(solution)/shard_map/ppermute | solution.py:369
  215.6 2.9 %collective-permute-start.62 = (bf16[144,128]{1,0:T(8,128)(2,1)S(1)}, bf16[144,128]{1,0:T(8,128)(2,1)S(1)}, u32[]{:S(2)}, u32[]{:S(2)}) collective-permute-start(bf16[144,128]{1,0:T(8,128)(2,1)S(1)} %get-tuple-element.249), channel_id=1, source_target_pairs={{0,2},{1,3},{2,0},{3,1},{4,6},{5,7},{6,4},{7,5},{8,10},{9,11},{10,... | collective-permute-start | bytes 110600 | tf_op jit(solution)/shard_map/ppermute | solution.py:369
  224.0 3.1 %collective-permute-start.65 = (bf16[144,128]{1,0:T(8,128)(2,1)S(1)}, bf16[144,128]{1,0:T(8,128)(2,1)S(1)}, u32[]{:S(2)}, u32[]{:S(2)}) collective-permute-start(bf16[144,128]{1,0:T(8,128)(2,1)S(1)} %add_convert_fusion), channel_id=1, source_target_pairs={{0,8},{1,9},{2,10},{3,11},{4,12},{5,13},{6,14},{7,15},{8,0},{9,1},... | collective-permute-start | bytes 110600 | tf_op jit(solution)/shard_map/ppermute | solution.py:369
  (169 shorter events, 109.2 us)
Async XLA Ops:
  14.1 9.8 %collective-permute-start.4 = (f32[4,1,128]{2,1,0:T(1,128)S(1)}, f32[4,1,128]{2,1,0:T(1,128)S(1)}, u32[]{:S(2)}, u32[]{:S(2)}) collective-permute-start(f32[4,1,128]{2,1,0:T(1,128)S(1)} %get-tuple-element.130.refs_0_), channel_id=1, source_target_pairs={{0,8},{1,9},{2,10},{3,11},{4,12},{5,13},{6,14},{7,15},{8,0},{9,1},... | collective-permute-start | bytes 6152 | tf_op jit(solution)/shard_map/ppermute | solution.py:369
  26.1 11.1 %collective-permute-start.10 = (bf16[672,128]{1,0:T(8,128)(2,1)S(1)}, bf16[672,128]{1,0:T(8,128)(2,1)S(1)}, u32[]{:S(2)}, u32[]{:S(2)}) collective-permute-start(bf16[672,128]{1,0:T(8,128)(2,1)S(1)} %pair.8.part_a), channel_id=1, source_target_pairs={{0,3},{1,2},{2,1},{3,0},{4,7},{5,6},{6,5},{7,4},{8,11},{9,10},{10,... | collective-permute-start | bytes 516104 | tf_op jit(solution)/shard_map/ppermute | solution.py:369
  29.2 8.8 %collective-permute-start.8 = (bf16[672,128]{1,0:T(8,128)(2,1)S(1)}, bf16[672,128]{1,0:T(8,128)(2,1)S(1)}, u32[]{:S(2)}, u32[]{:S(2)}) collective-permute-start(bf16[672,128]{1,0:T(8,128)(2,1)S(1)} %pair.8.part_a), channel_id=1, source_target_pairs={{0,2},{1,3},{2,0},{3,1},{4,6},{5,7},{6,4},{7,5},{8,10},{9,11},{10,... | collective-permute-start | bytes 516104 | tf_op jit(solution)/shard_map/ppermute | solution.py:369
  29.8 8.5 %collective-permute-start.9 = (bf16[672,128]{1,0:T(8,128)(2,1)S(1)}, bf16[672,128]{1,0:T(8,128)(2,1)S(1)}, u32[]{:S(2)}, u32[]{:S(2)}) collective-permute-start(bf16[672,128]{1,0:T(8,128)(2,1)S(1)} %pair.8.part_a), channel_id=1, source_target_pairs={{0,1},{1,0},{2,3},{3,2},{4,5},{5,4},{6,7},{7,6},{8,9},{9,8},{10,11... | collective-permute-start | bytes 516104 | tf_op jit(solution)/shard_map/ppermute | solution.py:369
  50.8 9.0 %collective-permute-start.15 = (bf16[656,128]{1,0:T(8,128)(2,1)S(1)}, bf16[656,128]{1,0:T(8,128)(2,1)S(1)}, u32[]{:S(2)}, u32[]{:S(2)}) collective-permute-start(bf16[656,128]{1,0:T(8,128)(2,1)S(1)} %pair.9.part_a), channel_id=1, source_target_pairs={{0,64},{16,80},{32,96},{48,112},{64,0},{80,16},{96,32},{112,48},{1... | collective-permute-start | bytes 503816 | tf_op jit(solution)/shard_map/ppermute | solution.py:369
  51.7 8.5 %collective-permute-start.16 = (bf16[656,128]{1,0:T(8,128)(2,1)S(1)}, bf16[656,128]{1,0:T(8,128)(2,1)S(1)}, u32[]{:S(2)}, u32[]{:S(2)}) collective-permute-start(bf16[656,128]{1,0:T(8,128)(2,1)S(1)} %pair.9.part_a), channel_id=1, source_target_pairs={{0,32},{16,48},{32,0},{48,16},{64,96},{80,112},{96,64},{112,80},{1... | collective-permute-start | bytes 503816 | tf_op jit(solution)/shard_map/ppermute | solution.py:369
  52.3 10.0 %collective-permute-start.17 = (bf16[656,128]{1,0:T(8,128)(2,1)S(1)}, bf16[656,128]{1,0:T(8,128)(2,1)S(1)}, u32[]{:S(2)}, u32[]{:S(2)}) collective-permute-start(bf16[656,128]{1,0:T(8,128)(2,1)S(1)} %pair.9.part_a), channel_id=1, source_target_pairs={{0,96},{16,112},{32,64},{48,80},{64,32},{80,48},{96,0},{112,16},{1... | collective-permute-start | bytes 503816 | tf_op jit(solution)/shard_map/ppermute | solution.py:369
  62.6 8.0 %collective-permute-start.18 = (bf16[528,128]{1,0:T(8,128)(2,1)S(1)}, bf16[528,128]{1,0:T(8,128)(2,1)S(1)}, u32[]{:S(2)}, u32[]{:S(2)}) collective-permute-start(bf16[528,128]{1,0:T(8,128)(2,1)S(1)} %get-tuple-element.153.refs_0_), channel_id=1, source_target_pairs={{0,8},{1,9},{2,10},{3,11},{4,12},{5,13},{6,14},{7,15},{8,0},{9,1},... | collective-permute-start | bytes 405512 | tf_op jit(solution)/shard_map/ppermute | solution.py:369
  74.6 9.0 %collective-permute-start.22 = (bf16[656,128]{1,0:T(8,128)(2,1)S(1)}, bf16[656,128]{1,0:T(8,128)(2,1)S(1)}, u32[]{:S(2)}, u32[]{:S(2)}) collective-permute-start(bf16[656,128]{1,0:T(8,128)(2,1)S(1)} %pair.10.part_a), channel_id=1, source_target_pairs={{0,2},{1,3},{2,0},{3,1},{4,6},{5,7},{6,4},{7,5},{8,10},{9,11},{10,... | collective-permute-start | bytes 503816 | tf_op jit(solution)/shard_map/ppermute | solution.py:369
  77.7 8.6 %collective-permute-start.23 = (bf16[656,128]{1,0:T(8,128)(2,1)S(1)}, bf16[656,128]{1,0:T(8,128)(2,1)S(1)}, u32[]{:S(2)}, u32[]{:S(2)}) collective-permute-start(bf16[656,128]{1,0:T(8,128)(2,1)S(1)} %pair.10.part_a), channel_id=1, source_target_pairs={{0,1},{1,0},{2,3},{3,2},{4,5},{5,4},{6,7},{7,6},{8,9},{9,8},{10,11... | collective-permute-start | bytes 503816 | tf_op jit(solution)/shard_map/ppermute | solution.py:369
  78.3 8.0 %collective-permute-start.24 = (bf16[656,128]{1,0:T(8,128)(2,1)S(1)}, bf16[656,128]{1,0:T(8,128)(2,1)S(1)}, u32[]{:S(2)}, u32[]{:S(2)}) collective-permute-start(bf16[656,128]{1,0:T(8,128)(2,1)S(1)} %pair.10.part_a), channel_id=1, source_target_pairs={{0,3},{1,2},{2,1},{3,0},{4,7},{5,6},{6,5},{7,4},{8,11},{9,10},{10,... | collective-permute-start | bytes 503816 | tf_op jit(solution)/shard_map/ppermute | solution.py:369
  86.5 7.9 %collective-permute-start.25 = (bf16[528,128]{1,0:T(8,128)(2,1)S(1)}, bf16[528,128]{1,0:T(8,128)(2,1)S(1)}, u32[]{:S(2)}, u32[]{:S(2)}) collective-permute-start(bf16[528,128]{1,0:T(8,128)(2,1)S(1)} %get-tuple-element.165.refs_0_), channel_id=1, source_target_pairs={{0,8},{1,9},{2,10},{3,11},{4,12},{5,13},{6,14},{7,15},{8,0},{9,1},... | collective-permute-start | bytes 405512 | tf_op jit(solution)/shard_map/ppermute | solution.py:369
  98.1 9.0 %collective-permute-start.29 = (bf16[656,128]{1,0:T(8,128)(2,1)S(1)}, bf16[656,128]{1,0:T(8,128)(2,1)S(1)}, u32[]{:S(2)}, u32[]{:S(2)}) collective-permute-start(bf16[656,128]{1,0:T(8,128)(2,1)S(1)} %pair.11.part_a), channel_id=1, source_target_pairs={{0,64},{16,80},{32,96},{48,112},{64,0},{80,16},{96,32},{112,48},{1... | collective-permute-start | bytes 503816 | tf_op jit(solution)/shard_map/ppermute | solution.py:369
  99.0 8.2 %collective-permute-start.30 = (bf16[656,128]{1,0:T(8,128)(2,1)S(1)}, bf16[656,128]{1,0:T(8,128)(2,1)S(1)}, u32[]{:S(2)}, u32[]{:S(2)}) collective-permute-start(bf16[656,128]{1,0:T(8,128)(2,1)S(1)} %pair.11.part_a), channel_id=1, source_target_pairs={{0,32},{16,48},{32,0},{48,16},{64,96},{80,112},{96,64},{112,80},{1... | collective-permute-start | bytes 503816 | tf_op jit(solution)/shard_map/ppermute | solution.py:369
  99.1 10.5 %collective-permute-start.31 = (bf16[656,128]{1,0:T(8,128)(2,1)S(1)}, bf16[656,128]{1,0:T(8,128)(2,1)S(1)}, u32[]{:S(2)}, u32[]{:S(2)}) collective-permute-start(bf16[656,128]{1,0:T(8,128)(2,1)S(1)} %pair.11.part_a), channel_id=1, source_target_pairs={{0,96},{16,112},{32,64},{48,80},{64,32},{80,48},{96,0},{112,16},{1... | collective-permute-start | bytes 503816 | tf_op jit(solution)/shard_map/ppermute | solution.py:369
  109.9 8.0 %collective-permute-start.32 = (bf16[528,128]{1,0:T(8,128)(2,1)S(1)}, bf16[528,128]{1,0:T(8,128)(2,1)S(1)}, u32[]{:S(2)}, u32[]{:S(2)}) collective-permute-start(bf16[528,128]{1,0:T(8,128)(2,1)S(1)} %get-tuple-element.175.refs_0_), channel_id=1, source_target_pairs={{0,8},{1,9},{2,10},{3,11},{4,12},{5,13},{6,14},{7,15},{8,0},{9,1},... | collective-permute-start | bytes 405512 | tf_op jit(solution)/shard_map/ppermute | solution.py:369
  121.8 9.2 %collective-permute-start.36 = (bf16[656,128]{1,0:T(8,128)(2,1)S(1)}, bf16[656,128]{1,0:T(8,128)(2,1)S(1)}, u32[]{:S(2)}, u32[]{:S(2)}) collective-permute-start(bf16[656,128]{1,0:T(8,128)(2,1)S(1)} %pair.12.part_a), channel_id=1, source_target_pairs={{0,2},{1,3},{2,0},{3,1},{4,6},{5,7},{6,4},{7,5},{8,10},{9,11},{10,... | collective-permute-start | bytes 503816 | tf_op jit(solution)/shard_map/ppermute | solution.py:369
  125.1 8.6 %collective-permute-start.37 = (bf16[656,128]{1,0:T(8,128)(2,1)S(1)}, bf16[656,128]{1,0:T(8,128)(2,1)S(1)}, u32[]{:S(2)}, u32[]{:S(2)}) collective-permute-start(bf16[656,128]{1,0:T(8,128)(2,1)S(1)} %pair.12.part_a), channel_id=1, source_target_pairs={{0,1},{1,0},{2,3},{3,2},{4,5},{5,4},{6,7},{7,6},{8,9},{9,8},{10,11... | collective-permute-start | bytes 503816 | tf_op jit(solution)/shard_map/ppermute | solution.py:369
  125.8 8.0 %collective-permute-start.38 = (bf16[656,128]{1,0:T(8,128)(2,1)S(1)}, bf16[656,128]{1,0:T(8,128)(2,1)S(1)}, u32[]{:S(2)}, u32[]{:S(2)}) collective-permute-start(bf16[656,128]{1,0:T(8,128)(2,1)S(1)} %pair.12.part_a), channel_id=1, source_target_pairs={{0,3},{1,2},{2,1},{3,0},{4,7},{5,6},{6,5},{7,4},{8,11},{9,10},{10,... | collective-permute-start | bytes 503816 | tf_op jit(solution)/shard_map/ppermute | solution.py:369
  145.6 9.0 %collective-permute-start.43 = (bf16[656,128]{1,0:T(8,128)(2,1)S(1)}, bf16[656,128]{1,0:T(8,128)(2,1)S(1)}, u32[]{:S(2)}, u32[]{:S(2)}) collective-permute-start(bf16[656,128]{1,0:T(8,128)(2,1)S(1)} %pair.13.part_a), channel_id=1, source_target_pairs={{0,64},{16,80},{32,96},{48,112},{64,0},{80,16},{96,32},{112,48},{1... | collective-permute-start | bytes 503816 | tf_op jit(solution)/shard_map/ppermute | solution.py:369
  146.4 8.2 %collective-permute-start.44 = (bf16[656,128]{1,0:T(8,128)(2,1)S(1)}, bf16[656,128]{1,0:T(8,128)(2,1)S(1)}, u32[]{:S(2)}, u32[]{:S(2)}) collective-permute-start(bf16[656,128]{1,0:T(8,128)(2,1)S(1)} %pair.13.part_a), channel_id=1, source_target_pairs={{0,32},{16,48},{32,0},{48,16},{64,96},{80,112},{96,64},{112,80},{1... | collective-permute-start | bytes 503816 | tf_op jit(solution)/shard_map/ppermute | solution.py:369
  146.5 10.6 %collective-permute-start.45 = (bf16[656,128]{1,0:T(8,128)(2,1)S(1)}, bf16[656,128]{1,0:T(8,128)(2,1)S(1)}, u32[]{:S(2)}, u32[]{:S(2)}) collective-permute-start(bf16[656,128]{1,0:T(8,128)(2,1)S(1)} %pair.13.part_a), channel_id=1, source_target_pairs={{0,96},{16,112},{32,64},{48,80},{64,32},{80,48},{96,0},{112,16},{1... | collective-permute-start | bytes 503816 | tf_op jit(solution)/shard_map/ppermute | solution.py:369
  157.3 8.0 %collective-permute-start.46 = (bf16[528,128]{1,0:T(8,128)(2,1)S(1)}, bf16[528,128]{1,0:T(8,128)(2,1)S(1)}, u32[]{:S(2)}, u32[]{:S(2)}) collective-permute-start(bf16[528,128]{1,0:T(8,128)(2,1)S(1)} %get-tuple-element.207.refs_0_), channel_id=1, source_target_pairs={{0,8},{1,9},{2,10},{3,11},{4,12},{5,13},{6,14},{7,15},{8,0},{9,1},... | collective-permute-start | bytes 405512 | tf_op jit(solution)/shard_map/ppermute | solution.py:369
  170.1 9.4 %collective-permute-start.50 = (bf16[784,128]{1,0:T(8,128)(2,1)S(1)}, bf16[784,128]{1,0:T(8,128)(2,1)S(1)}, u32[]{:S(2)}, u32[]{:S(2)}) collective-permute-start(bf16[784,128]{1,0:T(8,128)(2,1)S(1)} %pair.14.part_a), channel_id=1, source_target_pairs={{0,2},{1,3},{2,0},{3,1},{4,6},{5,7},{6,4},{7,5},{8,10},{9,11},{10,... | collective-permute-start | bytes 602120 | tf_op jit(solution)/shard_map/ppermute | solution.py:369
  173.4 10.0 %collective-permute-start.51 = (bf16[784,128]{1,0:T(8,128)(2,1)S(1)}, bf16[784,128]{1,0:T(8,128)(2,1)S(1)}, u32[]{:S(2)}, u32[]{:S(2)}) collective-permute-start(bf16[784,128]{1,0:T(8,128)(2,1)S(1)} %pair.14.part_a), channel_id=1, source_target_pairs={{0,1},{1,0},{2,3},{3,2},{4,5},{5,4},{6,7},{7,6},{8,9},{9,8},{10,11... | collective-permute-start | bytes 602120 | tf_op jit(solution)/shard_map/ppermute | solution.py:369
  174.0 9.4 %collective-permute-start.52 = (bf16[784,128]{1,0:T(8,128)(2,1)S(1)}, bf16[784,128]{1,0:T(8,128)(2,1)S(1)}, u32[]{:S(2)}, u32[]{:S(2)}) collective-permute-start(bf16[784,128]{1,0:T(8,128)(2,1)S(1)} %pair.14.part_a), channel_id=1, source_target_pairs={{0,3},{1,2},{2,1},{3,0},{4,7},{5,6},{6,5},{7,4},{8,11},{9,10},{10,... | collective-permute-start | bytes 602120 | tf_op jit(solution)/shard_map/ppermute | solution.py:369
  183.7 9.5 %collective-permute-start.53 = (bf16[784,128]{1,0:T(8,128)(2,1)S(1)}, bf16[784,128]{1,0:T(8,128)(2,1)S(1)}, u32[]{:S(2)}, u32[]{:S(2)}) collective-permute-start(bf16[784,128]{1,0:T(8,128)(2,1)S(1)} %get-tuple-element.230.refs_0_.part_a), channel_id=1, source_target_pairs={{0,8},{1,9},{2,10},{3,11},{4,12},{5,13},{6,14},{7,15},{8,0},{9,1},... | collective-permute-start | bytes 602120 | tf_op jit(solution)/shard_map/ppermute | solution.py:369
  185.5 9.5 %collective-permute-start.54 = (bf16[784,128]{1,0:T(8,128)(2,1)S(1)}, bf16[784,128]{1,0:T(8,128)(2,1)S(1)}, u32[]{:S(2)}, u32[]{:S(2)}) collective-permute-start(bf16[784,128]{1,0:T(8,128)(2,1)S(1)} %get-tuple-element.230.refs_0_.part_a), channel_id=1, source_target_pairs={{0,4},{1,5},{2,6},{3,7},{4,0},{5,1},{6,2},{7,3},{8,12},{9,13},{10,... | collective-permute-start | bytes 602120 | tf_op jit(solution)/shard_map/ppermute | solution.py:369
  186.5 9.3 %collective-permute-start.55 = (bf16[784,128]{1,0:T(8,128)(2,1)S(1)}, bf16[784,128]{1,0:T(8,128)(2,1)S(1)}, u32[]{:S(2)}, u32[]{:S(2)}) collective-permute-start(bf16[784,128]{1,0:T(8,128)(2,1)S(1)} %get-tuple-element.230.refs_0_.part_a), channel_id=1, source_target_pairs={{0,12},{1,13},{2,14},{3,15},{4,8},{5,9},{6,10},{7,11},{8,4},{9,5},... | collective-permute-start | bytes 602120 | tf_op jit(solution)/shard_map/ppermute | solution.py:369
  197.8 9.5 %collective-permute-start.57 = (bf16[784,128]{1,0:T(8,128)(2,1)S(1)}, bf16[784,128]{1,0:T(8,128)(2,1)S(1)}, u32[]{:S(2)}, u32[]{:S(2)}) collective-permute-start(bf16[784,128]{1,0:T(8,128)(2,1)S(1)} %pair.15.part_a), channel_id=1, source_target_pairs={{0,64},{16,80},{32,96},{48,112},{64,0},{80,16},{96,32},{112,48},{1... | collective-permute-start | bytes 602120 | tf_op jit(solution)/shard_map/ppermute | solution.py:369
  198.7 9.6 %collective-permute-start.58 = (bf16[784,128]{1,0:T(8,128)(2,1)S(1)}, bf16[784,128]{1,0:T(8,128)(2,1)S(1)}, u32[]{:S(2)}, u32[]{:S(2)}) collective-permute-start(bf16[784,128]{1,0:T(8,128)(2,1)S(1)} %pair.15.part_a), channel_id=1, source_target_pairs={{0,32},{16,48},{32,0},{48,16},{64,96},{80,112},{96,64},{112,80},{1... | collective-permute-start | bytes 602120 | tf_op jit(solution)/shard_map/ppermute | solution.py:369
  199.0 11.7 %collective-permute-start.59 = (bf16[784,128]{1,0:T(8,128)(2,1)S(1)}, bf16[784,128]{1,0:T(8,128)(2,1)S(1)}, u32[]{:S(2)}, u32[]{:S(2)}) collective-permute-start(bf16[784,128]{1,0:T(8,128)(2,1)S(1)} %pair.15.part_a), channel_id=1, source_target_pairs={{0,96},{16,112},{32,64},{48,80},{64,32},{80,48},{96,0},{112,16},{1... | collective-permute-start | bytes 602120 | tf_op jit(solution)/shard_map/ppermute | solution.py:369
  (37 other events, 175.8 us)

commit v5 on v4

--- a/solution.py
+++ b/solution.py
@@ -96,16 +96,24 @@
     return lax.optimization_barrier((value, *others))[0]
 
 
-def pack_kernel(seed, student_seed, plane, gain, student_gain, out):
+def pack_kernel(seed, student_seed, plane, gain_hbm, student_gain_hbm, out, gain, student_gain, sems):
+    start = pl.multiple_of(plane[0] * STEP_Q, STEP_Q)
+    copies = [
+        pltpu.make_async_copy(gain_hbm, gain, sems.at[0]),
+        pltpu.make_async_copy(student_gain_hbm.at[:, pl.ds(start, STEP_Q)], student_gain, sems.at[1]),
+    ]
+    for copy in copies:
+        copy.start()
+    for copy in copies:
+        copy.wait()
     rows = [gain[:, index * PIECE : (index + 1) * PIECE] for index in range(SEG)]
     for value in (seed[0], student_seed[0]):
         for shift in (16, 8, 0):
             byte = jnp.bitwise_and(lax.shift_right_logical(value, jnp.int32(shift)), jnp.int32(255))
             rows.append(jnp.full((1, PIECE), byte, jnp.int32).astype(F32).astype(BF))
     rows += [jnp.zeros((1, PIECE), BF)] * 2
-    start = plane[0] * STEP_Q
     for index in range(4 * SEG):
-        rows.append(student_gain[:, pl.ds(pl.multiple_of(start + index * PIECE, PIECE), PIECE)])
+        rows.append(student_gain[:, index * PIECE : (index + 1) * PIECE])
     for first in range(0, FACTS, 16):
         out[first : first + 16, :] = jnp.concatenate([row.astype(F32) for row in rows[first : first + 16]], axis=0).astype(BF)
 
@@ -119,7 +127,7 @@
     parts, (along_z_out, along_y_out, even_out, place_out, student_out) = refs[:4], refs[4:9]
     fold_place_out, fold_gain_out, up_place_out, up_gain_out, facts = refs[9:]
     core, column, row, plane = place[1], place[2], place[3], place[4]
-    for partner, part in zip(PARTNERS, parts):
+    for partner, part in zip(SHORT, parts):
         facts[pl.ds(2 * jnp.bitwise_xor(column, partner), 2)] = part[...].astype(F32)
 
     def seed(layer, first):
@@ -175,12 +183,12 @@
 
 
 def first_scale_kernel(embedded, tile, *refs):
-    gains, outs = refs[:4], refs[4:]
-    for partner in range(4):
+    gains, outs = dict(zip(SHORT, refs[:4])), refs[4:]
+    for slot, partner in enumerate(PARTNERS):
         for digit in range(4):
             rows = slice(digit * TOK, (digit + 1) * TOK)
-            outs[partner][rows, :] = (embedded[partner, rows, :].astype(F32) * gains[partner][digit]).astype(BF)
-        outs[partner][STATE:, :] = tile[...] if partner == 0 else jnp.zeros((16, TOK), BF)
+            outs[slot][rows, :] = (embedded[slot, rows, :].astype(F32) * gains[partner][digit]).astype(BF)
+        outs[slot][STATE:, :] = tile[...] if slot == 0 else jnp.zeros((16, TOK), BF)
 
 
 def weight_kernel(layer, plane, place, out):
@@ -194,7 +202,7 @@
     def step(index, carry):
         piece = index // 2
         slot = piece // 4
-        partner = jnp.where(slot == 1, PARTNERS[1], jnp.where(slot == 2, PARTNERS[2], slot))
+        partner = jnp.where(slot == 0, 0, jnp.where(slot == 1, PARTNERS[1], jnp.where(slot == 2, PARTNERS[2], PARTNERS[3])))
         first = jnp.bitwise_xor(plane[0], partner) * (STEP_Q * 16411) + (piece % 4) * (row_step * 16411) + (index % 2) * (chunk * 16411)
         start = pl.multiple_of(index * chunk, chunk)
         out[pl.ds(start, chunk), :] = hashed(base + first, math.sqrt(3.0 / D)).astype(BF)
@@ -257,8 +265,9 @@
 
 
 def pre_kernel(part_a, part_b, part_c, part_d, out):
-    wide = [part[GATHER + TOK :, :].astype(F32) for part in (part_a, part_b, part_c, part_d)]
-    out[...] = (wide[0] + wide[2]) + (wide[1] + wide[3])
+    parts = zip(PARTNERS, (part_a, part_b, part_c, part_d))
+    wide = {partner: part[GATHER + TOK :, :].astype(F32) for partner, part in parts}
+    out[...] = (wide[0] + wide[1]) + (wide[2] + wide[3])
 
 
 def keep_kernel(digit, part_a, part_b, part_c, part_d, out):
@@ -291,8 +300,8 @@
     placed(digit, parts, stream_out)
 
     def total(rows):
-        wide = [part[rows, :].astype(F32) for part in parts]
-        return (wide[0] + wide[2]) + (wide[1] + wide[3])
+        wide = {partner: part[rows, :].astype(F32) for partner, part in zip(PARTNERS, parts)}
+        return (wide[0] + wide[1]) + (wide[2] + wide[3])
 
     if not following:
         odd_out[...] = stream_out[...]
@@ -358,21 +367,28 @@
 }
 
 
-PARTNERS = (0, 2, 1, 3)
-
-
-def exchange(values, physical):
+PARTNERS = (0, 3, 2, 1)
+SHORT = (0, 3, 2, 1)
+
+
+def exchange(values, physical, order=PARTNERS):
     axis, step = ALONG[physical]
     size = SEG if axis == "segment" else MP
     values = values if isinstance(values, (list, tuple)) else [values] * 4
     return [values[0]] + [
-        lax.ppermute(values[k], axis, [(i, i ^ (k * step)) for i in range(size)]) for k in PARTNERS[1:]
+        lax.ppermute(values[k], axis, [(i, i ^ (k * step)) for i in range(size)]) for k in order[1:]
     ]
 
 
-def summed_along(value, physical):
-    own, second, first, third = (part.astype(F32) for part in exchange(value.astype(BF), physical))
-    return (own + first) + (second + third)
+def sum_kernel(*refs):
+    parts, out = dict(zip(SHORT, refs[:4])), refs[4]
+    own, first, second, third = (parts[k][...].astype(F32) for k in range(4))
+    out[...] = ((own + first) + (second + third)).astype(out.dtype)
+
+
+def summed_along(value, physical, dtype):
+    parts = exchange(value, physical, SHORT)
+    return call(sum_kernel, "sum", sds(value.shape, dtype), [VMEM] * 4)(*parts)
 
 
 def ternary_base(place):
@@ -410,10 +426,16 @@
     other_out[...] = jnp.where(first, totals[1], totals[0]).astype(BF)
 
 
+def down_weight_kernel(place, out):
+    base = ternary_base(place) + R
+    for index in range(SEG):
+        made = ternary(base + index * PIECE * 16411, math.sqrt(1.5 / R))
+        out[index * PIECE : (index + 1) * PIECE, :] = made.astype(BF)
+
+
 def student_error_kernel(
-    segment, core, place, mine, near, far, pre, last_pre, mean, last_mean, back_out, scaled_out, squared_out, pre_out
+    segment, core, down_weights, mine, near, far, pre, last_pre, mean, last_mean, back_out, scaled_out, squared_out, pre_out
 ):
-    base = ternary_base(place) + R
     last = segment[0] == SEG - 1
     scale = lax.rsqrt(jnp.where(last, last_mean[...], mean[...]) + EPSILON)
     rectified = jnp.maximum(jnp.where(last, last_pre[...], pre[...]) * scale, 0.0)
@@ -423,7 +445,7 @@
     back = jnp.zeros((TOK, R), F32)
     squares = jnp.zeros((TOK, PIECE), F32)
     for index in range(SEG):
-        down_weight = ternary(base + index * PIECE * 16411, math.sqrt(1.5 / R)).astype(BF)
+        down_weight = down_weights[index * PIECE : (index + 1) * PIECE, :]
         student = lax.dot_general(squared, down_weight, (((1,), (1,)), ((), ())), preferred_element_type=F32)
         given, target = pieces_of(core, index, mine, near, far)
         error = given + student - target
@@ -444,13 +466,13 @@
         columns = slice(index * PIECE, (index + 1) * PIECE)
         given, _ = pieces_of(core, index, mine, near, far)
         normed = given * scale * gain[:, columns].astype(F32)
-        normed_out[:, columns] = normed.astype(BF)
+        normed_out[columns, :] = jnp.transpose(normed).astype(BF)
     down_out[...] = lax.dot_general(scaled[...], squared[...], OVER_TOKENS, preferred_element_type=F32)
 
 
 def student_grad_kernel(normed, rectified, back, up_out, loss_out):
     back_pre = (back[:TOK, :] * 2.0 * rectified[...]).astype(BF)
-    up_out[...] = lax.dot_general(normed[...], back_pre, OVER_TOKENS, preferred_element_type=F32)
+    up_out[...] = jnp.dot(normed[...], back_pre, preferred_element_type=F32)
     total = jnp.sum(jnp.sum(back[TOK:, :], axis=0, keepdims=True), axis=1, keepdims=True)
     loss_out[...] = total * np.float32(1.0 / (TOK * D))
 
@@ -466,13 +488,16 @@
     state_shape = sds((STATE, PIECE), BF)
     gain_shape = sds((4, 1, PIECE), F32)
 
-    facts = call(pack_kernel, "pack", sds((FACTS, PIECE), BF), [SMEM] * 3 + [VMEM] * 2)(
+    pack_scratch = (pltpu.VMEM((1, WIDTH), BF), pltpu.VMEM((1, STEP_Q), BF), pltpu.SemaphoreType.DMA((2,)))
+    facts = call(
+        pack_kernel, "pack", sds((FACTS, PIECE), BF), [SMEM] * 3 + [HBM] * 2, scratch=pack_scratch
+    )(
         teacher_seeds, student_seeds, plane, teacher_gain, student_gain
     )
     facts = call(chip_kernel, "chip", sds((2, FACTS, PIECE), BF), [SMEM, VMEM, VMEM])(
         core, facts, lax.ppermute(facts, "segment", CORE)
     )
-    facts = exchange(facts, "x")
+    facts = exchange(facts, "x", SHORT)
     embedded, tile = call(
         embed_kernel, "embed", (sds((4, STATE, PIECE), BF), sds((16, TOK), BF)), [SMEM, VMEM]
     )(place, token_ids.reshape(TOK, 1))
@@ -484,7 +509,7 @@
         [SMEM] * 2 + [VMEM] * 4,
         scratch=(pltpu.VMEM((SEG, FACTS, PIECE), F32),),
     )(place, student_seeds, *facts)
-    first_gains = exchange(first_gain, "z")
+    first_gains = exchange(first_gain, "z", SHORT)
     weight = teacher_weight(0, plane, places)
     parts = call(
         first_scale_kernel, "first_scale", tuple(sds((GATHER, PIECE), BF) for _ in range(4)), [VMEM] * 6
@@ -550,6 +575,10 @@
         elif not last:
             out.append(sds((GATHER, PIECE), BF))
         else:
+            down_weight = call(down_weight_kernel, "down_weight", sds((WIDTH, R), BF), [VMEM])(
+                gate(student_place, summed)
+            )
+            *parts, down_weight = lax.optimization_barrier((*parts, down_weight))
             out += [state_shape, sds((TOK, R), F32)]
         if layer == 0:
             out.append(sds((4, 4, 1, PIECE), F32))
@@ -576,11 +605,11 @@
         "student_error",
         (sds((TOK + 16, R), BF), sds((TOK, WIDTH), BF), sds((TOK, R), BF), sds((TOK, R), F32)),
         [SMEM] * 2 + [VMEM] * 8,
-    )(segment, core, student_place, mine, near, far, pre, last_pre, mean, last_mean)
+    )(segment, core, down_weight, mine, near, far, pre, last_pre, mean, last_mean)
     normed, grad_down = call(
-        student_down_kernel, "student_down", (sds((TOK, WIDTH), BF), sds((WIDTH, R), F32)), [SMEM] * 2 + [VMEM] * 8
+        student_down_kernel, "student_down", (sds((WIDTH, TOK), BF), sds((WIDTH, R), F32)), [SMEM] * 2 + [VMEM] * 8
     )(segment, core, mine, near, far, student_columns, mean, last_mean, scaled, squared)
-    back = summed_along(summed_along(back, "y"), "z")
+    back = summed_along(summed_along(back, "y", BF), "z", F32)
     grad_up, loss = call(
         student_grad_kernel, "student_grad", (sds((WIDTH, R), F32), sds((1, 1), F32)), [VMEM] * 3
     )(normed, rectified, back)

time: 234 us -> 229 us (0.979)
  waiting for transfers between devices: 89.8 us -> 86.4 us
    ppermute x57, waiting for transfers between devices: 80.3 us -> 76.8 us  [exchange(): lax.ppermute(values[k], axis, [(i, i ^ k * step) for i in range(size)])]
  transfers between devices with their start and end apart: 67 -> 67, of which waited for: 50 -> 44; matrix products, arithmetic and copies ran while one was open for 1% -> 1% of each run, Pallas kernels for 20% -> 20%
where the time goes in v5:
time: 229 us
  waiting for transfers between devices  86.4 us (38%)
  starting transfers between devices  81.3 us (36%)
  Pallas kernels  55.5 us (24%)
  local copies, waits for them, and re-layouts  3.07 us (1%)
  between operations  2.44 us (1%)
    ppermute x57, starting transfers between devices, exchange(): lax.ppermute(values[k], axis, [(i, i ^ k * step) for i in range(size)])  80.5 us
    ppermute x57, waiting for transfers between devices, exchange(): lax.ppermute(values[k], axis, [(i, i ^ k * step) for i in range(size)])  76.8 us
    pallas_call x8, Pallas kernels, teacher_weight(): call(body, 'weight', sds((2048, WIDTH), BF), [SMEM, VMEM], flops=20 * WEI...  39 us
    ppermute x8, waiting for transfers between devices, local(): other = lax.ppermute(other, 'segment', CORE)  6.91 us
  transfers between devices with their start and end apart: 67, of which 44 were waited for; matrix products, arithmetic and copies ran while one was open for 1% of the time, Pallas kernels for 20%

profile of v5, /device:TPU:0, one launch (start us, length us, event | category | flops | bytes accessed | tf_op | source)
XLA Modules:
  0.0 228.7 jit_solution(8966119226596580736)
XLA Ops:
  4.8 2.8 %collective-permute-start.1 = (bf16[2,48,128]{2,1,0:T(8,128)(2,1)S(1)}, bf16[2,48,128]{2,1,0:T(8,128)(2,1)S(1)}, u32[]{:S(2)}, u32[]{:S(2)}) collective-permute-start(bf16[2,48,128]{2,1,0:T(8,128)(2,1)S(1)} %chip.1.refs_0_), channel_id=1, source_target_pairs={{0,96},{16,112},{32,64},{48,80},{64,32},{80,48},{96,0},{112,16},{1... | collective-permute-start | bytes 73736 | tf_op jit(solution)/shard_map/ppermute | solution.py:379
  13.6 4.1 %collective-permute-start.4 = (f32[4,1,128]{2,1,0:T(1,128)S(1)}, f32[4,1,128]{2,1,0:T(1,128)S(1)}, u32[]{:S(2)}, u32[]{:S(2)}) collective-permute-start(f32[4,1,128]{2,1,0:T(1,128)S(1)} %get-tuple-element.136.refs_0_), channel_id=1, source_target_pairs={{0,12},{1,13},{2,14},{3,15},{4,8},{5,9},{6,10},{7,11},{8,4},{9,5},... | collective-permute-start | bytes 6152 | tf_op jit(solution)/shard_map/ppermute | solution.py:379
  18.6 4.9 %weight.8.refs_4_ = bf16[2048,1024]{1,0:T(8,128)(2,1)S(1)} custom-call(s32[1]{0:T(128)} %bitcast.4.plane, s32[8,128]{1,0:T(8,128)S(1)} %get-tuple-element.240.place), custom_call_target="tpu_custom_call" | custom-call | flops 41943040 | bytes 4194304 | tf_op jit(solution)/shard_map/weight/pallas_call | solution.py:219
  27.3 2.2 collective-permute-start.8
  30.2 4.9 %weight.9.refs_4_ = bf16[2048,1024]{1,0:T(8,128)(2,1)S(1)} custom-call(s32[1]{0:T(128)} %bitcast.4.plane, s32[8,128]{1,0:T(8,128)S(1)} %get-tuple-element.240.place), custom_call_target="tpu_custom_call" | custom-call | flops 41943040 | bytes 4194304 | tf_op jit(solution)/shard_map/weight/pallas_call | solution.py:219
  38.6 3.2 %collective-permute-start.11 = (bf16[528,128]{1,0:T(8,128)(2,1)S(1)}, bf16[528,128]{1,0:T(8,128)(2,1)S(1)}, u32[]{:S(2)}, u32[]{:S(2)}) collective-permute-start(bf16[528,128]{1,0:T(8,128)(2,1)S(1)} %get-tuple-element.148.refs_0_), channel_id=1, source_target_pairs={{0,12},{1,13},{2,14},{3,15},{4,8},{5,9},{6,10},{7,11},{8,4},{9,5},... | collective-permute-start | bytes 405512 | tf_op jit(solution)/shard_map/ppermute | solution.py:379
  42.8 4.3 %collective-permute-done.11.refs_1_ = bf16[528,128]{1,0:T(8,128)(2,1)S(1)} collective-permute-done((bf16[528,128]{1,0:T(8,128)(2,1)S(1)}, bf16[528,128]{1,0:T(8,128)(2,1)S(1)}, u32[]{:S(2)}, u32[]{:S(2)}) %collective-permute-start.11) | collective-permute-done | bytes 135200 | tf_op jit(solution)/shard_map/ppermute | solution.py:379
  47.0 2.2 collective-permute-done.12.refs_2_
  55.4 4.9 %weight.10.refs_4_ = bf16[2048,1024]{1,0:T(8,128)(2,1)S(1)} custom-call(s32[1]{0:T(128)} %bitcast.4.plane, s32[8,128]{1,0:T(8,128)S(1)} %get-tuple-element.240.place), custom_call_target="tpu_custom_call" | custom-call | flops 41943040 | bytes 4194304 | tf_op jit(solution)/shard_map/weight/pallas_call | solution.py:219
  60.2 2.2 collective-permute-done.15.part_b
  63.3 2.1 collective-permute-start.18
  67.5 4.1 %collective-permute-done.18.refs_1_ = bf16[528,128]{1,0:T(8,128)(2,1)S(1)} collective-permute-done((bf16[528,128]{1,0:T(8,128)(2,1)S(1)}, bf16[528,128]{1,0:T(8,128)(2,1)S(1)}, u32[]{:S(2)}, u32[]{:S(2)}) %collective-permute-start.18) | collective-permute-done | bytes 135200 | tf_op jit(solution)/shard_map/ppermute | solution.py:379
  78.8 4.9 %weight.11.refs_4_ = bf16[2048,1024]{1,0:T(8,128)(2,1)S(1)} custom-call(s32[1]{0:T(128)} %bitcast.4.plane, s32[8,128]{1,0:T(8,128)S(1)} %get-tuple-element.240.place), custom_call_target="tpu_custom_call" | custom-call | flops 41943040 | bytes 4194304 | tf_op jit(solution)/shard_map/weight/pallas_call | solution.py:219
  83.7 2.2 collective-permute-done.22.part_b
  90.9 4.1 %collective-permute-done.25.refs_1_ = bf16[528,128]{1,0:T(8,128)(2,1)S(1)} collective-permute-done((bf16[528,128]{1,0:T(8,128)(2,1)S(1)}, bf16[528,128]{1,0:T(8,128)(2,1)S(1)}, u32[]{:S(2)}, u32[]{:S(2)}) %collective-permute-start.25) | collective-permute-done | bytes 135200 | tf_op jit(solution)/shard_map/ppermute | solution.py:379
  102.2 4.9 %weight.12.refs_4_ = bf16[2048,1024]{1,0:T(8,128)(2,1)S(1)} custom-call(s32[1]{0:T(128)} %bitcast.4.plane, s32[8,128]{1,0:T(8,128)S(1)} %get-tuple-element.240.place), custom_call_target="tpu_custom_call" | custom-call | flops 41943040 | bytes 4194304 | tf_op jit(solution)/shard_map/weight/pallas_call | solution.py:219
  107.1 2.2 collective-permute-done.29.part_b
  110.1 2.1 collective-permute-start.32
  114.3 4.1 %collective-permute-done.32.refs_1_ = bf16[528,128]{1,0:T(8,128)(2,1)S(1)} collective-permute-done((bf16[528,128]{1,0:T(8,128)(2,1)S(1)}, bf16[528,128]{1,0:T(8,128)(2,1)S(1)}, u32[]{:S(2)}, u32[]{:S(2)}) %collective-permute-start.32) | collective-permute-done | bytes 135200 | tf_op jit(solution)/shard_map/ppermute | solution.py:379
  125.6 4.9 %weight.13.refs_4_ = bf16[2048,1024]{1,0:T(8,128)(2,1)S(1)} custom-call(s32[1]{0:T(128)} %bitcast.4.plane, s32[8,128]{1,0:T(8,128)S(1)} %get-tuple-element.240.place), custom_call_target="tpu_custom_call" | custom-call | flops 41943040 | bytes 4194304 | tf_op jit(solution)/shard_map/weight/pallas_call | solution.py:219
  130.5 2.2 collective-permute-done.36.part_b
  137.7 4.1 %collective-permute-done.39.refs_1_ = bf16[528,128]{1,0:T(8,128)(2,1)S(1)} collective-permute-done((bf16[528,128]{1,0:T(8,128)(2,1)S(1)}, bf16[528,128]{1,0:T(8,128)(2,1)S(1)}, u32[]{:S(2)}, u32[]{:S(2)}) %collective-permute-start.39) | collective-permute-done | bytes 135200 | tf_op jit(solution)/shard_map/ppermute | solution.py:379
  149.0 4.9 %weight.14.refs_4_ = bf16[2048,1024]{1,0:T(8,128)(2,1)S(1)} custom-call(s32[1]{0:T(128)} %bitcast.4.plane, s32[8,128]{1,0:T(8,128)S(1)} %get-tuple-element.240.place), custom_call_target="tpu_custom_call" | custom-call | flops 41943040 | bytes 4194304 | tf_op jit(solution)/shard_map/weight/pallas_call | solution.py:219
  153.9 2.2 collective-permute-done.43.part_b
  161.1 4.1 %collective-permute-done.46.refs_1_ = bf16[528,128]{1,0:T(8,128)(2,1)S(1)} collective-permute-done((bf16[528,128]{1,0:T(8,128)(2,1)S(1)}, bf16[528,128]{1,0:T(8,128)(2,1)S(1)}, u32[]{:S(2)}, u32[]{:S(2)}) %collective-permute-start.46) | collective-permute-done | bytes 135200 | tf_op jit(solution)/shard_map/ppermute | solution.py:379
  173.5 8.2 %collective-permute-done.50.part_b = bf16[784,128]{1,0:T(8,128)(2,1)S(1)} collective-permute-done((bf16[784,128]{1,0:T(8,128)(2,1)S(1)}, bf16[784,128]{1,0:T(8,128)(2,1)S(1)}, u32[]{:S(2)}, u32[]{:S(2)}) %collective-permute-start.50) | collective-permute-done | bytes 200736 | tf_op jit(solution)/shard_map/ppermute | solution.py:379
  182.6 2.1 collective-permute-start.53
  186.8 4.9 %weight.15.refs_4_ = bf16[2048,1024]{1,0:T(8,128)(2,1)S(1)} custom-call(s32[1]{0:T(128)} %bitcast.4.plane, s32[8,128]{1,0:T(8,128)S(1)} %get-tuple-element.240.place), custom_call_target="tpu_custom_call" | custom-call | flops 41943040 | bytes 4194304 | tf_op jit(solution)/shard_map/weight/pallas_call | solution.py:219
  191.7 2.4 %collective-permute-done.53.refs_1_.part_b = bf16[784,128]{1,0:T(8,128)(2,1)S(1)} collective-permute-done((bf16[784,128]{1,0:T(8,128)(2,1)S(1)}, bf16[784,128]{1,0:T(8,128)(2,1)S(1)}, u32[]{:S(2)}, u32[]{:S(2)}) %collective-permute-start.53) | collective-permute-done | bytes 200736 | tf_op jit(solution)/shard_map/ppermute | solution.py:379
  201.4 8.0 %collective-permute-done.57.part_b = bf16[784,128]{1,0:T(8,128)(2,1)S(1)} collective-permute-done((bf16[784,128]{1,0:T(8,128)(2,1)S(1)}, bf16[784,128]{1,0:T(8,128)(2,1)S(1)}, u32[]{:S(2)}, u32[]{:S(2)}) %collective-permute-start.57) | collective-permute-done | bytes 200736 | tf_op jit(solution)/shard_map/ppermute | solution.py:379
  217.8 2.3 collective-permute-done.62.refs_2_
  220.1 2.1 collective-permute-start.64
  (170 shorter events, 107.8 us)
Async XLA Ops:
  13.6 10.0 %collective-permute-start.4 = (f32[4,1,128]{2,1,0:T(1,128)S(1)}, f32[4,1,128]{2,1,0:T(1,128)S(1)}, u32[]{:S(2)}, u32[]{:S(2)}) collective-permute-start(f32[4,1,128]{2,1,0:T(1,128)S(1)} %get-tuple-element.136.refs_0_), channel_id=1, source_target_pairs={{0,12},{1,13},{2,14},{3,15},{4,8},{5,9},{6,10},{7,11},{8,4},{9,5},... | collective-permute-start | bytes 6152 | tf_op jit(solution)/shard_map/ppermute | solution.py:379
  25.6 9.5 %collective-permute-start.10 = (bf16[672,128]{1,0:T(8,128)(2,1)S(1)}, bf16[672,128]{1,0:T(8,128)(2,1)S(1)}, u32[]{:S(2)}, u32[]{:S(2)}) collective-permute-start(bf16[672,128]{1,0:T(8,128)(2,1)S(1)} %pair.8.part_a), channel_id=1, source_target_pairs={{0,1},{1,0},{2,3},{3,2},{4,5},{5,4},{6,7},{7,6},{8,9},{9,8},{10,11... | collective-permute-start | bytes 516104 | tf_op jit(solution)/shard_map/ppermute | solution.py:379
  27.3 9.5 %collective-permute-start.8 = (bf16[672,128]{1,0:T(8,128)(2,1)S(1)}, bf16[672,128]{1,0:T(8,128)(2,1)S(1)}, u32[]{:S(2)}, u32[]{:S(2)}) collective-permute-start(bf16[672,128]{1,0:T(8,128)(2,1)S(1)} %pair.8.part_a), channel_id=1, source_target_pairs={{0,3},{1,2},{2,1},{3,0},{4,7},{5,6},{6,5},{7,4},{8,11},{9,10},{10,... | collective-permute-start | bytes 516104 | tf_op jit(solution)/shard_map/ppermute | solution.py:379
  29.5 8.9 %collective-permute-start.9 = (bf16[672,128]{1,0:T(8,128)(2,1)S(1)}, bf16[672,128]{1,0:T(8,128)(2,1)S(1)}, u32[]{:S(2)}, u32[]{:S(2)}) collective-permute-start(bf16[672,128]{1,0:T(8,128)(2,1)S(1)} %pair.8.part_a), channel_id=1, source_target_pairs={{0,2},{1,3},{2,0},{3,1},{4,6},{5,7},{6,4},{7,5},{8,10},{9,11},{10,... | collective-permute-start | bytes 516104 | tf_op jit(solution)/shard_map/ppermute | solution.py:379
  38.6 8.4 %collective-permute-start.11 = (bf16[528,128]{1,0:T(8,128)(2,1)S(1)}, bf16[528,128]{1,0:T(8,128)(2,1)S(1)}, u32[]{:S(2)}, u32[]{:S(2)}) collective-permute-start(bf16[528,128]{1,0:T(8,128)(2,1)S(1)} %get-tuple-element.148.refs_0_), channel_id=1, source_target_pairs={{0,12},{1,13},{2,14},{3,15},{4,8},{5,9},{6,10},{7,11},{8,4},{9,5},... | collective-permute-start | bytes 405512 | tf_op jit(solution)/shard_map/ppermute | solution.py:379
  51.2 11.2 %collective-permute-start.15 = (bf16[656,128]{1,0:T(8,128)(2,1)S(1)}, bf16[656,128]{1,0:T(8,128)(2,1)S(1)}, u32[]{:S(2)}, u32[]{:S(2)}) collective-permute-start(bf16[656,128]{1,0:T(8,128)(2,1)S(1)} %pair.9.part_a), channel_id=1, source_target_pairs={{0,96},{16,112},{32,64},{48,80},{64,32},{80,48},{96,0},{112,16},{1... | collective-permute-start | bytes 503816 | tf_op jit(solution)/shard_map/ppermute | solution.py:379
  52.7 9.8 %collective-permute-start.16 = (bf16[656,128]{1,0:T(8,128)(2,1)S(1)}, bf16[656,128]{1,0:T(8,128)(2,1)S(1)}, u32[]{:S(2)}, u32[]{:S(2)}) collective-permute-start(bf16[656,128]{1,0:T(8,128)(2,1)S(1)} %pair.9.part_a), channel_id=1, source_target_pairs={{0,64},{16,80},{32,96},{48,112},{64,0},{80,16},{96,32},{112,48},{1... | collective-permute-start | bytes 503816 | tf_op jit(solution)/shard_map/ppermute | solution.py:379
  53.7 9.4 %collective-permute-start.17 = (bf16[656,128]{1,0:T(8,128)(2,1)S(1)}, bf16[656,128]{1,0:T(8,128)(2,1)S(1)}, u32[]{:S(2)}, u32[]{:S(2)}) collective-permute-start(bf16[656,128]{1,0:T(8,128)(2,1)S(1)} %pair.9.part_a), channel_id=1, source_target_pairs={{0,32},{16,48},{32,0},{48,16},{64,96},{80,112},{96,64},{112,80},{1... | collective-permute-start | bytes 503816 | tf_op jit(solution)/shard_map/ppermute | solution.py:379
  74.6 11.2 %collective-permute-start.22 = (bf16[656,128]{1,0:T(8,128)(2,1)S(1)}, bf16[656,128]{1,0:T(8,128)(2,1)S(1)}, u32[]{:S(2)}, u32[]{:S(2)}) collective-permute-start(bf16[656,128]{1,0:T(8,128)(2,1)S(1)} %pair.10.part_a), channel_id=1, source_target_pairs={{0,3},{1,2},{2,1},{3,0},{4,7},{5,6},{6,5},{7,4},{8,11},{9,10},{10,... | collective-permute-start | bytes 503816 | tf_op jit(solution)/shard_map/ppermute | solution.py:379
  76.6 9.2 %collective-permute-start.23 = (bf16[656,128]{1,0:T(8,128)(2,1)S(1)}, bf16[656,128]{1,0:T(8,128)(2,1)S(1)}, u32[]{:S(2)}, u32[]{:S(2)}) collective-permute-start(bf16[656,128]{1,0:T(8,128)(2,1)S(1)} %pair.10.part_a), channel_id=1, source_target_pairs={{0,2},{1,3},{2,0},{3,1},{4,6},{5,7},{6,4},{7,5},{8,10},{9,11},{10,... | collective-permute-start | bytes 503816 | tf_op jit(solution)/shard_map/ppermute | solution.py:379
  76.9 9.6 %collective-permute-start.24 = (bf16[656,128]{1,0:T(8,128)(2,1)S(1)}, bf16[656,128]{1,0:T(8,128)(2,1)S(1)}, u32[]{:S(2)}, u32[]{:S(2)}) collective-permute-start(bf16[656,128]{1,0:T(8,128)(2,1)S(1)} %pair.10.part_a), channel_id=1, source_target_pairs={{0,1},{1,0},{2,3},{3,2},{4,5},{5,4},{6,7},{7,6},{8,9},{9,8},{10,11... | collective-permute-start | bytes 503816 | tf_op jit(solution)/shard_map/ppermute | solution.py:379
  86.7 8.3 %collective-permute-start.25 = (bf16[528,128]{1,0:T(8,128)(2,1)S(1)}, bf16[528,128]{1,0:T(8,128)(2,1)S(1)}, u32[]{:S(2)}, u32[]{:S(2)}) collective-permute-start(bf16[528,128]{1,0:T(8,128)(2,1)S(1)} %get-tuple-element.171.refs_0_), channel_id=1, source_target_pairs={{0,12},{1,13},{2,14},{3,15},{4,8},{5,9},{6,10},{7,11},{8,4},{9,5},... | collective-permute-start | bytes 405512 | tf_op jit(solution)/shard_map/ppermute | solution.py:379
  98.0 11.2 %collective-permute-start.29 = (bf16[656,128]{1,0:T(8,128)(2,1)S(1)}, bf16[656,128]{1,0:T(8,128)(2,1)S(1)}, u32[]{:S(2)}, u32[]{:S(2)}) collective-permute-start(bf16[656,128]{1,0:T(8,128)(2,1)S(1)} %pair.11.part_a), channel_id=1, source_target_pairs={{0,96},{16,112},{32,64},{48,80},{64,32},{80,48},{96,0},{112,16},{1... | collective-permute-start | bytes 503816 | tf_op jit(solution)/shard_map/ppermute | solution.py:379
  99.5 9.8 %collective-permute-start.30 = (bf16[656,128]{1,0:T(8,128)(2,1)S(1)}, bf16[656,128]{1,0:T(8,128)(2,1)S(1)}, u32[]{:S(2)}, u32[]{:S(2)}) collective-permute-start(bf16[656,128]{1,0:T(8,128)(2,1)S(1)} %pair.11.part_a), channel_id=1, source_target_pairs={{0,64},{16,80},{32,96},{48,112},{64,0},{80,16},{96,32},{112,48},{1... | collective-permute-start | bytes 503816 | tf_op jit(solution)/shard_map/ppermute | solution.py:379
  100.5 9.4 %collective-permute-start.31 = (bf16[656,128]{1,0:T(8,128)(2,1)S(1)}, bf16[656,128]{1,0:T(8,128)(2,1)S(1)}, u32[]{:S(2)}, u32[]{:S(2)}) collective-permute-start(bf16[656,128]{1,0:T(8,128)(2,1)S(1)} %pair.11.part_a), channel_id=1, source_target_pairs={{0,32},{16,48},{32,0},{48,16},{64,96},{80,112},{96,64},{112,80},{1... | collective-permute-start | bytes 503816 | tf_op jit(solution)/shard_map/ppermute | solution.py:379
  121.4 11.2 %collective-permute-start.36 = (bf16[656,128]{1,0:T(8,128)(2,1)S(1)}, bf16[656,128]{1,0:T(8,128)(2,1)S(1)}, u32[]{:S(2)}, u32[]{:S(2)}) collective-permute-start(bf16[656,128]{1,0:T(8,128)(2,1)S(1)} %pair.12.part_a), channel_id=1, source_target_pairs={{0,3},{1,2},{2,1},{3,0},{4,7},{5,6},{6,5},{7,4},{8,11},{9,10},{10,... | collective-permute-start | bytes 503816 | tf_op jit(solution)/shard_map/ppermute | solution.py:379
  123.5 9.2 %collective-permute-start.37 = (bf16[656,128]{1,0:T(8,128)(2,1)S(1)}, bf16[656,128]{1,0:T(8,128)(2,1)S(1)}, u32[]{:S(2)}, u32[]{:S(2)}) collective-permute-start(bf16[656,128]{1,0:T(8,128)(2,1)S(1)} %pair.12.part_a), channel_id=1, source_target_pairs={{0,2},{1,3},{2,0},{3,1},{4,6},{5,7},{6,4},{7,5},{8,10},{9,11},{10,... | collective-permute-start | bytes 503816 | tf_op jit(solution)/shard_map/ppermute | solution.py:379
  123.8 9.5 %collective-permute-start.38 = (bf16[656,128]{1,0:T(8,128)(2,1)S(1)}, bf16[656,128]{1,0:T(8,128)(2,1)S(1)}, u32[]{:S(2)}, u32[]{:S(2)}) collective-permute-start(bf16[656,128]{1,0:T(8,128)(2,1)S(1)} %pair.12.part_a), channel_id=1, source_target_pairs={{0,1},{1,0},{2,3},{3,2},{4,5},{5,4},{6,7},{7,6},{8,9},{9,8},{10,11... | collective-permute-start | bytes 503816 | tf_op jit(solution)/shard_map/ppermute | solution.py:379
  133.5 8.3 %collective-permute-start.39 = (bf16[528,128]{1,0:T(8,128)(2,1)S(1)}, bf16[528,128]{1,0:T(8,128)(2,1)S(1)}, u32[]{:S(2)}, u32[]{:S(2)}) collective-permute-start(bf16[528,128]{1,0:T(8,128)(2,1)S(1)} %get-tuple-element.192.refs_0_), channel_id=1, source_target_pairs={{0,12},{1,13},{2,14},{3,15},{4,8},{5,9},{6,10},{7,11},{8,4},{9,5},... | collective-permute-start | bytes 405512 | tf_op jit(solution)/shard_map/ppermute | solution.py:379
  144.8 11.2 %collective-permute-start.43 = (bf16[656,128]{1,0:T(8,128)(2,1)S(1)}, bf16[656,128]{1,0:T(8,128)(2,1)S(1)}, u32[]{:S(2)}, u32[]{:S(2)}) collective-permute-start(bf16[656,128]{1,0:T(8,128)(2,1)S(1)} %pair.13.part_a), channel_id=1, source_target_pairs={{0,96},{16,112},{32,64},{48,80},{64,32},{80,48},{96,0},{112,16},{1... | collective-permute-start | bytes 503816 | tf_op jit(solution)/shard_map/ppermute | solution.py:379
  146.3 9.8 %collective-permute-start.44 = (bf16[656,128]{1,0:T(8,128)(2,1)S(1)}, bf16[656,128]{1,0:T(8,128)(2,1)S(1)}, u32[]{:S(2)}, u32[]{:S(2)}) collective-permute-start(bf16[656,128]{1,0:T(8,128)(2,1)S(1)} %pair.13.part_a), channel_id=1, source_target_pairs={{0,64},{16,80},{32,96},{48,112},{64,0},{80,16},{96,32},{112,48},{1... | collective-permute-start | bytes 503816 | tf_op jit(solution)/shard_map/ppermute | solution.py:379
  147.3 9.4 %collective-permute-start.45 = (bf16[656,128]{1,0:T(8,128)(2,1)S(1)}, bf16[656,128]{1,0:T(8,128)(2,1)S(1)}, u32[]{:S(2)}, u32[]{:S(2)}) collective-permute-start(bf16[656,128]{1,0:T(8,128)(2,1)S(1)} %pair.13.part_a), channel_id=1, source_target_pairs={{0,32},{16,48},{32,0},{48,16},{64,96},{80,112},{96,64},{112,80},{1... | collective-permute-start | bytes 503816 | tf_op jit(solution)/shard_map/ppermute | solution.py:379
  156.9 8.3 %collective-permute-start.46 = (bf16[528,128]{1,0:T(8,128)(2,1)S(1)}, bf16[528,128]{1,0:T(8,128)(2,1)S(1)}, u32[]{:S(2)}, u32[]{:S(2)}) collective-permute-start(bf16[528,128]{1,0:T(8,128)(2,1)S(1)} %get-tuple-element.213.refs_0_), channel_id=1, source_target_pairs={{0,12},{1,13},{2,14},{3,15},{4,8},{5,9},{6,10},{7,11},{8,4},{9,5},... | collective-permute-start | bytes 405512 | tf_op jit(solution)/shard_map/ppermute | solution.py:379
  169.0 12.6 %collective-permute-start.50 = (bf16[784,128]{1,0:T(8,128)(2,1)S(1)}, bf16[784,128]{1,0:T(8,128)(2,1)S(1)}, u32[]{:S(2)}, u32[]{:S(2)}) collective-permute-start(bf16[784,128]{1,0:T(8,128)(2,1)S(1)} %pair.14.part_a), channel_id=1, source_target_pairs={{0,3},{1,2},{2,1},{3,0},{4,7},{5,6},{6,5},{7,4},{8,11},{9,10},{10,... | collective-permute-start | bytes 602120 | tf_op jit(solution)/shard_map/ppermute | solution.py:379
  171.1 10.6 %collective-permute-start.51 = (bf16[784,128]{1,0:T(8,128)(2,1)S(1)}, bf16[784,128]{1,0:T(8,128)(2,1)S(1)}, u32[]{:S(2)}, u32[]{:S(2)}) collective-permute-start(bf16[784,128]{1,0:T(8,128)(2,1)S(1)} %pair.14.part_a), channel_id=1, source_target_pairs={{0,2},{1,3},{2,0},{3,1},{4,6},{5,7},{6,4},{7,5},{8,10},{9,11},{10,... | collective-permute-start | bytes 602120 | tf_op jit(solution)/shard_map/ppermute | solution.py:379
  171.5 10.8 %collective-permute-start.52 = (bf16[784,128]{1,0:T(8,128)(2,1)S(1)}, bf16[784,128]{1,0:T(8,128)(2,1)S(1)}, u32[]{:S(2)}, u32[]{:S(2)}) collective-permute-start(bf16[784,128]{1,0:T(8,128)(2,1)S(1)} %pair.14.part_a), channel_id=1, source_target_pairs={{0,1},{1,0},{2,3},{3,2},{4,5},{5,4},{6,7},{7,6},{8,9},{9,8},{10,11... | collective-permute-start | bytes 602120 | tf_op jit(solution)/shard_map/ppermute | solution.py:379
  182.6 11.5 %collective-permute-start.53 = (bf16[784,128]{1,0:T(8,128)(2,1)S(1)}, bf16[784,128]{1,0:T(8,128)(2,1)S(1)}, u32[]{:S(2)}, u32[]{:S(2)}) collective-permute-start(bf16[784,128]{1,0:T(8,128)(2,1)S(1)} %get-tuple-element.236.refs_0_.part_a), channel_id=1, source_target_pairs={{0,12},{1,13},{2,14},{3,15},{4,8},{5,9},{6,10},{7,11},{8,4},{9,5},... | collective-permute-start | bytes 602120 | tf_op jit(solution)/shard_map/ppermute | solution.py:379
  184.7 9.4 %collective-permute-start.54 = (bf16[784,128]{1,0:T(8,128)(2,1)S(1)}, bf16[784,128]{1,0:T(8,128)(2,1)S(1)}, u32[]{:S(2)}, u32[]{:S(2)}) collective-permute-start(bf16[784,128]{1,0:T(8,128)(2,1)S(1)} %get-tuple-element.236.refs_0_.part_a), channel_id=1, source_target_pairs={{0,8},{1,9},{2,10},{3,11},{4,12},{5,13},{6,14},{7,15},{8,0},{9,1},... | collective-permute-start | bytes 602120 | tf_op jit(solution)/shard_map/ppermute | solution.py:379
  185.0 9.8 %collective-permute-start.55 = (bf16[784,128]{1,0:T(8,128)(2,1)S(1)}, bf16[784,128]{1,0:T(8,128)(2,1)S(1)}, u32[]{:S(2)}, u32[]{:S(2)}) collective-permute-start(bf16[784,128]{1,0:T(8,128)(2,1)S(1)} %get-tuple-element.236.refs_0_.part_a), channel_id=1, source_target_pairs={{0,4},{1,5},{2,6},{3,7},{4,0},{5,1},{6,2},{7,3},{8,12},{9,13},{10,... | collective-permute-start | bytes 602120 | tf_op jit(solution)/shard_map/ppermute | solution.py:379
  196.8 12.6 %collective-permute-start.57 = (bf16[784,128]{1,0:T(8,128)(2,1)S(1)}, bf16[784,128]{1,0:T(8,128)(2,1)S(1)}, u32[]{:S(2)}, u32[]{:S(2)}) collective-permute-start(bf16[784,128]{1,0:T(8,128)(2,1)S(1)} %pair.15.part_a), channel_id=1, source_target_pairs={{0,96},{16,112},{32,64},{48,80},{64,32},{80,48},{96,0},{112,16},{1... | collective-permute-start | bytes 602120 | tf_op jit(solution)/shard_map/ppermute | solution.py:379
  198.3 11.2 %collective-permute-start.58 = (bf16[784,128]{1,0:T(8,128)(2,1)S(1)}, bf16[784,128]{1,0:T(8,128)(2,1)S(1)}, u32[]{:S(2)}, u32[]{:S(2)}) collective-permute-start(bf16[784,128]{1,0:T(8,128)(2,1)S(1)} %pair.15.part_a), channel_id=1, source_target_pairs={{0,64},{16,80},{32,96},{48,112},{64,0},{80,16},{96,32},{112,48},{1... | collective-permute-start | bytes 602120 | tf_op jit(solution)/shard_map/ppermute | solution.py:379
  199.3 10.8 %collective-permute-start.59 = (bf16[784,128]{1,0:T(8,128)(2,1)S(1)}, bf16[784,128]{1,0:T(8,128)(2,1)S(1)}, u32[]{:S(2)}, u32[]{:S(2)}) collective-permute-start(bf16[784,128]{1,0:T(8,128)(2,1)S(1)} %pair.15.part_a), channel_id=1, source_target_pairs={{0,32},{16,48},{32,0},{48,16},{64,96},{80,112},{96,64},{112,80},{1... | collective-permute-start | bytes 602120 | tf_op jit(solution)/shard_map/ppermute | solution.py:379
  (37 other events, 178.7 us)

commit v6 on v5

--- a/solution.py
+++ b/solution.py
@@ -167,12 +167,12 @@
     return split_row(jnp.sum(jnp.transpose(squares), axis=0, keepdims=True))
 
 
-def embed_kernel(place, token, out, tile_out):
+def embed_kernel(place, token, out, tile_out, before_out):
     tokens = jnp.broadcast_to(token[...], (TOK, PIECE)) * 16411 + wrapped(EMBED_KEY * 1000003)
     tokens = tokens + lax.broadcasted_iota(jnp.int32, (TOK, PIECE), 1)
     tokens = tokens + (place[1] * STEP_C + place[3] * STEP_P)
     squares = jnp.zeros((TOK, PIECE), F32)
-    for slot, partner in enumerate(PARTNERS):
+    for slot, partner in enumerate(SLOTS):
         for digit in range(4):
             first = jnp.bitwise_xor(place[4], partner) * STEP_Q + digit * STEP_R
             part = hashed(tokens + first, math.sqrt(3.0)).astype(BF)
@@ -180,11 +180,15 @@
             wide = part.astype(F32)
             squares = squares + wide * wide
     tile_out[...] = squares_tile(squares)
+    tokens = tokens + (place[2] * STEP_R + place[4] * STEP_Q - place[3] * STEP_P)
+    for digit in range(4):
+        rows = slice(digit * TOK, (digit + 1) * TOK)
+        before_out[rows, :] = hashed(tokens + digit * STEP_P, math.sqrt(3.0)).astype(BF)
 
 
 def first_scale_kernel(embedded, tile, *refs):
     gains, outs = dict(zip(SHORT, refs[:4])), refs[4:]
-    for slot, partner in enumerate(PARTNERS):
+    for slot, partner in enumerate(SLOTS):
         for digit in range(4):
             rows = slice(digit * TOK, (digit + 1) * TOK)
             outs[slot][rows, :] = (embedded[slot, rows, :].astype(F32) * gains[partner][digit]).astype(BF)
@@ -202,7 +206,7 @@
     def step(index, carry):
         piece = index // 2
         slot = piece // 4
-        partner = jnp.where(slot == 0, 0, jnp.where(slot == 1, PARTNERS[1], jnp.where(slot == 2, PARTNERS[2], PARTNERS[3])))
+        partner = jnp.where(slot == 0, 0, jnp.where(slot == 1, SLOTS[1], jnp.where(slot == 2, SLOTS[2], SLOTS[3])))
         first = jnp.bitwise_xor(plane[0], partner) * (STEP_Q * 16411) + (piece % 4) * (row_step * 16411) + (index % 2) * (chunk * 16411)
         start = pl.multiple_of(index * chunk, chunk)
         out[pl.ds(start, chunk), :] = hashed(base + first, math.sqrt(3.0 / D)).astype(BF)
@@ -221,10 +225,27 @@
     )
 
 
+BEGUN = 1536
+
+
+def rows_of(parts):
+    return jnp.concatenate([part[digit * TOK : (digit + 1) * TOK, :] for part in parts for digit in range(4)], axis=1)
+
+
+def begin_kernel(core, part_a, part_b, part_c, weight, their_out, own_out):
+    scaled = rows_of((part_a, part_b, part_c))
+    for first, out in (((1 - core[0]) * STATE, their_out), (core[0] * STATE, own_out)):
+        for pair in range(2):
+            columns = pl.ds(pl.multiple_of(first + pair * 256, 256), 256)
+            part = jnp.dot(scaled, weight[:BEGUN, columns], preferred_element_type=F32)
+            for half in range(2):
+                rows = slice((2 * pair + half) * TOK, (2 * pair + half + 1) * TOK)
+                out[rows, :] = part[:, half * PIECE : (half + 1) * PIECE]
+
+
 def contract_kernel(theirs, core, *refs):
-    parts, (weight, *more, out) = refs[:4], refs[4:]
-    scaled = [part[digit * TOK : (digit + 1) * TOK, :] for part in parts for digit in range(4)]
-    scaled = jnp.concatenate(scaled, axis=1)
+    parts, (weight, begun, *more, out) = refs[:4], refs[4:]
+    scaled = rows_of(parts[3:])
     squares = joined_row(parts[0][STATE:, :])
     for part in parts[1:]:
         squares = squares + joined_row(part[STATE:, :])
@@ -239,22 +260,24 @@
     first = (1 - core[0] if theirs else core[0]) * STATE
     for pair in range(2):
         columns = pl.ds(pl.multiple_of(first + pair * 256, 256), 256)
-        part = jnp.dot(scaled, weight[:, columns], preferred_element_type=F32).astype(out.dtype)
+        part = jnp.dot(scaled, weight[BEGUN:, columns], preferred_element_type=F32)
         for half in range(2):
             rows = slice((2 * pair + half) * TOK, (2 * pair + half + 1) * TOK)
-            out[rows, :] = part[:, half * PIECE : (half + 1) * PIECE]
+            out[rows, :] = (begun[rows, :] + part[:, half * PIECE : (half + 1) * PIECE]).astype(out.dtype)
 
 
 def pair_kernel(digit, own, other, stream, *refs):
     *more, out = refs
     total = own[...] + other[...].astype(F32)
     out[:STATE, :] = total[:STATE].astype(BF)
+    if more:
+        out[STATE:GATHER, :] = split_row(joined_row(total[STATE:GATHER]))
+        out[GATHER:, :] = more[0][...]
+        return
     start = pl.multiple_of(digit[0] * TOK, TOK)
     out[STATE : STATE + TOK, :] = stream[pl.ds(start, TOK), :]
     out[STATE + TOK : SUM, :] = split_row(joined_row(total[STATE:GATHER]))
-    if more:
-        out[SUM:, :] = more[0][...]
-    elif total.shape[0] > GATHER:
+    if total.shape[0] > GATHER:
         out[SUM:, :] = total[GATHER:].astype(BF)
 
 
@@ -265,7 +288,7 @@
 
 
 def pre_kernel(part_a, part_b, part_c, part_d, out):
-    parts = zip(PARTNERS, (part_a, part_b, part_c, part_d))
+    parts = zip(SLOTS, (part_a, part_b, part_c, part_d))
     wide = {partner: part[GATHER + TOK :, :].astype(F32) for partner, part in parts}
     out[...] = (wide[0] + wide[1]) + (wide[2] + wide[3])
 
@@ -286,10 +309,10 @@
     following = layer + 1 < LAYERS
     fold = layer + 2 == LAYERS
     if layer == 0:
-        stream_out, mean_out, message_out, gains = refs
+        before, stream_out, mean_out, message_out, gains = refs
         for partner, part in zip(PARTNERS, parts):
             for index in range(4):
-                row = part[SUM : SUM + 16, :][index : index + 1].astype(F32)
+                row = part[GATHER : GATHER + 16, :][index : index + 1].astype(F32)
                 gains[index, jnp.bitwise_xor(digit[0], partner)] = row
     elif fold:
         gains, fold_weight, fold_gain, stream_out, mean_out, message_out = refs
@@ -297,7 +320,10 @@
         gains, stream_out, mean_out, message_out = refs
     else:
         stream_out, mean_out, odd_out, pre_out = refs
-    placed(digit, parts, stream_out)
+    if layer:
+        placed(digit, parts, stream_out)
+    else:
+        stream_out[...] = before[...]
 
     def total(rows):
         wide = {partner: part[rows, :].astype(F32) for partner, part in zip(PARTNERS, parts)}
@@ -306,7 +332,7 @@
     if not following:
         odd_out[...] = stream_out[...]
         pre_out[...] = total(slice(SUM, SUM + TOK))
-    squares = joined_row(total(slice(STATE + TOK, SUM)))
+    squares = joined_row(total(slice(STATE + TOK, SUM) if layer else slice(STATE, GATHER)))
     mean = jnp.transpose(jnp.broadcast_to(squares, (TOK, TOK))) * np.float32(1.0 / D)
     mean_out[...] = mean
     scale = lax.rsqrt(mean + EPSILON)
@@ -368,6 +394,7 @@
 
 
 PARTNERS = (0, 3, 2, 1)
+SLOTS = (0, 3, 1, 2)
 SHORT = (0, 3, 2, 1)
 
 
@@ -498,8 +525,8 @@
         core, facts, lax.ppermute(facts, "segment", CORE)
     )
     facts = exchange(facts, "x", SHORT)
-    embedded, tile = call(
-        embed_kernel, "embed", (sds((4, STATE, PIECE), BF), sds((16, TOK), BF)), [SMEM, VMEM]
+    embedded, tile, before = call(
+        embed_kernel, "embed", (sds((4, STATE, PIECE), BF), sds((16, TOK), BF), state_shape), [SMEM, VMEM]
     )(place, token_ids.reshape(TOK, 1))
     first_gain, odd_gain, even_gains, places, student_place, fold_place, fold_gain, up_place, up_gain = call(
         facts_kernel,
@@ -521,9 +548,10 @@
         (axis, digit), other_digit = (("y", row), column) if even else (("x", column), row)
         last = layer + 1 == LAYERS
         if layer:
-            parts = exchange(message, "z")
+            arrived = dict(zip(PARTNERS, exchange(message, "z")))
+            parts = [arrived[partner] for partner in SLOTS]
         if layer in (2, 4, 6):
-            *parts, odd_halves[-1] = lax.optimization_barrier((*parts, odd_halves[-1]))
+            parts[3], odd_halves[-1] = lax.optimization_barrier((parts[3], odd_halves[-1]))
         if last:
             weight = teacher_weight(layer, plane, gate(places, message))
         if layer + 2 == LAYERS:
@@ -541,29 +569,37 @@
                 [SMEM] + [VMEM] * 4,
                 flops=1 << 25,
             )(core, up_place, up_gain, now, odd_half)
-            *parts, pre_own, pre_other = lax.optimization_barrier((*parts, pre_own, pre_other))
+            parts[3], pre_own, pre_other = lax.optimization_barrier((parts[3], pre_own, pre_other))
         if last:
             mean = call(mean_kernel, "mean", mean_shape, [SMEM] + [VMEM] * 7)(segment, *means)
-            *parts, mean = lax.optimization_barrier((*parts, mean))
+            parts[3], mean = lax.optimization_barrier((parts[3], mean))
             pre = call(pre_kernel, "pre", sds((TOK, R), F32), [VMEM] * 4)(*parts)
         rows = GATHER + (TOK if layer + 2 >= LAYERS else 0)
         extra = ([pre_other], [pre_own]) if layer + 2 == LAYERS else ([], [])
-        contract = dict(in_specs=[SMEM] + [VMEM] * (5 + len(extra[0])), flops=TOK * WEIGHTS, nbytes=2 * WEIGHTS)
+        begun = call(
+            begin_kernel,
+            "begin",
+            (sds((STATE, PIECE), F32),) * 2,
+            [SMEM] + [VMEM] * 4,
+            flops=2 * TOK * WEIGHTS,
+            nbytes=2 * WEIGHTS,
+        )(core, *parts[:3], weight)
+        contract = dict(in_specs=[SMEM] + [VMEM] * (6 + len(extra[0])), flops=TOK * WEIGHTS // 4, nbytes=WEIGHTS // 2)
         other = call(functools.partial(contract_kernel, True), "contract_other", sds((rows, PIECE), BF), **contract)(
-            core, *parts, weight, *extra[0]
+            core, *parts, weight, begun[0], *extra[0]
         )
         own = call(functools.partial(contract_kernel, False), "contract_own", sds((rows, PIECE), F32), **contract)(
-            core, *parts, weight, *extra[1]
+            core, *parts, weight, begun[1], *extra[1]
         )
         other = lax.ppermute(other, "segment", CORE)
         more = [odd_gain] if layer == 0 else []
-        rows = SUM + (16 if layer == 0 else TOK if layer + 2 >= LAYERS else 0)
+        rows = GATHER + 16 if layer == 0 else SUM + (TOK if layer + 2 >= LAYERS else 0)
         summed = call(pair_kernel, "pair", sds((rows, PIECE), BF), [SMEM] + [VMEM] * (3 + len(more)))(
             other_digit, own, other, streams[-1], *more
         )
         parts = exchange(summed, axis)
         out = [state_shape, mean_shape]
-        given = [] if layer == 0 or last else [odd_gains if even else even_gains]
+        given = [before] if layer == 0 else [] if last else [odd_gains if even else even_gains]
         if layer + 2 < LAYERS:
             weight = teacher_weight(layer + 1, plane, gate(places, summed))
             *parts, weight = lax.optimization_barrier((*parts, weight))

time: 229 us -> 229 us (level)
    pallas_call x0 -> x8, Pallas kernels: none -> 4.96 us  [local(): call(begin_kernel, 'begin', (sds((STATE, PIECE), F32),) * 2, [SMEM] + [VM...]
    ppermute x57, waiting for transfers between devices: 76.8 us -> 73.1 us  [exchange(): lax.ppermute(values[k], axis, [(i, i ^ k * step) for i in range(size)])]
  transfers between devices with their start and end apart: 67 -> 67, of which waited for: 44 -> 50; matrix products, arithmetic and copies ran while one was open for 1% -> 1% of each run, Pallas kernels for 20% -> 21%
where the time goes in v6:
time: 229 us; the launch traced here: 228 us
  waiting for transfers between devices  84.5 us (37%)
  starting transfers between devices  81.4 us (36%)
  Pallas kernels  56.9 us (25%)
  local copies, waits for them, and re-layouts  3.07 us (1%)
  between operations  2.49 us (1%)
    ppermute x57, starting transfers between devices, exchange(): lax.ppermute(values[k], axis, [(i, i ^ k * step) for i in range(size)])  80.6 us
    ppermute x57, waiting for transfers between devices, exchange(): lax.ppermute(values[k], axis, [(i, i ^ k * step) for i in range(size)])  73.1 us
    pallas_call x8, Pallas kernels, teacher_weight(): call(body, 'weight', sds((2048, WIDTH), BF), [SMEM, VMEM], flops=20 * WEI...  39 us
    ppermute x8, waiting for transfers between devices, local(): other = lax.ppermute(other, 'segment', CORE)  8.75 us
    pallas_call x8, Pallas kernels, local(): call(begin_kernel, 'begin', (sds((STATE, PIECE), F32),) * 2, [SMEM] + [VM...  4.96 us
  transfers between devices with their start and end apart: 67, of which 50 were waited for; matrix products, arithmetic and copies ran while one was open for 1% of the time, Pallas kernels for 21%

profile of v6, /device:TPU:0, one launch (start us, length us, event | category | flops | bytes accessed | tf_op | source)
XLA Modules:
  0.0 228.3 jit_solution(6137080692005059455)
XLA Ops:
  4.8 2.8 %collective-permute-start.1 = (bf16[2,48,128]{2,1,0:T(8,128)(2,1)S(1)}, bf16[2,48,128]{2,1,0:T(8,128)(2,1)S(1)}, u32[]{:S(2)}, u32[]{:S(2)}) collective-permute-start(bf16[2,48,128]{2,1,0:T(8,128)(2,1)S(1)} %chip.1.refs_0_), channel_id=1, source_target_pairs={{0,96},{16,112},{32,64},{48,80},{64,32},{80,48},{96,0},{112,16},{1... | collective-permute-start | bytes 73736 | tf_op jit(solution)/shard_map/ppermute | solution.py:406
  13.6 4.1 %collective-permute-start.4 = (f32[4,1,128]{2,1,0:T(1,128)S(1)}, f32[4,1,128]{2,1,0:T(1,128)S(1)}, u32[]{:S(2)}, u32[]{:S(2)}) collective-permute-start(f32[4,1,128]{2,1,0:T(1,128)S(1)} %get-tuple-element.138.refs_0_), channel_id=1, source_target_pairs={{0,12},{1,13},{2,14},{3,15},{4,8},{5,9},{6,10},{7,11},{8,4},{9,5},... | collective-permute-start | bytes 6152 | tf_op jit(solution)/shard_map/ppermute | solution.py:406
  18.6 4.9 %weight.8.refs_4_ = bf16[2048,1024]{1,0:T(8,128)(2,1)S(1)} custom-call(s32[1]{0:T(128)} %bitcast.4.plane, s32[8,128]{1,0:T(8,128)S(1)} %get-tuple-element.242.place), custom_call_target="tpu_custom_call" | custom-call | flops 41943040 | bytes 4194304 | tf_op jit(solution)/shard_map/weight/pallas_call | solution.py:223
  26.0 3.1 %collective-permute-start.8 = (bf16[544,128]{1,0:T(8,128)(2,1)S(1)}, bf16[544,128]{1,0:T(8,128)(2,1)S(1)}, u32[]{:S(2)}, u32[]{:S(2)}) collective-permute-start(bf16[544,128]{1,0:T(8,128)(2,1)S(1)} %pair.8.part_a), channel_id=1, source_target_pairs={{0,3},{1,2},{2,1},{3,0},{4,7},{5,6},{6,5},{7,4},{8,11},{9,10},{10,... | collective-permute-start | bytes 417800 | tf_op jit(solution)/shard_map/ppermute | solution.py:406
  30.2 4.9 %weight.9.refs_4_ = bf16[2048,1024]{1,0:T(8,128)(2,1)S(1)} custom-call(s32[1]{0:T(128)} %bitcast.4.plane, s32[8,128]{1,0:T(8,128)S(1)} %get-tuple-element.242.place), custom_call_target="tpu_custom_call" | custom-call | flops 41943040 | bytes 4194304 | tf_op jit(solution)/shard_map/weight/pallas_call | solution.py:223
  37.4 3.2 %collective-permute-start.11 = (bf16[528,128]{1,0:T(8,128)(2,1)S(1)}, bf16[528,128]{1,0:T(8,128)(2,1)S(1)}, u32[]{:S(2)}, u32[]{:S(2)}) collective-permute-start(bf16[528,128]{1,0:T(8,128)(2,1)S(1)} %get-tuple-element.153.part_a.refs_0_), channel_id=1, source_target_pairs={{0,12},{1,13},{2,14},{3,15},{4,8},{5,9},{6,10},{7,11},{8,4},{9,5},... | collective-permute-start | bytes 405512 | tf_op jit(solution)/shard_map/ppermute | solution.py:406
  42.2 2.5 %collective-permute-done.11.part_b.refs_1_ = bf16[528,128]{1,0:T(8,128)(2,1)S(1)} collective-permute-done((bf16[528,128]{1,0:T(8,128)(2,1)S(1)}, bf16[528,128]{1,0:T(8,128)(2,1)S(1)}, u32[]{:S(2)}, u32[]{:S(2)}) %collective-permute-start.11) | collective-permute-done | bytes 135200 | tf_op jit(solution)/shard_map/ppermute | solution.py:406
  53.5 4.9 %weight.10.refs_4_ = bf16[2048,1024]{1,0:T(8,128)(2,1)S(1)} custom-call(s32[1]{0:T(128)} %bitcast.4.plane, s32[8,128]{1,0:T(8,128)S(1)} %get-tuple-element.242.place), custom_call_target="tpu_custom_call" | custom-call | flops 41943040 | bytes 4194304 | tf_op jit(solution)/shard_map/weight/pallas_call | solution.py:223
  63.2 2.5 %collective-permute-start.19 = (bf16[528,128]{1,0:T(8,128)(2,1)S(1)}, bf16[528,128]{1,0:T(8,128)(2,1)S(1)}, u32[]{:S(2)}, u32[]{:S(2)}) collective-permute-start(bf16[528,128]{1,0:T(8,128)(2,1)S(1)} %get-tuple-element.164.part_a.refs_0_), channel_id=1, source_target_pairs={{0,12},{1,13},{2,14},{3,15},{4,8},{5,9},{6,10},{7,11},{8,4},{9,5},... | collective-permute-start | bytes 405512 | tf_op jit(solution)/shard_map/ppermute | solution.py:406
  65.8 3.3 %collective-permute-done.18.refs_3_ = bf16[528,128]{1,0:T(8,128)(2,1)S(1)} collective-permute-done((bf16[528,128]{1,0:T(8,128)(2,1)S(1)}, bf16[528,128]{1,0:T(8,128)(2,1)S(1)}, u32[]{:S(2)}, u32[]{:S(2)}) %collective-permute-start.18) | collective-permute-done | bytes 135200 | tf_op jit(solution)/shard_map/ppermute | solution.py:406
  73.3 2.8 %collective-permute-start.22 = (bf16[656,128]{1,0:T(8,128)(2,1)S(1)}, bf16[656,128]{1,0:T(8,128)(2,1)S(1)}, u32[]{:S(2)}, u32[]{:S(2)}) collective-permute-start(bf16[656,128]{1,0:T(8,128)(2,1)S(1)} %pair.10.part_a), channel_id=1, source_target_pairs={{0,3},{1,2},{2,1},{3,0},{4,7},{5,6},{6,5},{7,4},{8,11},{9,10},{10,... | collective-permute-start | bytes 503816 | tf_op jit(solution)/shard_map/ppermute | solution.py:406
  77.4 4.9 %weight.11.refs_4_ = bf16[2048,1024]{1,0:T(8,128)(2,1)S(1)} custom-call(s32[1]{0:T(128)} %bitcast.4.plane, s32[8,128]{1,0:T(8,128)S(1)} %get-tuple-element.242.place), custom_call_target="tpu_custom_call" | custom-call | flops 41943040 | bytes 4194304 | tf_op jit(solution)/shard_map/weight/pallas_call | solution.py:223
  85.4 2.3 collective-permute-start.25
  87.6 2.5 %collective-permute-start.27 = (bf16[528,128]{1,0:T(8,128)(2,1)S(1)}, bf16[528,128]{1,0:T(8,128)(2,1)S(1)}, u32[]{:S(2)}, u32[]{:S(2)}) collective-permute-start(bf16[528,128]{1,0:T(8,128)(2,1)S(1)} %get-tuple-element.177.part_a.refs_0_), channel_id=1, source_target_pairs={{0,8},{1,9},{2,10},{3,11},{4,12},{5,13},{6,14},{7,15},{8,0},{9,1},... | collective-permute-start | bytes 405512 | tf_op jit(solution)/shard_map/ppermute | solution.py:406
  90.1 3.0 %collective-permute-done.25.part_b.refs_1_ = bf16[528,128]{1,0:T(8,128)(2,1)S(1)} collective-permute-done((bf16[528,128]{1,0:T(8,128)(2,1)S(1)}, bf16[528,128]{1,0:T(8,128)(2,1)S(1)}, u32[]{:S(2)}, u32[]{:S(2)}) %collective-permute-start.25) | collective-permute-done | bytes 135200 | tf_op jit(solution)/shard_map/ppermute | solution.py:406
  101.2 4.9 %weight.12.refs_4_ = bf16[2048,1024]{1,0:T(8,128)(2,1)S(1)} custom-call(s32[1]{0:T(128)} %bitcast.4.plane, s32[8,128]{1,0:T(8,128)S(1)} %get-tuple-element.242.place), custom_call_target="tpu_custom_call" | custom-call | flops 41943040 | bytes 4194304 | tf_op jit(solution)/shard_map/weight/pallas_call | solution.py:223
  112.8 4.0 %collective-permute-done.32.refs_3_ = bf16[528,128]{1,0:T(8,128)(2,1)S(1)} collective-permute-done((bf16[528,128]{1,0:T(8,128)(2,1)S(1)}, bf16[528,128]{1,0:T(8,128)(2,1)S(1)}, u32[]{:S(2)}, u32[]{:S(2)}) %collective-permute-start.32) | collective-permute-done | bytes 135200 | tf_op jit(solution)/shard_map/ppermute | solution.py:406
  120.5 2.8 %collective-permute-start.36 = (bf16[656,128]{1,0:T(8,128)(2,1)S(1)}, bf16[656,128]{1,0:T(8,128)(2,1)S(1)}, u32[]{:S(2)}, u32[]{:S(2)}) collective-permute-start(bf16[656,128]{1,0:T(8,128)(2,1)S(1)} %pair.12.part_a), channel_id=1, source_target_pairs={{0,3},{1,2},{2,1},{3,0},{4,7},{5,6},{6,5},{7,4},{8,11},{9,10},{10,... | collective-permute-start | bytes 503816 | tf_op jit(solution)/shard_map/ppermute | solution.py:406
  124.7 4.9 %weight.13.refs_4_ = bf16[2048,1024]{1,0:T(8,128)(2,1)S(1)} custom-call(s32[1]{0:T(128)} %bitcast.4.plane, s32[8,128]{1,0:T(8,128)S(1)} %get-tuple-element.242.place), custom_call_target="tpu_custom_call" | custom-call | flops 41943040 | bytes 4194304 | tf_op jit(solution)/shard_map/weight/pallas_call | solution.py:223
  132.6 2.3 %collective-permute-start.39 = (bf16[528,128]{1,0:T(8,128)(2,1)S(1)}, bf16[528,128]{1,0:T(8,128)(2,1)S(1)}, u32[]{:S(2)}, u32[]{:S(2)}) collective-permute-start(bf16[528,128]{1,0:T(8,128)(2,1)S(1)} %get-tuple-element.199.part_a.refs_0_), channel_id=1, source_target_pairs={{0,12},{1,13},{2,14},{3,15},{4,8},{5,9},{6,10},{7,11},{8,4},{9,5},... | collective-permute-start | bytes 405512 | tf_op jit(solution)/shard_map/ppermute | solution.py:406
  134.9 2.5 %collective-permute-start.41 = (bf16[528,128]{1,0:T(8,128)(2,1)S(1)}, bf16[528,128]{1,0:T(8,128)(2,1)S(1)}, u32[]{:S(2)}, u32[]{:S(2)}) collective-permute-start(bf16[528,128]{1,0:T(8,128)(2,1)S(1)} %get-tuple-element.199.part_a.refs_0_), channel_id=1, source_target_pairs={{0,8},{1,9},{2,10},{3,11},{4,12},{5,13},{6,14},{7,15},{8,0},{9,1},... | collective-permute-start | bytes 405512 | tf_op jit(solution)/shard_map/ppermute | solution.py:406
  137.4 3.0 %collective-permute-done.39.part_b.refs_1_ = bf16[528,128]{1,0:T(8,128)(2,1)S(1)} collective-permute-done((bf16[528,128]{1,0:T(8,128)(2,1)S(1)}, bf16[528,128]{1,0:T(8,128)(2,1)S(1)}, u32[]{:S(2)}, u32[]{:S(2)}) %collective-permute-start.39) | collective-permute-done | bytes 135200 | tf_op jit(solution)/shard_map/ppermute | solution.py:406
  148.4 4.9 %weight.14.refs_4_ = bf16[2048,1024]{1,0:T(8,128)(2,1)S(1)} custom-call(s32[1]{0:T(128)} %bitcast.4.plane, s32[8,128]{1,0:T(8,128)S(1)} %get-tuple-element.242.place), custom_call_target="tpu_custom_call" | custom-call | flops 41943040 | bytes 4194304 | tf_op jit(solution)/shard_map/weight/pallas_call | solution.py:223
  160.0 3.9 %collective-permute-done.46.refs_3_ = bf16[528,128]{1,0:T(8,128)(2,1)S(1)} collective-permute-done((bf16[528,128]{1,0:T(8,128)(2,1)S(1)}, bf16[528,128]{1,0:T(8,128)(2,1)S(1)}, u32[]{:S(2)}, u32[]{:S(2)}) %collective-permute-start.46) | collective-permute-done | bytes 135200 | tf_op jit(solution)/shard_map/ppermute | solution.py:406
  167.7 2.8 %collective-permute-start.50 = (bf16[784,128]{1,0:T(8,128)(2,1)S(1)}, bf16[784,128]{1,0:T(8,128)(2,1)S(1)}, u32[]{:S(2)}, u32[]{:S(2)}) collective-permute-start(bf16[784,128]{1,0:T(8,128)(2,1)S(1)} %pair.14.part_a), channel_id=1, source_target_pairs={{0,3},{1,2},{2,1},{3,0},{4,7},{5,6},{6,5},{7,4},{8,11},{9,10},{10,... | collective-permute-start | bytes 602120 | tf_op jit(solution)/shard_map/ppermute | solution.py:406
  172.2 8.2 %collective-permute-done.50.part_b = bf16[784,128]{1,0:T(8,128)(2,1)S(1)} collective-permute-done((bf16[784,128]{1,0:T(8,128)(2,1)S(1)}, bf16[784,128]{1,0:T(8,128)(2,1)S(1)}, u32[]{:S(2)}, u32[]{:S(2)}) %collective-permute-start.50) | collective-permute-done | bytes 200736 | tf_op jit(solution)/shard_map/ppermute | solution.py:406
  185.0 4.9 %weight.15.refs_4_ = bf16[2048,1024]{1,0:T(8,128)(2,1)S(1)} custom-call(s32[1]{0:T(128)} %bitcast.4.plane, s32[8,128]{1,0:T(8,128)S(1)} %get-tuple-element.242.place), custom_call_target="tpu_custom_call" | custom-call | flops 41943040 | bytes 4194304 | tf_op jit(solution)/shard_map/weight/pallas_call | solution.py:223
  190.8 2.4 %collective-permute-done.53.part_b.refs_1_ = bf16[784,128]{1,0:T(8,128)(2,1)S(1)} collective-permute-done((bf16[784,128]{1,0:T(8,128)(2,1)S(1)}, bf16[784,128]{1,0:T(8,128)(2,1)S(1)}, u32[]{:S(2)}, u32[]{:S(2)}) %collective-permute-start.53) | collective-permute-done | bytes 200736 | tf_op jit(solution)/shard_map/ppermute | solution.py:406
  200.2 8.0 %collective-permute-done.57.part_b = bf16[784,128]{1,0:T(8,128)(2,1)S(1)} collective-permute-done((bf16[784,128]{1,0:T(8,128)(2,1)S(1)}, bf16[784,128]{1,0:T(8,128)(2,1)S(1)}, u32[]{:S(2)}, u32[]{:S(2)}) %collective-permute-start.57) | collective-permute-done | bytes 200736 | tf_op jit(solution)/shard_map/ppermute | solution.py:406
  211.3 2.8 %collective-permute-start.61 = (bf16[144,128]{1,0:T(8,128)(2,1)S(1)}, bf16[144,128]{1,0:T(8,128)(2,1)S(1)}, u32[]{:S(2)}, u32[]{:S(2)}) collective-permute-start(bf16[144,128]{1,0:T(8,128)(2,1)S(1)} %get-tuple-element.265.refs_0_), channel_id=1, source_target_pairs={{0,3},{1,2},{2,1},{3,0},{4,7},{5,6},{6,5},{7,4},{8,11},{9,10},{10,... | collective-permute-start | bytes 110600 | tf_op jit(solution)/shard_map/ppermute | solution.py:406
  216.6 3.0 %collective-permute-done.62.refs_2_ = bf16[144,128]{1,0:T(8,128)(2,1)S(1)} collective-permute-done((bf16[144,128]{1,0:T(8,128)(2,1)S(1)}, bf16[144,128]{1,0:T(8,128)(2,1)S(1)}, u32[]{:S(2)}, u32[]{:S(2)}) %collective-permute-start.62) | collective-permute-done | bytes 36896 | tf_op jit(solution)/shard_map/ppermute | solution.py:406
  219.6 2.3 collective-permute-start.64
  (178 shorter events, 107.0 us)
Async XLA Ops:
  13.6 10.0 %collective-permute-start.4 = (f32[4,1,128]{2,1,0:T(1,128)S(1)}, f32[4,1,128]{2,1,0:T(1,128)S(1)}, u32[]{:S(2)}, u32[]{:S(2)}) collective-permute-start(f32[4,1,128]{2,1,0:T(1,128)S(1)} %get-tuple-element.138.refs_0_), channel_id=1, source_target_pairs={{0,12},{1,13},{2,14},{3,15},{4,8},{5,9},{6,10},{7,11},{8,4},{9,5},... | collective-permute-start | bytes 6152 | tf_op jit(solution)/shard_map/ppermute | solution.py:406
  26.0 9.3 %collective-permute-start.8 = (bf16[544,128]{1,0:T(8,128)(2,1)S(1)}, bf16[544,128]{1,0:T(8,128)(2,1)S(1)}, u32[]{:S(2)}, u32[]{:S(2)}) collective-permute-start(bf16[544,128]{1,0:T(8,128)(2,1)S(1)} %pair.8.part_a), channel_id=1, source_target_pairs={{0,3},{1,2},{2,1},{3,0},{4,7},{5,6},{6,5},{7,4},{8,11},{9,10},{10,... | collective-permute-start | bytes 417800 | tf_op jit(solution)/shard_map/ppermute | solution.py:406
  29.1 8.1 %collective-permute-start.9 = (bf16[544,128]{1,0:T(8,128)(2,1)S(1)}, bf16[544,128]{1,0:T(8,128)(2,1)S(1)}, u32[]{:S(2)}, u32[]{:S(2)}) collective-permute-start(bf16[544,128]{1,0:T(8,128)(2,1)S(1)} %pair.8.part_a), channel_id=1, source_target_pairs={{0,2},{1,3},{2,0},{3,1},{4,6},{5,7},{6,4},{7,5},{8,10},{9,11},{10,... | collective-permute-start | bytes 417800 | tf_op jit(solution)/shard_map/ppermute | solution.py:406
  49.3 11.2 %collective-permute-start.15 = (bf16[656,128]{1,0:T(8,128)(2,1)S(1)}, bf16[656,128]{1,0:T(8,128)(2,1)S(1)}, u32[]{:S(2)}, u32[]{:S(2)}) collective-permute-start(bf16[656,128]{1,0:T(8,128)(2,1)S(1)} %pair.9.part_a), channel_id=1, source_target_pairs={{0,96},{16,112},{32,64},{48,80},{64,32},{80,48},{96,0},{112,16},{1... | collective-permute-start | bytes 503816 | tf_op jit(solution)/shard_map/ppermute | solution.py:406
  50.8 9.8 %collective-permute-start.16 = (bf16[656,128]{1,0:T(8,128)(2,1)S(1)}, bf16[656,128]{1,0:T(8,128)(2,1)S(1)}, u32[]{:S(2)}, u32[]{:S(2)}) collective-permute-start(bf16[656,128]{1,0:T(8,128)(2,1)S(1)} %pair.9.part_a), channel_id=1, source_target_pairs={{0,64},{16,80},{32,96},{48,112},{64,0},{80,16},{96,32},{112,48},{1... | collective-permute-start | bytes 503816 | tf_op jit(solution)/shard_map/ppermute | solution.py:406
  51.8 9.4 %collective-permute-start.17 = (bf16[656,128]{1,0:T(8,128)(2,1)S(1)}, bf16[656,128]{1,0:T(8,128)(2,1)S(1)}, u32[]{:S(2)}, u32[]{:S(2)}) collective-permute-start(bf16[656,128]{1,0:T(8,128)(2,1)S(1)} %pair.9.part_a), channel_id=1, source_target_pairs={{0,32},{16,48},{32,0},{48,16},{64,96},{80,112},{96,64},{112,80},{1... | collective-permute-start | bytes 503816 | tf_op jit(solution)/shard_map/ppermute | solution.py:406
  61.4 7.7 %collective-permute-start.18 = (bf16[528,128]{1,0:T(8,128)(2,1)S(1)}, bf16[528,128]{1,0:T(8,128)(2,1)S(1)}, u32[]{:S(2)}, u32[]{:S(2)}) collective-permute-start(bf16[528,128]{1,0:T(8,128)(2,1)S(1)} %get-tuple-element.164.part_a.refs_0_), channel_id=1, source_target_pairs={{0,8},{1,9},{2,10},{3,11},{4,12},{5,13},{6,14},{7,15},{8,0},{9,1},... | collective-permute-start | bytes 405512 | tf_op jit(solution)/shard_map/ppermute | solution.py:406
  73.3 11.0 %collective-permute-start.22 = (bf16[656,128]{1,0:T(8,128)(2,1)S(1)}, bf16[656,128]{1,0:T(8,128)(2,1)S(1)}, u32[]{:S(2)}, u32[]{:S(2)}) collective-permute-start(bf16[656,128]{1,0:T(8,128)(2,1)S(1)} %pair.10.part_a), channel_id=1, source_target_pairs={{0,3},{1,2},{2,1},{3,0},{4,7},{5,6},{6,5},{7,4},{8,11},{9,10},{10,... | collective-permute-start | bytes 503816 | tf_op jit(solution)/shard_map/ppermute | solution.py:406
  76.0 8.7 %collective-permute-start.23 = (bf16[656,128]{1,0:T(8,128)(2,1)S(1)}, bf16[656,128]{1,0:T(8,128)(2,1)S(1)}, u32[]{:S(2)}, u32[]{:S(2)}) collective-permute-start(bf16[656,128]{1,0:T(8,128)(2,1)S(1)} %pair.10.part_a), channel_id=1, source_target_pairs={{0,2},{1,3},{2,0},{3,1},{4,6},{5,7},{6,4},{7,5},{8,10},{9,11},{10,... | collective-permute-start | bytes 503816 | tf_op jit(solution)/shard_map/ppermute | solution.py:406
  76.7 8.5 %collective-permute-start.24 = (bf16[656,128]{1,0:T(8,128)(2,1)S(1)}, bf16[656,128]{1,0:T(8,128)(2,1)S(1)}, u32[]{:S(2)}, u32[]{:S(2)}) collective-permute-start(bf16[656,128]{1,0:T(8,128)(2,1)S(1)} %pair.10.part_a), channel_id=1, source_target_pairs={{0,1},{1,0},{2,3},{3,2},{4,5},{5,4},{6,7},{7,6},{8,9},{9,8},{10,11... | collective-permute-start | bytes 503816 | tf_op jit(solution)/shard_map/ppermute | solution.py:406
  85.4 7.8 %collective-permute-start.25 = (bf16[528,128]{1,0:T(8,128)(2,1)S(1)}, bf16[528,128]{1,0:T(8,128)(2,1)S(1)}, u32[]{:S(2)}, u32[]{:S(2)}) collective-permute-start(bf16[528,128]{1,0:T(8,128)(2,1)S(1)} %get-tuple-element.177.part_a.refs_0_), channel_id=1, source_target_pairs={{0,12},{1,13},{2,14},{3,15},{4,8},{5,9},{6,10},{7,11},{8,4},{9,5},... | collective-permute-start | bytes 405512 | tf_op jit(solution)/shard_map/ppermute | solution.py:406
  97.0 11.2 %collective-permute-start.29 = (bf16[656,128]{1,0:T(8,128)(2,1)S(1)}, bf16[656,128]{1,0:T(8,128)(2,1)S(1)}, u32[]{:S(2)}, u32[]{:S(2)}) collective-permute-start(bf16[656,128]{1,0:T(8,128)(2,1)S(1)} %pair.11.part_a), channel_id=1, source_target_pairs={{0,96},{16,112},{32,64},{48,80},{64,32},{80,48},{96,0},{112,16},{1... | collective-permute-start | bytes 503816 | tf_op jit(solution)/shard_map/ppermute | solution.py:406
  98.4 9.8 %collective-permute-start.30 = (bf16[656,128]{1,0:T(8,128)(2,1)S(1)}, bf16[656,128]{1,0:T(8,128)(2,1)S(1)}, u32[]{:S(2)}, u32[]{:S(2)}) collective-permute-start(bf16[656,128]{1,0:T(8,128)(2,1)S(1)} %pair.11.part_a), channel_id=1, source_target_pairs={{0,64},{16,80},{32,96},{48,112},{64,0},{80,16},{96,32},{112,48},{1... | collective-permute-start | bytes 503816 | tf_op jit(solution)/shard_map/ppermute | solution.py:406
  99.5 9.4 %collective-permute-start.31 = (bf16[656,128]{1,0:T(8,128)(2,1)S(1)}, bf16[656,128]{1,0:T(8,128)(2,1)S(1)}, u32[]{:S(2)}, u32[]{:S(2)}) collective-permute-start(bf16[656,128]{1,0:T(8,128)(2,1)S(1)} %pair.11.part_a), channel_id=1, source_target_pairs={{0,32},{16,48},{32,0},{48,16},{64,96},{80,112},{96,64},{112,80},{1... | collective-permute-start | bytes 503816 | tf_op jit(solution)/shard_map/ppermute | solution.py:406
  109.1 7.7 %collective-permute-start.32 = (bf16[528,128]{1,0:T(8,128)(2,1)S(1)}, bf16[528,128]{1,0:T(8,128)(2,1)S(1)}, u32[]{:S(2)}, u32[]{:S(2)}) collective-permute-start(bf16[528,128]{1,0:T(8,128)(2,1)S(1)} %get-tuple-element.187.part_a.refs_0_), channel_id=1, source_target_pairs={{0,8},{1,9},{2,10},{3,11},{4,12},{5,13},{6,14},{7,15},{8,0},{9,1},... | collective-permute-start | bytes 405512 | tf_op jit(solution)/shard_map/ppermute | solution.py:406
  120.5 11.0 %collective-permute-start.36 = (bf16[656,128]{1,0:T(8,128)(2,1)S(1)}, bf16[656,128]{1,0:T(8,128)(2,1)S(1)}, u32[]{:S(2)}, u32[]{:S(2)}) collective-permute-start(bf16[656,128]{1,0:T(8,128)(2,1)S(1)} %pair.12.part_a), channel_id=1, source_target_pairs={{0,3},{1,2},{2,1},{3,0},{4,7},{5,6},{6,5},{7,4},{8,11},{9,10},{10,... | collective-permute-start | bytes 503816 | tf_op jit(solution)/shard_map/ppermute | solution.py:406
  123.2 8.7 %collective-permute-start.37 = (bf16[656,128]{1,0:T(8,128)(2,1)S(1)}, bf16[656,128]{1,0:T(8,128)(2,1)S(1)}, u32[]{:S(2)}, u32[]{:S(2)}) collective-permute-start(bf16[656,128]{1,0:T(8,128)(2,1)S(1)} %pair.12.part_a), channel_id=1, source_target_pairs={{0,2},{1,3},{2,0},{3,1},{4,6},{5,7},{6,4},{7,5},{8,10},{9,11},{10,... | collective-permute-start | bytes 503816 | tf_op jit(solution)/shard_map/ppermute | solution.py:406
  123.9 8.5 %collective-permute-start.38 = (bf16[656,128]{1,0:T(8,128)(2,1)S(1)}, bf16[656,128]{1,0:T(8,128)(2,1)S(1)}, u32[]{:S(2)}, u32[]{:S(2)}) collective-permute-start(bf16[656,128]{1,0:T(8,128)(2,1)S(1)} %pair.12.part_a), channel_id=1, source_target_pairs={{0,1},{1,0},{2,3},{3,2},{4,5},{5,4},{6,7},{7,6},{8,9},{9,8},{10,11... | collective-permute-start | bytes 503816 | tf_op jit(solution)/shard_map/ppermute | solution.py:406
  132.6 7.8 %collective-permute-start.39 = (bf16[528,128]{1,0:T(8,128)(2,1)S(1)}, bf16[528,128]{1,0:T(8,128)(2,1)S(1)}, u32[]{:S(2)}, u32[]{:S(2)}) collective-permute-start(bf16[528,128]{1,0:T(8,128)(2,1)S(1)} %get-tuple-element.199.part_a.refs_0_), channel_id=1, source_target_pairs={{0,12},{1,13},{2,14},{3,15},{4,8},{5,9},{6,10},{7,11},{8,4},{9,5},... | collective-permute-start | bytes 405512 | tf_op jit(solution)/shard_map/ppermute | solution.py:406
  144.2 11.2 %collective-permute-start.43 = (bf16[656,128]{1,0:T(8,128)(2,1)S(1)}, bf16[656,128]{1,0:T(8,128)(2,1)S(1)}, u32[]{:S(2)}, u32[]{:S(2)}) collective-permute-start(bf16[656,128]{1,0:T(8,128)(2,1)S(1)} %pair.13.part_a), channel_id=1, source_target_pairs={{0,96},{16,112},{32,64},{48,80},{64,32},{80,48},{96,0},{112,16},{1... | collective-permute-start | bytes 503816 | tf_op jit(solution)/shard_map/ppermute | solution.py:406
  145.7 9.8 %collective-permute-start.44 = (bf16[656,128]{1,0:T(8,128)(2,1)S(1)}, bf16[656,128]{1,0:T(8,128)(2,1)S(1)}, u32[]{:S(2)}, u32[]{:S(2)}) collective-permute-start(bf16[656,128]{1,0:T(8,128)(2,1)S(1)} %pair.13.part_a), channel_id=1, source_target_pairs={{0,64},{16,80},{32,96},{48,112},{64,0},{80,16},{96,32},{112,48},{1... | collective-permute-start | bytes 503816 | tf_op jit(solution)/shard_map/ppermute | solution.py:406
  146.7 9.4 %collective-permute-start.45 = (bf16[656,128]{1,0:T(8,128)(2,1)S(1)}, bf16[656,128]{1,0:T(8,128)(2,1)S(1)}, u32[]{:S(2)}, u32[]{:S(2)}) collective-permute-start(bf16[656,128]{1,0:T(8,128)(2,1)S(1)} %pair.13.part_a), channel_id=1, source_target_pairs={{0,32},{16,48},{32,0},{48,16},{64,96},{80,112},{96,64},{112,80},{1... | collective-permute-start | bytes 503816 | tf_op jit(solution)/shard_map/ppermute | solution.py:406
  156.3 7.6 %collective-permute-start.46 = (bf16[528,128]{1,0:T(8,128)(2,1)S(1)}, bf16[528,128]{1,0:T(8,128)(2,1)S(1)}, u32[]{:S(2)}, u32[]{:S(2)}) collective-permute-start(bf16[528,128]{1,0:T(8,128)(2,1)S(1)} %get-tuple-element.209.part_a.refs_0_), channel_id=1, source_target_pairs={{0,8},{1,9},{2,10},{3,11},{4,12},{5,13},{6,14},{7,15},{8,0},{9,1},... | collective-permute-start | bytes 405512 | tf_op jit(solution)/shard_map/ppermute | solution.py:406
  167.7 12.6 %collective-permute-start.50 = (bf16[784,128]{1,0:T(8,128)(2,1)S(1)}, bf16[784,128]{1,0:T(8,128)(2,1)S(1)}, u32[]{:S(2)}, u32[]{:S(2)}) collective-permute-start(bf16[784,128]{1,0:T(8,128)(2,1)S(1)} %pair.14.part_a), channel_id=1, source_target_pairs={{0,3},{1,2},{2,1},{3,0},{4,7},{5,6},{6,5},{7,4},{8,11},{9,10},{10,... | collective-permute-start | bytes 602120 | tf_op jit(solution)/shard_map/ppermute | solution.py:406
  170.5 9.9 %collective-permute-start.51 = (bf16[784,128]{1,0:T(8,128)(2,1)S(1)}, bf16[784,128]{1,0:T(8,128)(2,1)S(1)}, u32[]{:S(2)}, u32[]{:S(2)}) collective-permute-start(bf16[784,128]{1,0:T(8,128)(2,1)S(1)} %pair.14.part_a), channel_id=1, source_target_pairs={{0,2},{1,3},{2,0},{3,1},{4,6},{5,7},{6,4},{7,5},{8,10},{9,11},{10,... | collective-permute-start | bytes 602120 | tf_op jit(solution)/shard_map/ppermute | solution.py:406
  171.1 9.9 %collective-permute-start.52 = (bf16[784,128]{1,0:T(8,128)(2,1)S(1)}, bf16[784,128]{1,0:T(8,128)(2,1)S(1)}, u32[]{:S(2)}, u32[]{:S(2)}) collective-permute-start(bf16[784,128]{1,0:T(8,128)(2,1)S(1)} %pair.14.part_a), channel_id=1, source_target_pairs={{0,1},{1,0},{2,3},{3,2},{4,5},{5,4},{6,7},{7,6},{8,9},{9,8},{10,11... | collective-permute-start | bytes 602120 | tf_op jit(solution)/shard_map/ppermute | solution.py:406
  181.3 9.5 %collective-permute-start.55 = (bf16[784,128]{1,0:T(8,128)(2,1)S(1)}, bf16[784,128]{1,0:T(8,128)(2,1)S(1)}, u32[]{:S(2)}, u32[]{:S(2)}) collective-permute-start(bf16[784,128]{1,0:T(8,128)(2,1)S(1)} %get-tuple-element.233.part_a.refs_0_), channel_id=1, source_target_pairs={{0,8},{1,9},{2,10},{3,11},{4,12},{5,13},{6,14},{7,15},{8,0},{9,1},... | collective-permute-start | bytes 602120 | tf_op jit(solution)/shard_map/ppermute | solution.py:406
  183.1 10.0 %collective-permute-start.53 = (bf16[784,128]{1,0:T(8,128)(2,1)S(1)}, bf16[784,128]{1,0:T(8,128)(2,1)S(1)}, u32[]{:S(2)}, u32[]{:S(2)}) collective-permute-start(bf16[784,128]{1,0:T(8,128)(2,1)S(1)} %get-tuple-element.233.part_a.refs_0_), channel_id=1, source_target_pairs={{0,12},{1,13},{2,14},{3,15},{4,8},{5,9},{6,10},{7,11},{8,4},{9,5},... | collective-permute-start | bytes 602120 | tf_op jit(solution)/shard_map/ppermute | solution.py:406
  185.0 8.2 %collective-permute-start.54 = (bf16[784,128]{1,0:T(8,128)(2,1)S(1)}, bf16[784,128]{1,0:T(8,128)(2,1)S(1)}, u32[]{:S(2)}, u32[]{:S(2)}) collective-permute-start(bf16[784,128]{1,0:T(8,128)(2,1)S(1)} %get-tuple-element.233.part_a.refs_0_), channel_id=1, source_target_pairs={{0,4},{1,5},{2,6},{3,7},{4,0},{5,1},{6,2},{7,3},{8,12},{9,13},{10,... | collective-permute-start | bytes 602120 | tf_op jit(solution)/shard_map/ppermute | solution.py:406
  195.6 12.6 %collective-permute-start.57 = (bf16[784,128]{1,0:T(8,128)(2,1)S(1)}, bf16[784,128]{1,0:T(8,128)(2,1)S(1)}, u32[]{:S(2)}, u32[]{:S(2)}) collective-permute-start(bf16[784,128]{1,0:T(8,128)(2,1)S(1)} %pair.15.part_a), channel_id=1, source_target_pairs={{0,96},{16,112},{32,64},{48,80},{64,32},{80,48},{96,0},{112,16},{1... | collective-permute-start | bytes 602120 | tf_op jit(solution)/shard_map/ppermute | solution.py:406
  197.0 11.2 %collective-permute-start.58 = (bf16[784,128]{1,0:T(8,128)(2,1)S(1)}, bf16[784,128]{1,0:T(8,128)(2,1)S(1)}, u32[]{:S(2)}, u32[]{:S(2)}) collective-permute-start(bf16[784,128]{1,0:T(8,128)(2,1)S(1)} %pair.15.part_a), channel_id=1, source_target_pairs={{0,64},{16,80},{32,96},{48,112},{64,0},{80,16},{96,32},{112,48},{1... | collective-permute-start | bytes 602120 | tf_op jit(solution)/shard_map/ppermute | solution.py:406
  198.0 10.8 %collective-permute-start.59 = (bf16[784,128]{1,0:T(8,128)(2,1)S(1)}, bf16[784,128]{1,0:T(8,128)(2,1)S(1)}, u32[]{:S(2)}, u32[]{:S(2)}) collective-permute-start(bf16[784,128]{1,0:T(8,128)(2,1)S(1)} %pair.15.part_a), channel_id=1, source_target_pairs={{0,32},{16,48},{32,0},{48,16},{64,96},{80,112},{96,64},{112,80},{1... | collective-permute-start | bytes 602120 | tf_op jit(solution)/shard_map/ppermute | solution.py:406
  (37 other events, 166.7 us)

commit v7 on v5

--- a/solution.py
+++ b/solution.py
@@ -167,7 +167,7 @@
     return split_row(jnp.sum(jnp.transpose(squares), axis=0, keepdims=True))
 
 
-def embed_kernel(place, token, out, tile_out):
+def embed_kernel(place, token, out, tile_out, before_out):
     tokens = jnp.broadcast_to(token[...], (TOK, PIECE)) * 16411 + wrapped(EMBED_KEY * 1000003)
     tokens = tokens + lax.broadcasted_iota(jnp.int32, (TOK, PIECE), 1)
     tokens = tokens + (place[1] * STEP_C + place[3] * STEP_P)
@@ -180,6 +180,10 @@
             wide = part.astype(F32)
             squares = squares + wide * wide
     tile_out[...] = squares_tile(squares)
+    tokens = tokens + (place[2] * STEP_R + place[4] * STEP_Q - place[3] * STEP_P)
+    for digit in range(4):
+        rows = slice(digit * TOK, (digit + 1) * TOK)
+        before_out[rows, :] = hashed(tokens + digit * STEP_P, math.sqrt(3.0)).astype(BF)
 
 
 def first_scale_kernel(embedded, tile, *refs):
@@ -249,12 +253,14 @@
     *more, out = refs
     total = own[...] + other[...].astype(F32)
     out[:STATE, :] = total[:STATE].astype(BF)
+    if more:
+        out[STATE:GATHER, :] = split_row(joined_row(total[STATE:GATHER]))
+        out[GATHER:, :] = more[0][...]
+        return
     start = pl.multiple_of(digit[0] * TOK, TOK)
     out[STATE : STATE + TOK, :] = stream[pl.ds(start, TOK), :]
     out[STATE + TOK : SUM, :] = split_row(joined_row(total[STATE:GATHER]))
-    if more:
-        out[SUM:, :] = more[0][...]
-    elif total.shape[0] > GATHER:
+    if total.shape[0] > GATHER:
         out[SUM:, :] = total[GATHER:].astype(BF)
 
 
@@ -286,10 +292,10 @@
     following = layer + 1 < LAYERS
     fold = layer + 2 == LAYERS
     if layer == 0:
-        stream_out, mean_out, message_out, gains = refs
+        before, stream_out, mean_out, message_out, gains = refs
         for partner, part in zip(PARTNERS, parts):
             for index in range(4):
-                row = part[SUM : SUM + 16, :][index : index + 1].astype(F32)
+                row = part[GATHER : GATHER + 16, :][index : index + 1].astype(F32)
                 gains[index, jnp.bitwise_xor(digit[0], partner)] = row
     elif fold:
         gains, fold_weight, fold_gain, stream_out, mean_out, message_out = refs
@@ -297,7 +303,10 @@
         gains, stream_out, mean_out, message_out = refs
     else:
         stream_out, mean_out, odd_out, pre_out = refs
-    placed(digit, parts, stream_out)
+    if layer:
+        placed(digit, parts, stream_out)
+    else:
+        stream_out[...] = before[...]
 
     def total(rows):
         wide = {partner: part[rows, :].astype(F32) for partner, part in zip(PARTNERS, parts)}
@@ -306,7 +315,7 @@
     if not following:
         odd_out[...] = stream_out[...]
         pre_out[...] = total(slice(SUM, SUM + TOK))
-    squares = joined_row(total(slice(STATE + TOK, SUM)))
+    squares = joined_row(total(slice(STATE + TOK, SUM) if layer else slice(STATE, GATHER)))
     mean = jnp.transpose(jnp.broadcast_to(squares, (TOK, TOK))) * np.float32(1.0 / D)
     mean_out[...] = mean
     scale = lax.rsqrt(mean + EPSILON)
@@ -498,8 +507,8 @@
         core, facts, lax.ppermute(facts, "segment", CORE)
     )
     facts = exchange(facts, "x", SHORT)
-    embedded, tile = call(
-        embed_kernel, "embed", (sds((4, STATE, PIECE), BF), sds((16, TOK), BF)), [SMEM, VMEM]
+    embedded, tile, before = call(
+        embed_kernel, "embed", (sds((4, STATE, PIECE), BF), sds((16, TOK), BF), state_shape), [SMEM, VMEM]
     )(place, token_ids.reshape(TOK, 1))
     first_gain, odd_gain, even_gains, places, student_place, fold_place, fold_gain, up_place, up_gain = call(
         facts_kernel,
@@ -557,13 +566,13 @@
         )
         other = lax.ppermute(other, "segment", CORE)
         more = [odd_gain] if layer == 0 else []
-        rows = SUM + (16 if layer == 0 else TOK if layer + 2 >= LAYERS else 0)
+        rows = GATHER + 16 if layer == 0 else SUM + (TOK if layer + 2 >= LAYERS else 0)
         summed = call(pair_kernel, "pair", sds((rows, PIECE), BF), [SMEM] + [VMEM] * (3 + len(more)))(
             other_digit, own, other, streams[-1], *more
         )
         parts = exchange(summed, axis)
         out = [state_shape, mean_shape]
-        given = [] if layer == 0 or last else [odd_gains if even else even_gains]
+        given = [before] if layer == 0 else [] if last else [odd_gains if even else even_gains]
         if layer + 2 < LAYERS:
             weight = teacher_weight(layer + 1, plane, gate(places, summed))
             *parts, weight = lax.optimization_barrier((*parts, weight))

time: 229 us -> 228 us (level)
  no operation moved by 1% of the time
where the time goes in v7:
time: 228 us; the launch traced here: 227 us
  waiting for transfers between devices  84.8 us (37%)
  starting transfers between devices  81.3 us (36%)
  Pallas kernels  55.6 us (24%)
  local copies, waits for them, and re-layouts  3.07 us (1%)
  between operations  2.45 us (1%)
    ppermute x57, starting transfers between devices, exchange(): lax.ppermute(values[k], axis, [(i, i ^ k * step) for i in range(size)])  80.5 us
    ppermute x57, waiting for transfers between devices, exchange(): lax.ppermute(values[k], axis, [(i, i ^ k * step) for i in range(size)])  75.3 us
    pallas_call x8, Pallas kernels, teacher_weight(): call(body, 'weight', sds((2048, WIDTH), BF), [SMEM, VMEM], flops=20 * WEI...  39 us
    ppermute x8, waiting for transfers between devices, local(): other = lax.ppermute(other, 'segment', CORE)  6.89 us
  transfers between devices with their start and end apart: 67, of which 44 were waited for; matrix products, arithmetic and copies ran while one was open for 1% of the time, Pallas kernels for 20%

profile of v7, /device:TPU:0, one launch (start us, length us, event | category | flops | bytes accessed | tf_op | source)
XLA Modules:
  0.0 227.3 jit_solution(15623592211738544690)
XLA Ops:
  4.8 2.8 %collective-permute-start.1 = (bf16[2,48,128]{2,1,0:T(8,128)(2,1)S(1)}, bf16[2,48,128]{2,1,0:T(8,128)(2,1)S(1)}, u32[]{:S(2)}, u32[]{:S(2)}) collective-permute-start(bf16[2,48,128]{2,1,0:T(8,128)(2,1)S(1)} %chip.1.refs_0_), channel_id=1, source_target_pairs={{0,96},{16,112},{32,64},{48,80},{64,32},{80,48},{96,0},{112,16},{1... | collective-permute-start | bytes 73736 | tf_op jit(solution)/shard_map/ppermute | solution.py:388
  13.6 4.1 %collective-permute-start.4 = (f32[4,1,128]{2,1,0:T(1,128)S(1)}, f32[4,1,128]{2,1,0:T(1,128)S(1)}, u32[]{:S(2)}, u32[]{:S(2)}) collective-permute-start(f32[4,1,128]{2,1,0:T(1,128)S(1)} %get-tuple-element.137.refs_0_), channel_id=1, source_target_pairs={{0,12},{1,13},{2,14},{3,15},{4,8},{5,9},{6,10},{7,11},{8,4},{9,5},... | collective-permute-start | bytes 6152 | tf_op jit(solution)/shard_map/ppermute | solution.py:388
  18.6 4.9 %weight.8.refs_4_ = bf16[2048,1024]{1,0:T(8,128)(2,1)S(1)} custom-call(s32[1]{0:T(128)} %bitcast.4.plane, s32[8,128]{1,0:T(8,128)S(1)} %get-tuple-element.242.place), custom_call_target="tpu_custom_call" | custom-call | flops 41943040 | bytes 4194304 | tf_op jit(solution)/shard_map/weight/pallas_call | solution.py:223
  27.3 2.2 collective-permute-start.8
  30.2 4.9 %weight.9.refs_4_ = bf16[2048,1024]{1,0:T(8,128)(2,1)S(1)} custom-call(s32[1]{0:T(128)} %bitcast.4.plane, s32[8,128]{1,0:T(8,128)S(1)} %get-tuple-element.242.place), custom_call_target="tpu_custom_call" | custom-call | flops 41943040 | bytes 4194304 | tf_op jit(solution)/shard_map/weight/pallas_call | solution.py:223
  37.2 3.2 %collective-permute-start.11 = (bf16[528,128]{1,0:T(8,128)(2,1)S(1)}, bf16[528,128]{1,0:T(8,128)(2,1)S(1)}, u32[]{:S(2)}, u32[]{:S(2)}) collective-permute-start(bf16[528,128]{1,0:T(8,128)(2,1)S(1)} %get-tuple-element.150.refs_0_), channel_id=1, source_target_pairs={{0,12},{1,13},{2,14},{3,15},{4,8},{5,9},{6,10},{7,11},{8,4},{9,5},... | collective-permute-start | bytes 405512 | tf_op jit(solution)/shard_map/ppermute | solution.py:388
  41.3 4.4 %collective-permute-done.11.refs_1_ = bf16[528,128]{1,0:T(8,128)(2,1)S(1)} collective-permute-done((bf16[528,128]{1,0:T(8,128)(2,1)S(1)}, bf16[528,128]{1,0:T(8,128)(2,1)S(1)}, u32[]{:S(2)}, u32[]{:S(2)}) %collective-permute-start.11) | collective-permute-done | bytes 135200 | tf_op jit(solution)/shard_map/ppermute | solution.py:388
  45.7 2.2 collective-permute-done.12.refs_2_
  54.1 4.9 %weight.10.refs_4_ = bf16[2048,1024]{1,0:T(8,128)(2,1)S(1)} custom-call(s32[1]{0:T(128)} %bitcast.4.plane, s32[8,128]{1,0:T(8,128)S(1)} %get-tuple-element.242.place), custom_call_target="tpu_custom_call" | custom-call | flops 41943040 | bytes 4194304 | tf_op jit(solution)/shard_map/weight/pallas_call | solution.py:223
  59.0 2.2 collective-permute-done.15.part_b
  62.0 2.1 collective-permute-start.18
  66.2 4.1 %collective-permute-done.18.refs_1_ = bf16[528,128]{1,0:T(8,128)(2,1)S(1)} collective-permute-done((bf16[528,128]{1,0:T(8,128)(2,1)S(1)}, bf16[528,128]{1,0:T(8,128)(2,1)S(1)}, u32[]{:S(2)}, u32[]{:S(2)}) %collective-permute-start.18) | collective-permute-done | bytes 135200 | tf_op jit(solution)/shard_map/ppermute | solution.py:388
  75.2 2.2 collective-permute-start.24
  77.5 4.9 %weight.11.refs_4_ = bf16[2048,1024]{1,0:T(8,128)(2,1)S(1)} custom-call(s32[1]{0:T(128)} %bitcast.4.plane, s32[8,128]{1,0:T(8,128)S(1)} %get-tuple-element.242.place), custom_call_target="tpu_custom_call" | custom-call | flops 41943040 | bytes 4194304 | tf_op jit(solution)/shard_map/weight/pallas_call | solution.py:223
  82.4 2.2 collective-permute-done.22.part_b
  85.4 2.1 collective-permute-start.25
  89.6 4.1 %collective-permute-done.25.refs_1_ = bf16[528,128]{1,0:T(8,128)(2,1)S(1)} collective-permute-done((bf16[528,128]{1,0:T(8,128)(2,1)S(1)}, bf16[528,128]{1,0:T(8,128)(2,1)S(1)}, u32[]{:S(2)}, u32[]{:S(2)}) %collective-permute-start.25) | collective-permute-done | bytes 135200 | tf_op jit(solution)/shard_map/ppermute | solution.py:388
  100.9 4.9 %weight.12.refs_4_ = bf16[2048,1024]{1,0:T(8,128)(2,1)S(1)} custom-call(s32[1]{0:T(128)} %bitcast.4.plane, s32[8,128]{1,0:T(8,128)S(1)} %get-tuple-element.242.place), custom_call_target="tpu_custom_call" | custom-call | flops 41943040 | bytes 4194304 | tf_op jit(solution)/shard_map/weight/pallas_call | solution.py:223
  105.8 2.2 collective-permute-done.29.part_b
  113.0 4.1 %collective-permute-done.32.refs_1_ = bf16[528,128]{1,0:T(8,128)(2,1)S(1)} collective-permute-done((bf16[528,128]{1,0:T(8,128)(2,1)S(1)}, bf16[528,128]{1,0:T(8,128)(2,1)S(1)}, u32[]{:S(2)}, u32[]{:S(2)}) %collective-permute-start.32) | collective-permute-done | bytes 135200 | tf_op jit(solution)/shard_map/ppermute | solution.py:388
  124.3 4.9 %weight.13.refs_4_ = bf16[2048,1024]{1,0:T(8,128)(2,1)S(1)} custom-call(s32[1]{0:T(128)} %bitcast.4.plane, s32[8,128]{1,0:T(8,128)S(1)} %get-tuple-element.242.place), custom_call_target="tpu_custom_call" | custom-call | flops 41943040 | bytes 4194304 | tf_op jit(solution)/shard_map/weight/pallas_call | solution.py:223
  129.2 2.2 collective-permute-done.36.part_b
  136.4 4.1 %collective-permute-done.39.refs_1_ = bf16[528,128]{1,0:T(8,128)(2,1)S(1)} collective-permute-done((bf16[528,128]{1,0:T(8,128)(2,1)S(1)}, bf16[528,128]{1,0:T(8,128)(2,1)S(1)}, u32[]{:S(2)}, u32[]{:S(2)}) %collective-permute-start.39) | collective-permute-done | bytes 135200 | tf_op jit(solution)/shard_map/ppermute | solution.py:388
  147.7 4.9 %weight.14.refs_4_ = bf16[2048,1024]{1,0:T(8,128)(2,1)S(1)} custom-call(s32[1]{0:T(128)} %bitcast.4.plane, s32[8,128]{1,0:T(8,128)S(1)} %get-tuple-element.242.place), custom_call_target="tpu_custom_call" | custom-call | flops 41943040 | bytes 4194304 | tf_op jit(solution)/shard_map/weight/pallas_call | solution.py:223
  152.6 2.2 collective-permute-done.43.part_b
  159.8 4.1 %collective-permute-done.46.refs_1_ = bf16[528,128]{1,0:T(8,128)(2,1)S(1)} collective-permute-done((bf16[528,128]{1,0:T(8,128)(2,1)S(1)}, bf16[528,128]{1,0:T(8,128)(2,1)S(1)}, u32[]{:S(2)}, u32[]{:S(2)}) %collective-permute-start.46) | collective-permute-done | bytes 135200 | tf_op jit(solution)/shard_map/ppermute | solution.py:388
  172.2 8.2 %collective-permute-done.50.part_b = bf16[784,128]{1,0:T(8,128)(2,1)S(1)} collective-permute-done((bf16[784,128]{1,0:T(8,128)(2,1)S(1)}, bf16[784,128]{1,0:T(8,128)(2,1)S(1)}, u32[]{:S(2)}, u32[]{:S(2)}) %collective-permute-start.50) | collective-permute-done | bytes 200736 | tf_op jit(solution)/shard_map/ppermute | solution.py:388
  185.5 4.9 %weight.15.refs_4_ = bf16[2048,1024]{1,0:T(8,128)(2,1)S(1)} custom-call(s32[1]{0:T(128)} %bitcast.4.plane, s32[8,128]{1,0:T(8,128)S(1)} %get-tuple-element.242.place), custom_call_target="tpu_custom_call" | custom-call | flops 41943040 | bytes 4194304 | tf_op jit(solution)/shard_map/weight/pallas_call | solution.py:223
  190.4 2.4 %collective-permute-done.53.refs_1_.part_b = bf16[784,128]{1,0:T(8,128)(2,1)S(1)} collective-permute-done((bf16[784,128]{1,0:T(8,128)(2,1)S(1)}, bf16[784,128]{1,0:T(8,128)(2,1)S(1)}, u32[]{:S(2)}, u32[]{:S(2)}) %collective-permute-start.53) | collective-permute-done | bytes 200736 | tf_op jit(solution)/shard_map/ppermute | solution.py:388
  200.1 8.0 %collective-permute-done.57.part_b = bf16[784,128]{1,0:T(8,128)(2,1)S(1)} collective-permute-done((bf16[784,128]{1,0:T(8,128)(2,1)S(1)}, bf16[784,128]{1,0:T(8,128)(2,1)S(1)}, u32[]{:S(2)}, u32[]{:S(2)}) %collective-permute-start.57) | collective-permute-done | bytes 200736 | tf_op jit(solution)/shard_map/ppermute | solution.py:388
  216.5 2.2 collective-permute-done.62.refs_2_
  218.7 2.1 collective-permute-start.64
  (170 shorter events, 106.2 us)
Async XLA Ops:
  13.6 10.0 %collective-permute-start.4 = (f32[4,1,128]{2,1,0:T(1,128)S(1)}, f32[4,1,128]{2,1,0:T(1,128)S(1)}, u32[]{:S(2)}, u32[]{:S(2)}) collective-permute-start(f32[4,1,128]{2,1,0:T(1,128)S(1)} %get-tuple-element.137.refs_0_), channel_id=1, source_target_pairs={{0,12},{1,13},{2,14},{3,15},{4,8},{5,9},{6,10},{7,11},{8,4},{9,5},... | collective-permute-start | bytes 6152 | tf_op jit(solution)/shard_map/ppermute | solution.py:388
  25.6 9.5 %collective-permute-start.10 = (bf16[544,128]{1,0:T(8,128)(2,1)S(1)}, bf16[544,128]{1,0:T(8,128)(2,1)S(1)}, u32[]{:S(2)}, u32[]{:S(2)}) collective-permute-start(bf16[544,128]{1,0:T(8,128)(2,1)S(1)} %pair.8.part_a), channel_id=1, source_target_pairs={{0,1},{1,0},{2,3},{3,2},{4,5},{5,4},{6,7},{7,6},{8,9},{9,8},{10,11... | collective-permute-start | bytes 417800 | tf_op jit(solution)/shard_map/ppermute | solution.py:388
  37.2 8.6 %collective-permute-start.11 = (bf16[528,128]{1,0:T(8,128)(2,1)S(1)}, bf16[528,128]{1,0:T(8,128)(2,1)S(1)}, u32[]{:S(2)}, u32[]{:S(2)}) collective-permute-start(bf16[528,128]{1,0:T(8,128)(2,1)S(1)} %get-tuple-element.150.refs_0_), channel_id=1, source_target_pairs={{0,12},{1,13},{2,14},{3,15},{4,8},{5,9},{6,10},{7,11},{8,4},{9,5},... | collective-permute-start | bytes 405512 | tf_op jit(solution)/shard_map/ppermute | solution.py:388
  49.9 11.2 %collective-permute-start.15 = (bf16[656,128]{1,0:T(8,128)(2,1)S(1)}, bf16[656,128]{1,0:T(8,128)(2,1)S(1)}, u32[]{:S(2)}, u32[]{:S(2)}) collective-permute-start(bf16[656,128]{1,0:T(8,128)(2,1)S(1)} %pair.9.part_a), channel_id=1, source_target_pairs={{0,96},{16,112},{32,64},{48,80},{64,32},{80,48},{96,0},{112,16},{1... | collective-permute-start | bytes 503816 | tf_op jit(solution)/shard_map/ppermute | solution.py:388
  51.4 9.8 %collective-permute-start.16 = (bf16[656,128]{1,0:T(8,128)(2,1)S(1)}, bf16[656,128]{1,0:T(8,128)(2,1)S(1)}, u32[]{:S(2)}, u32[]{:S(2)}) collective-permute-start(bf16[656,128]{1,0:T(8,128)(2,1)S(1)} %pair.9.part_a), channel_id=1, source_target_pairs={{0,64},{16,80},{32,96},{48,112},{64,0},{80,16},{96,32},{112,48},{1... | collective-permute-start | bytes 503816 | tf_op jit(solution)/shard_map/ppermute | solution.py:388
  52.4 9.4 %collective-permute-start.17 = (bf16[656,128]{1,0:T(8,128)(2,1)S(1)}, bf16[656,128]{1,0:T(8,128)(2,1)S(1)}, u32[]{:S(2)}, u32[]{:S(2)}) collective-permute-start(bf16[656,128]{1,0:T(8,128)(2,1)S(1)} %pair.9.part_a), channel_id=1, source_target_pairs={{0,32},{16,48},{32,0},{48,16},{64,96},{80,112},{96,64},{112,80},{1... | collective-permute-start | bytes 503816 | tf_op jit(solution)/shard_map/ppermute | solution.py:388
  62.0 8.3 %collective-permute-start.18 = (bf16[528,128]{1,0:T(8,128)(2,1)S(1)}, bf16[528,128]{1,0:T(8,128)(2,1)S(1)}, u32[]{:S(2)}, u32[]{:S(2)}) collective-permute-start(bf16[528,128]{1,0:T(8,128)(2,1)S(1)} %get-tuple-element.161.refs_0_), channel_id=1, source_target_pairs={{0,12},{1,13},{2,14},{3,15},{4,8},{5,9},{6,10},{7,11},{8,4},{9,5},... | collective-permute-start | bytes 405512 | tf_op jit(solution)/shard_map/ppermute | solution.py:388
  73.3 11.2 %collective-permute-start.22 = (bf16[656,128]{1,0:T(8,128)(2,1)S(1)}, bf16[656,128]{1,0:T(8,128)(2,1)S(1)}, u32[]{:S(2)}, u32[]{:S(2)}) collective-permute-start(bf16[656,128]{1,0:T(8,128)(2,1)S(1)} %pair.10.part_a), channel_id=1, source_target_pairs={{0,3},{1,2},{2,1},{3,0},{4,7},{5,6},{6,5},{7,4},{8,11},{9,10},{10,... | collective-permute-start | bytes 503816 | tf_op jit(solution)/shard_map/ppermute | solution.py:388
  75.2 9.3 %collective-permute-start.23 = (bf16[656,128]{1,0:T(8,128)(2,1)S(1)}, bf16[656,128]{1,0:T(8,128)(2,1)S(1)}, u32[]{:S(2)}, u32[]{:S(2)}) collective-permute-start(bf16[656,128]{1,0:T(8,128)(2,1)S(1)} %pair.10.part_a), channel_id=1, source_target_pairs={{0,2},{1,3},{2,0},{3,1},{4,6},{5,7},{6,4},{7,5},{8,10},{9,11},{10,... | collective-permute-start | bytes 503816 | tf_op jit(solution)/shard_map/ppermute | solution.py:388
  75.2 9.9 %collective-permute-start.24 = (bf16[656,128]{1,0:T(8,128)(2,1)S(1)}, bf16[656,128]{1,0:T(8,128)(2,1)S(1)}, u32[]{:S(2)}, u32[]{:S(2)}) collective-permute-start(bf16[656,128]{1,0:T(8,128)(2,1)S(1)} %pair.10.part_a), channel_id=1, source_target_pairs={{0,1},{1,0},{2,3},{3,2},{4,5},{5,4},{6,7},{7,6},{8,9},{9,8},{10,11... | collective-permute-start | bytes 503816 | tf_op jit(solution)/shard_map/ppermute | solution.py:388
  85.4 8.3 %collective-permute-start.25 = (bf16[528,128]{1,0:T(8,128)(2,1)S(1)}, bf16[528,128]{1,0:T(8,128)(2,1)S(1)}, u32[]{:S(2)}, u32[]{:S(2)}) collective-permute-start(bf16[528,128]{1,0:T(8,128)(2,1)S(1)} %get-tuple-element.173.refs_0_), channel_id=1, source_target_pairs={{0,12},{1,13},{2,14},{3,15},{4,8},{5,9},{6,10},{7,11},{8,4},{9,5},... | collective-permute-start | bytes 405512 | tf_op jit(solution)/shard_map/ppermute | solution.py:388
  96.7 11.2 %collective-permute-start.29 = (bf16[656,128]{1,0:T(8,128)(2,1)S(1)}, bf16[656,128]{1,0:T(8,128)(2,1)S(1)}, u32[]{:S(2)}, u32[]{:S(2)}) collective-permute-start(bf16[656,128]{1,0:T(8,128)(2,1)S(1)} %pair.11.part_a), channel_id=1, source_target_pairs={{0,96},{16,112},{32,64},{48,80},{64,32},{80,48},{96,0},{112,16},{1... | collective-permute-start | bytes 503816 | tf_op jit(solution)/shard_map/ppermute | solution.py:388
  98.2 9.8 %collective-permute-start.30 = (bf16[656,128]{1,0:T(8,128)(2,1)S(1)}, bf16[656,128]{1,0:T(8,128)(2,1)S(1)}, u32[]{:S(2)}, u32[]{:S(2)}) collective-permute-start(bf16[656,128]{1,0:T(8,128)(2,1)S(1)} %pair.11.part_a), channel_id=1, source_target_pairs={{0,64},{16,80},{32,96},{48,112},{64,0},{80,16},{96,32},{112,48},{1... | collective-permute-start | bytes 503816 | tf_op jit(solution)/shard_map/ppermute | solution.py:388
  99.2 9.4 %collective-permute-start.31 = (bf16[656,128]{1,0:T(8,128)(2,1)S(1)}, bf16[656,128]{1,0:T(8,128)(2,1)S(1)}, u32[]{:S(2)}, u32[]{:S(2)}) collective-permute-start(bf16[656,128]{1,0:T(8,128)(2,1)S(1)} %pair.11.part_a), channel_id=1, source_target_pairs={{0,32},{16,48},{32,0},{48,16},{64,96},{80,112},{96,64},{112,80},{1... | collective-permute-start | bytes 503816 | tf_op jit(solution)/shard_map/ppermute | solution.py:388
  108.8 8.3 %collective-permute-start.32 = (bf16[528,128]{1,0:T(8,128)(2,1)S(1)}, bf16[528,128]{1,0:T(8,128)(2,1)S(1)}, u32[]{:S(2)}, u32[]{:S(2)}) collective-permute-start(bf16[528,128]{1,0:T(8,128)(2,1)S(1)} %get-tuple-element.183.refs_0_), channel_id=1, source_target_pairs={{0,12},{1,13},{2,14},{3,15},{4,8},{5,9},{6,10},{7,11},{8,4},{9,5},... | collective-permute-start | bytes 405512 | tf_op jit(solution)/shard_map/ppermute | solution.py:388
  120.1 11.2 %collective-permute-start.36 = (bf16[656,128]{1,0:T(8,128)(2,1)S(1)}, bf16[656,128]{1,0:T(8,128)(2,1)S(1)}, u32[]{:S(2)}, u32[]{:S(2)}) collective-permute-start(bf16[656,128]{1,0:T(8,128)(2,1)S(1)} %pair.12.part_a), channel_id=1, source_target_pairs={{0,3},{1,2},{2,1},{3,0},{4,7},{5,6},{6,5},{7,4},{8,11},{9,10},{10,... | collective-permute-start | bytes 503816 | tf_op jit(solution)/shard_map/ppermute | solution.py:388
  122.0 9.3 %collective-permute-start.37 = (bf16[656,128]{1,0:T(8,128)(2,1)S(1)}, bf16[656,128]{1,0:T(8,128)(2,1)S(1)}, u32[]{:S(2)}, u32[]{:S(2)}) collective-permute-start(bf16[656,128]{1,0:T(8,128)(2,1)S(1)} %pair.12.part_a), channel_id=1, source_target_pairs={{0,2},{1,3},{2,0},{3,1},{4,6},{5,7},{6,4},{7,5},{8,10},{9,11},{10,... | collective-permute-start | bytes 503816 | tf_op jit(solution)/shard_map/ppermute | solution.py:388
  122.6 9.4 %collective-permute-start.38 = (bf16[656,128]{1,0:T(8,128)(2,1)S(1)}, bf16[656,128]{1,0:T(8,128)(2,1)S(1)}, u32[]{:S(2)}, u32[]{:S(2)}) collective-permute-start(bf16[656,128]{1,0:T(8,128)(2,1)S(1)} %pair.12.part_a), channel_id=1, source_target_pairs={{0,1},{1,0},{2,3},{3,2},{4,5},{5,4},{6,7},{7,6},{8,9},{9,8},{10,11... | collective-permute-start | bytes 503816 | tf_op jit(solution)/shard_map/ppermute | solution.py:388
  132.2 8.3 %collective-permute-start.39 = (bf16[528,128]{1,0:T(8,128)(2,1)S(1)}, bf16[528,128]{1,0:T(8,128)(2,1)S(1)}, u32[]{:S(2)}, u32[]{:S(2)}) collective-permute-start(bf16[528,128]{1,0:T(8,128)(2,1)S(1)} %get-tuple-element.194.refs_0_), channel_id=1, source_target_pairs={{0,12},{1,13},{2,14},{3,15},{4,8},{5,9},{6,10},{7,11},{8,4},{9,5},... | collective-permute-start | bytes 405512 | tf_op jit(solution)/shard_map/ppermute | solution.py:388
  143.5 11.2 %collective-permute-start.43 = (bf16[656,128]{1,0:T(8,128)(2,1)S(1)}, bf16[656,128]{1,0:T(8,128)(2,1)S(1)}, u32[]{:S(2)}, u32[]{:S(2)}) collective-permute-start(bf16[656,128]{1,0:T(8,128)(2,1)S(1)} %pair.13.part_a), channel_id=1, source_target_pairs={{0,96},{16,112},{32,64},{48,80},{64,32},{80,48},{96,0},{112,16},{1... | collective-permute-start | bytes 503816 | tf_op jit(solution)/shard_map/ppermute | solution.py:388
  145.0 9.8 %collective-permute-start.44 = (bf16[656,128]{1,0:T(8,128)(2,1)S(1)}, bf16[656,128]{1,0:T(8,128)(2,1)S(1)}, u32[]{:S(2)}, u32[]{:S(2)}) collective-permute-start(bf16[656,128]{1,0:T(8,128)(2,1)S(1)} %pair.13.part_a), channel_id=1, source_target_pairs={{0,64},{16,80},{32,96},{48,112},{64,0},{80,16},{96,32},{112,48},{1... | collective-permute-start | bytes 503816 | tf_op jit(solution)/shard_map/ppermute | solution.py:388
  146.0 9.4 %collective-permute-start.45 = (bf16[656,128]{1,0:T(8,128)(2,1)S(1)}, bf16[656,128]{1,0:T(8,128)(2,1)S(1)}, u32[]{:S(2)}, u32[]{:S(2)}) collective-permute-start(bf16[656,128]{1,0:T(8,128)(2,1)S(1)} %pair.13.part_a), channel_id=1, source_target_pairs={{0,32},{16,48},{32,0},{48,16},{64,96},{80,112},{96,64},{112,80},{1... | collective-permute-start | bytes 503816 | tf_op jit(solution)/shard_map/ppermute | solution.py:388
  155.6 8.3 %collective-permute-start.46 = (bf16[528,128]{1,0:T(8,128)(2,1)S(1)}, bf16[528,128]{1,0:T(8,128)(2,1)S(1)}, u32[]{:S(2)}, u32[]{:S(2)}) collective-permute-start(bf16[528,128]{1,0:T(8,128)(2,1)S(1)} %get-tuple-element.215.refs_0_), channel_id=1, source_target_pairs={{0,12},{1,13},{2,14},{3,15},{4,8},{5,9},{6,10},{7,11},{8,4},{9,5},... | collective-permute-start | bytes 405512 | tf_op jit(solution)/shard_map/ppermute | solution.py:388
  167.8 12.6 %collective-permute-start.50 = (bf16[784,128]{1,0:T(8,128)(2,1)S(1)}, bf16[784,128]{1,0:T(8,128)(2,1)S(1)}, u32[]{:S(2)}, u32[]{:S(2)}) collective-permute-start(bf16[784,128]{1,0:T(8,128)(2,1)S(1)} %pair.14.part_a), channel_id=1, source_target_pairs={{0,3},{1,2},{2,1},{3,0},{4,7},{5,6},{6,5},{7,4},{8,11},{9,10},{10,... | collective-permute-start | bytes 602120 | tf_op jit(solution)/shard_map/ppermute | solution.py:388
  169.7 10.7 %collective-permute-start.51 = (bf16[784,128]{1,0:T(8,128)(2,1)S(1)}, bf16[784,128]{1,0:T(8,128)(2,1)S(1)}, u32[]{:S(2)}, u32[]{:S(2)}) collective-permute-start(bf16[784,128]{1,0:T(8,128)(2,1)S(1)} %pair.14.part_a), channel_id=1, source_target_pairs={{0,2},{1,3},{2,0},{3,1},{4,6},{5,7},{6,4},{7,5},{8,10},{9,11},{10,... | collective-permute-start | bytes 602120 | tf_op jit(solution)/shard_map/ppermute | solution.py:388
  170.2 10.8 %collective-permute-start.52 = (bf16[784,128]{1,0:T(8,128)(2,1)S(1)}, bf16[784,128]{1,0:T(8,128)(2,1)S(1)}, u32[]{:S(2)}, u32[]{:S(2)}) collective-permute-start(bf16[784,128]{1,0:T(8,128)(2,1)S(1)} %pair.14.part_a), channel_id=1, source_target_pairs={{0,1},{1,0},{2,3},{3,2},{4,5},{5,4},{6,7},{7,6},{8,9},{9,8},{10,11... | collective-permute-start | bytes 602120 | tf_op jit(solution)/shard_map/ppermute | solution.py:388
  181.3 11.5 %collective-permute-start.53 = (bf16[784,128]{1,0:T(8,128)(2,1)S(1)}, bf16[784,128]{1,0:T(8,128)(2,1)S(1)}, u32[]{:S(2)}, u32[]{:S(2)}) collective-permute-start(bf16[784,128]{1,0:T(8,128)(2,1)S(1)} %get-tuple-element.238.refs_0_.part_a), channel_id=1, source_target_pairs={{0,12},{1,13},{2,14},{3,15},{4,8},{5,9},{6,10},{7,11},{8,4},{9,5},... | collective-permute-start | bytes 602120 | tf_op jit(solution)/shard_map/ppermute | solution.py:388
  183.4 9.5 %collective-permute-start.54 = (bf16[784,128]{1,0:T(8,128)(2,1)S(1)}, bf16[784,128]{1,0:T(8,128)(2,1)S(1)}, u32[]{:S(2)}, u32[]{:S(2)}) collective-permute-start(bf16[784,128]{1,0:T(8,128)(2,1)S(1)} %get-tuple-element.238.refs_0_.part_a), channel_id=1, source_target_pairs={{0,8},{1,9},{2,10},{3,11},{4,12},{5,13},{6,14},{7,15},{8,0},{9,1},... | collective-permute-start | bytes 602120 | tf_op jit(solution)/shard_map/ppermute | solution.py:388
  183.7 9.7 %collective-permute-start.55 = (bf16[784,128]{1,0:T(8,128)(2,1)S(1)}, bf16[784,128]{1,0:T(8,128)(2,1)S(1)}, u32[]{:S(2)}, u32[]{:S(2)}) collective-permute-start(bf16[784,128]{1,0:T(8,128)(2,1)S(1)} %get-tuple-element.238.refs_0_.part_a), channel_id=1, source_target_pairs={{0,4},{1,5},{2,6},{3,7},{4,0},{5,1},{6,2},{7,3},{8,12},{9,13},{10,... | collective-permute-start | bytes 602120 | tf_op jit(solution)/shard_map/ppermute | solution.py:388
  195.5 12.6 %collective-permute-start.57 = (bf16[784,128]{1,0:T(8,128)(2,1)S(1)}, bf16[784,128]{1,0:T(8,128)(2,1)S(1)}, u32[]{:S(2)}, u32[]{:S(2)}) collective-permute-start(bf16[784,128]{1,0:T(8,128)(2,1)S(1)} %pair.15.part_a), channel_id=1, source_target_pairs={{0,96},{16,112},{32,64},{48,80},{64,32},{80,48},{96,0},{112,16},{1... | collective-permute-start | bytes 602120 | tf_op jit(solution)/shard_map/ppermute | solution.py:388
  197.0 11.2 %collective-permute-start.58 = (bf16[784,128]{1,0:T(8,128)(2,1)S(1)}, bf16[784,128]{1,0:T(8,128)(2,1)S(1)}, u32[]{:S(2)}, u32[]{:S(2)}) collective-permute-start(bf16[784,128]{1,0:T(8,128)(2,1)S(1)} %pair.15.part_a), channel_id=1, source_target_pairs={{0,64},{16,80},{32,96},{48,112},{64,0},{80,16},{96,32},{112,48},{1... | collective-permute-start | bytes 602120 | tf_op jit(solution)/shard_map/ppermute | solution.py:388
  198.0 10.8 %collective-permute-start.59 = (bf16[784,128]{1,0:T(8,128)(2,1)S(1)}, bf16[784,128]{1,0:T(8,128)(2,1)S(1)}, u32[]{:S(2)}, u32[]{:S(2)}) collective-permute-start(bf16[784,128]{1,0:T(8,128)(2,1)S(1)} %pair.15.part_a), channel_id=1, source_target_pairs={{0,32},{16,48},{32,0},{48,16},{64,96},{80,112},{96,64},{112,80},{1... | collective-permute-start | bytes 602120 | tf_op jit(solution)/shard_map/ppermute | solution.py:388
  (37 other events, 177.8 us)
